TPU v7x, 32 devices: a whole 2x2x4 slice. The times are simulated.
32 devices in a mesh: page: 4 (over x, core), strip: 8 (over z, y).
Axes of the slice: x: 2, y: 2, z: 4, core: 2. Of those that a mesh axis runs over, the one named last changes fastest.
Arguments:
- visual_in: bfloat16 [8, 48, 96, 768], P('page', 'strip'), may hold values from -6 to 6
- query_in: bfloat16 [8, 1024, 768], P('page', 'strip'), may hold values from -6 to 6
- row_valid: int32 [8, 48], P('page', 'strip'), may hold values from 0 to 1, as said below
- segment_ids: int32 [8, 1024], P('page'), may hold values from 0 to 63, never falling along the last dimension, each value on 1 to 32 neighbouring positions
- slot_valid: int32 [8, 1024], P('page', 'strip'), may hold values from 0 to 1, as said below
- col_shift: int32 [8], P('page'), may hold values from 0 to 11
- row_shifted: int32 [8], P('page'), may hold values from 0 to 1, as said below
- norm_gains: float32 [768, 4], replicated, may hold values from 0.1 to 1.9
- w_vqkv: bfloat16 [768, 2304], replicated, may hold values from -0.21875 to 0.21875
- w_vout: bfloat16 [768, 768], replicated, may hold values from -1.5 to 1.5
- w_up: bfloat16 [768, 3072], replicated, may hold values from -0.21875 to 0.21875
- w_down: bfloat16 [3072, 768], replicated, may hold values from -0.109375 to 0.109375
- w_qqkv: bfloat16 [768, 2304], replicated, may hold values from -0.3125 to 0.3125
- w_xkv: bfloat16 [768, 1536], replicated, may hold values from -0.3125 to 0.3125
- w_qout: bfloat16 [768, 768], replicated, may hold values from -3 to 3
- w_qup: bfloat16 [768, 3072], replicated, may hold values from -0.21875 to 0.21875
- w_qdown: bfloat16 [3072, 768], replicated, may hold values from -0.109375 to 0.109375
- visual_cot: bfloat16 [8, 48, 96, 768], P('page', 'strip'), may hold values from -6 to 6
- query_cot: bfloat16 [8, 1024, 768], P('page', 'strip'), may hold values from -6 to 6
Outputs:
- visual_out: bfloat16 [8, 48, 96, 768], P('page', 'strip')
- query_out: bfloat16 [8, 1024, 768], P('page', 'strip')
- visual_in_grad: float32 [8, 48, 96, 768], P('page', 'strip')
- query_in_grad: float32 [8, 1024, 768], P('page', 'strip')
- gain_grads: float32 [768, 4], P('strip', 'page')
- w_vqkv_grad: float32 [768, 2304], P('strip', 'page')
- w_vout_grad: float32 [768, 768], P('strip', 'page')
- w_up_grad: float32 [768, 3072], P('strip', 'page')
- w_down_grad: float32 [3072, 768], P('strip', 'page')
- w_qqkv_grad: float32 [768, 2304], P('strip', 'page')
- w_xkv_grad: float32 [768, 1536], P('strip', 'page')
- w_qout_grad: float32 [768, 768], P('strip', 'page')
- w_qup_grad: float32 [768, 3072], P('strip', 'page')
- w_qdown_grad: float32 [3072, 768], P('strip', 'page')
Inputs may be any that keep to these rules, and one draw needn't show every extreme that they name: `row_valid`: for each page, 1 on a leading run of patch rows and 0 after it; the run holds 24 rows or more. `slot_valid`: for each page, 1 on a leading run of slots and 0 after it; the run holds 512 slots or more. `segment_ids`: along a page's slots the ids never fall; a segment holds 1 to 32 slots. `row_shifted`: of pages 2k and 2k + 1, exactly one has 1.
All inputs are finite; a program needn't handle non-finite values.
Results may differ from a plain program's by a relative error of at most 0.0144.
Values may be sent and summed in bfloat16 or wider, within the bound.
A program may use at most 448 MiB of HBM per device.

v0:
```python
import functools

import jax
import jax.numpy as jnp
from jax import lax
from jax.experimental import pallas as pl
from jax.experimental.pallas import tpu as pltpu
from jax.sharding import PartitionSpec as P

HEADS = 12
WIN = 12
EPS = 1e-05
MASKED = -1e9
SCALE = 0.125
BF = jnp.bfloat16
F32 = jnp.float32
LANES = 128
VMEM_BYTES = 65400 * 1024


def dot(left, right, left_dim=1, right_dim=0):
    return lax.dot_general(
        left, right, (((left_dim,), (right_dim,)), ((), ())), preferred_element_type=F32
    )


def iota(shape, dim):
    return lax.broadcasted_iota(jnp.int32, shape, dim)


def norm_stats(rows):
    offset = rows - jnp.mean(rows, axis=-1, keepdims=True)
    spread = lax.rsqrt(jnp.mean(offset * offset, axis=-1, keepdims=True) + EPS)
    return offset * spread, spread


def norm_back(unit, spread, gain, grad):
    product = grad * unit
    scaled = grad * gain
    centre = jnp.mean(scaled, axis=-1, keepdims=True)
    slope = jnp.mean(scaled * unit, axis=-1, keepdims=True)
    return spread * (scaled - centre - unit * slope), jnp.sum(product, axis=0, keepdims=True)


def gelu_pair(t):
    square = t * t
    plus = 0.5 * jnp.tanh(t * (0.7978845608 + 0.0356774081 * square)) + 0.5
    value = t * plus
    return value, plus + value * (1.0 - plus) * (1.5957691216 + 0.2140644488 * square)


def three_parts(value):
    high = value.astype(BF).astype(F32)
    rest = value - high
    middle = rest.astype(BF).astype(F32)
    low = (rest - middle).astype(BF).astype(F32)
    return high, middle, low


def place_lanes(column, lane, first):
    high, middle, low = three_parts(column)
    return (
        jnp.where(lane == first, high, 0.0)
        + jnp.where(lane == first + 16, middle, 0.0)
        + jnp.where(lane == first + 32, low, 0.0)
    )


def join_lanes(stats, first):
    total = stats
    rolled = []
    for part in range(3):
        amount = (first + 16 * part) % LANES
        rolled.append(total if amount == 0 else pltpu.roll(total, LANES - amount, 1))
    return rolled[0] + rolled[1] + rolled[2]


def spread_heads(values, width):
    head_dim = width // HEADS
    pick = (iota((LANES, width), 0) == iota((LANES, width), 1) // head_dim).astype(BF)
    high, middle, low = three_parts(values)
    return dot(high.astype(BF), pick) + dot(middle.astype(BF), pick) + dot(low.astype(BF), pick)


def whole(shape, single=False):
    mode = pl.Buffered(1) if single else None
    return pl.BlockSpec(shape, lambda *_: (0,) * len(shape), pipeline_mode=mode)


def sds(shape, kind):
    return jax.ShapeDtypeStruct(shape, kind)


ANY = pl.BlockSpec(memory_space=pl.ANY)


def call(kernel, name, ins, outs, grid=(1,), scratch=(), scalars=None, deps=(), work=(0, 0, 0), aliases={}):
    first = len(ins) + (scalars is not None)

    def body(*refs):
        kernel(*refs[:first], *refs[first + len(deps) :])

    return pl.pallas_call(
        body,
        grid_spec=pltpu.PrefetchScalarGridSpec(
            num_scalar_prefetch=int(scalars is not None),
            grid=grid,
            in_specs=[spec for _, spec in ins] + [ANY] * len(deps),
            out_specs=[spec for *_, spec in outs],
            scratch_shapes=list(scratch),
        ),
        out_shape=[sds(shape, kind) for shape, kind, _ in outs],
        input_output_aliases=aliases,
        compiler_params=pltpu.CompilerParams(vmem_limit_bytes=VMEM_BYTES),
        cost_estimate=pl.CostEstimate(flops=int(3 * work[0]), bytes_accessed=int(work[1]), transcendentals=int(work[2])),
        name=name,
    )(*([] if scalars is None else [scalars]), *[array for array, _ in ins], *deps)


UP, SHIFT, ODD, CORE, BIT_X, BIT_Y, BIT_LOW, BIT_HIGH, BASE = range(9)


def page_block(shape):
    return pl.BlockSpec((1, *shape[1:]), lambda *at: (at[-1][UP],) + (0,) * (len(shape) - 1))


def steps_below(value, size, count):
    total = jnp.zeros_like(value)
    for k in range(1, count):
        total = total + jnp.where(value >= size * k, 1, 0)
    return total


def into_windows(own, other, shift, strip_rows, columns):
    half, part = strip_rows * columns, strip_rows * WIN
    token = iota((half, 1), 0)
    window = steps_below(token, part, columns // WIN)
    inside = token - part * window
    row = steps_below(inside, WIN, strip_rows)
    column = inside - WIN * row + WIN * window + shift
    column = jnp.where(column >= columns, column - columns, column)
    onehot = (iota((half, half), 1) == row * columns + column).astype(F32).astype(BF)
    turned = [dot(onehot, own), dot(onehot, other)]
    pieces = [turned[side][w * part : (w + 1) * part] for w in range(columns // WIN) for side in range(2)]
    return jnp.concatenate(pieces, axis=0)


def out_of_windows(shift, strip_rows, columns):
    half = strip_rows * columns
    token = iota((half, 1), 0)
    row = steps_below(token, columns, strip_rows)
    column = token - columns * row - shift
    column = jnp.where(column < 0, column + columns, column)
    window = steps_below(column, WIN, columns // WIN)
    spot = window * (strip_rows * WIN) + row * WIN + column - WIN * window
    return (iota((half, half), 1) == spot).astype(F32).astype(BF)


def tile_index(strip, half, order):
    y = strip % 2
    lead = (y, half) if order == 0 else (half, y)
    return lead + ((strip // 2 % 2) * 2 + strip // 4,)


def tile_shape(rows, cols):
    return (2, 2, 2, 4, cols // 256 * (rows // 16), LANES)


def store_all(ref, value, order):
    rows, cols = value.shape
    size, tiles = rows // 16, cols // 256
    for strip in range(8):
        for core in range(2):
            at = (2 * strip + core) * size
            for half in range(2):
                lead = tile_index(strip, half, order)
                for t in range(tiles):
                    lanes = (half * tiles + t) * LANES
                    ref[(core, *lead, slice(t * size, (t + 1) * size), slice(None))] = value[at : at + size, lanes : lanes + LANES]


def store_columns(ref, value, order, half=0, first=0):
    size = value.shape[0] // 16
    for strip in range(8):
        for core in range(2):
            at = (2 * strip + core) * size
            lead = tile_index(strip, half, order)
            for t in range(value.shape[1] // LANES):
                rows = slice((first + t) * size, (first + t + 1) * size)
                ref[(core, *lead, rows, slice(None))] = value[at : at + size, t * LANES : (t + 1) * LANES]


def store_strips(ref, value, order, z=0):
    size, tiles = value.shape[0] // 4, value.shape[1] // 256
    for y in range(2):
        for core in range(2):
            for half in range(2):
                lead = (y, half) if order == 0 else (half, y)
                for t in range(tiles):
                    lanes = (half * tiles + t) * LANES
                    at = (2 * y + core) * size
                    ref[(core, *lead, z, slice(t * size, (t + 1) * size), slice(None))] = value[at : at + size, lanes : lanes + LANES]


def columns_spec(rows, chunk, per_half, order, at):
    block = (2, 2, 1, 4) if order == 0 else (2, 1, 2, 4)
    lead = lambda half: (0, 0, half, 0) if order == 0 else (0, half, 0, 0)
    return pl.BlockSpec(
        (*block, chunk // LANES * (rows // 16), LANES), lambda j, *_: (*lead(at(j) // per_half), at(j) % per_half, 0)
    )


def strips_spec(rows, cols):
    return pl.BlockSpec(
        (2, 2, 2, 1, cols // 256 * (rows // 16), LANES), lambda j, *_: (0, 0, 0, (j % 2) * 2 + j // 2, 0, 0)
    )


def grad_forms(width, hidden, chunk, tiled, wo_order):
    if not tiled:
        return [
            ((width, width), BF, whole((width, width))),
            ((width, hidden), BF, pl.BlockSpec((width, chunk), lambda j, *_: (0, j))),
            ((hidden, width), BF, pl.BlockSpec((chunk, width), lambda j, *_: (j, 0))),
        ]
    shapes = [tile_shape(width, width), tile_shape(width, hidden), tile_shape(hidden, width)]
    specs = [
        whole(shapes[0]),
        columns_spec(width, chunk, hidden // 2 // chunk, 0, lambda j: j),
        strips_spec(hidden, width),
    ]
    return [(shape, BF, spec) for shape, spec in zip(shapes, specs)]


def put_grad(ref, value, store, order, tiled):
    if tiled:
        store(ref, value, order)
    else:
        ref[...] = value


def patch_in_kernel(s_ref, ok_ref, own_ref, other_ref, gain_ref, wq_ref, wx_ref, x_ref, n_ref, qkv_ref, cross_ref, bias_ref, turned, *, form):
    strip_rows, half = form[0], own_ref.shape[1]
    row = steps_below(iota((WIN * WIN, 1), 0), WIN, WIN)
    valid = jnp.zeros((WIN * WIN, 1), F32)
    for r in range(strip_rows):
        mine = jnp.where(ok_ref[s_ref[UP], r] == 1, 1.0, 0.0)
        theirs = other_ref[half : half + 1, r : r + 1].astype(F32)
        valid = valid + jnp.where(row == r, mine, 0.0) + jnp.where(row == strip_rows + r, theirs, 0.0)
    bias = jnp.broadcast_to(jnp.where(valid > 0.5, 0.0, MASKED).astype(BF), (WIN * WIN, LANES))
    for k in range(2):
        bias_ref[k * WIN * WIN : (k + 1) * WIN * WIN, :] = bias
    @pl.when(pl.program_id(0) == 0)
    def _():
        turned[...] = into_windows(own_ref[0], other_ref[:half, :], s_ref[SHIFT], *form).astype(BF)

    step = x_ref.shape[0]
    x = turned[pl.ds(pl.multiple_of(pl.program_id(0) * step, step), step), :].astype(F32)
    x_ref[...] = x.astype(BF)
    unit, _ = norm_stats(x)
    normed = (unit * gain_ref[0:1, :]).astype(BF)
    n_ref[...] = normed
    qkv_ref[...] = dot(normed, wq_ref[...]).astype(BF)
    cross_ref[...] = dot(normed, wx_ref[...]).astype(BF)


def patch_in(scalars, rows_ok, visual, other, gains, wq, wx, form, deps):
    _, half, width = visual.shape
    tokens = 2 * half
    step = 4 * form[0] * WIN
    rows = lambda w: ((tokens, w), BF, pl.BlockSpec((step, w), lambda i, *_: (i, 0)))
    return call(
        functools.partial(patch_in_kernel, form=form),
        "patch_in",
        [(rows_ok, pl.BlockSpec(memory_space=pltpu.SMEM)), (visual, page_block(visual.shape))]
        + [(a, whole(a.shape, True)) for a in (other, gains, wq, wx)],
        [rows(width), rows(width), rows(wq.shape[1]), rows(wx.shape[1]), rows(LANES)],
        grid=(tokens // step,),
        scratch=[pltpu.VMEM((tokens, width), BF)],
        scalars=scalars,
        deps=deps,
        work=(2 * tokens * width * (wq.shape[1] + wx.shape[1]), 2e7, 0),
    )


def pack_kernel(s_ref, ok_a_ref, a_ref, ok_b_ref, b_ref, a_out, b_out):
    for ok_ref, rows_ref, out_ref in ((ok_a_ref, a_ref, a_out), (ok_b_ref, b_ref, b_out)):
        count, flags = rows_ref.shape[1], ok_ref.shape[1]
        out_ref[:count, :] = rows_ref[0]
        out_ref[count:, :] = jnp.zeros_like(out_ref[count:, :])
        theirs = jnp.where(s_ref[UP] == 0, ok_ref[1:2, :], ok_ref[0:1, :]).astype(F32).astype(BF)
        out_ref[count:, :flags] = jnp.broadcast_to(theirs, (out_ref.shape[0] - count, flags))


def other_page(shape):
    return pl.BlockSpec((1, *shape[1:]), lambda *at: (1 - at[-1][UP],) + (0,) * (len(shape) - 1))


def pack(scalars, arrays):
    ins, outs = [], []
    for rows, flags in arrays:
        ins += [(flags, whole(flags.shape)), (rows, other_page(rows.shape))]
        shape = (rows.shape[1] + 16, rows.shape[2])
        outs.append((shape, BF, whole(shape)))
    return call(pack_kernel, "pack", ins, outs, scalars=scalars)


def held_back(array, deps):
    [out] = call(lambda a_ref, out_ref: None, "held_back", [(array, ANY)], [(array.shape, array.dtype, ANY)], deps=deps, aliases={0: 0})
    return out


def pack_two_kernel(s_ref, a_ref, b_ref, a_out, b_out):
    a_out[...] = a_ref[0]
    b_out[...] = b_ref[0]


def pack_two(scalars, a, b, deps):
    return call(
        pack_two_kernel,
        "pack_two",
        [(x, other_page(x.shape)) for x in (a, b)],
        [(x.shape[1:], BF, whole(x.shape[1:])) for x in (a, b)],
        scalars=scalars,
        deps=deps,
    )


def put_two_kernel(s_ref, a_ref, b_ref, a_came, b_came, a_out, b_out):
    a_out[0] = a_came[...].astype(a_out.dtype)
    b_out[0] = b_came[...].astype(b_out.dtype)


def put_two(scalars, a, b, a_came, b_came, deps):
    return call(
        put_two_kernel,
        "put_two",
        [(a, ANY), (b, ANY)] + [(x, whole(x.shape)) for x in (a_came, b_came)],
        [(x.shape, x.dtype, other_page(x.shape)) for x in (a, b)],
        scalars=scalars,
        deps=deps,
        aliases={1: 0, 2: 1},
    )


def head_masks():
    lane = iota((1, LANES), 1)
    left = lane < 64
    return left, [left.astype(F32).astype(BF), (~left).astype(F32).astype(BF)]


def window_kernel(qkv_ref, out_ref):
    tokens, width = out_ref.shape
    left, masks = head_masks()
    for pair in range(HEADS // 2):
        at = pair * LANES
        q = qkv_ref[:, at : at + LANES] * SCALE
        k = qkv_ref[:, width + at : width + at + LANES]
        v = qkv_ref[:, 2 * width + at : 2 * width + at + LANES]
        all_scores = [dot(q * masks[side], k, 1, 1) for side in range(2)]
        mixed = []
        for scores in all_scores:
            raised = jnp.exp(scores - jnp.max(scores, axis=-1, keepdims=True))
            total = jnp.sum(raised, axis=-1, keepdims=True)
            mixed.append(dot(raised.astype(BF), v) * (1.0 / total))
        out_ref[:, at : at + LANES] = jnp.where(left, mixed[0], mixed[1]).astype(BF)


def window_forward(qkv, tokens, deps):
    total, width3 = qkv.shape
    width = width3 // 3
    rows = lambda w: pl.BlockSpec((tokens, w), lambda i: (i, 0))
    [att] = call(
        window_kernel,
        "window_forward",
        [(qkv, rows(width3))],
        [((total, width), BF, rows(width))],
        grid=(total // tokens,),
        deps=deps,
        work=(16 * total * tokens * width, 8e6, total * tokens * HEADS),
    )
    return att


def window_back_kernel(qkv_ref, go_ref, out_ref):
    tokens, width = go_ref.shape
    left, masks = head_masks()
    for pair in range(HEADS // 2):
        at = pair * LANES
        q = qkv_ref[:, at : at + LANES]
        k = qkv_ref[:, width + at : width + at + LANES]
        v = qkv_ref[:, 2 * width + at : 2 * width + at + LANES]
        g = go_ref[:, at : at + LANES]
        scaled = q * SCALE
        all_scores = [dot(k * masks[side], scaled, 1, 1) for side in range(2)]
        all_grads = [dot(v * masks[side], g, 1, 1) for side in range(2)]
        parts = []
        for scores, grads in zip(all_scores, all_grads):
            raised = jnp.exp(scores - jnp.max(scores, axis=0, keepdims=True))
            inverse = 1.0 / jnp.sum(raised, axis=0, keepdims=True)
            probs = raised * inverse
            inner = jnp.sum(probs * grads, axis=0, keepdims=True)
            dscore = (probs * (grads - inner)).astype(BF)
            parts.append((dot(dscore, k, 0, 0), dot(dscore, q), dot(probs.astype(BF), g)))
        for index, factor in ((0, SCALE), (1, SCALE), (2, 1.0)):
            joined = jnp.where(left, parts[0][index], parts[1][index]) * factor
            out_ref[:, index * width + at : index * width + at + LANES] = joined.astype(BF)


def window_backward(qkv, go, tokens, deps):
    total, width3 = qkv.shape
    width = width3 // 3
    rows = lambda w: pl.BlockSpec((tokens, w), lambda i: (i, 0))
    [out] = call(
        window_back_kernel,
        "window_backward",
        [(qkv, rows(width3)), (go, rows(width))],
        [((total, width3), BF, rows(width3))],
        grid=(total // tokens,),
        deps=deps,
        work=(40 * total * tokens * width, 1.3e7, total * tokens * HEADS),
    )
    return out


def split_halves(rows, part):
    count = rows.shape[0] // (2 * part)
    return [
        jnp.concatenate([rows[(2 * w + s) * part : (2 * w + s + 1) * part] for w in range(count)], axis=0)
        for s in range(2)
    ]


def patch_ffn_kernel(
    s_ref, att_ref, x_ref, own_ref, other_ref, gain_ref, wo_ref, up_ref, down_ref,
    out_own_ref, out_other_ref, after_grad_ref, att_grad_ref, wo_grad_ref, up_grad_ref, down_grad_ref, gain_grad_ref,
    after, normed, cot, total, acts, dacts,
    *, tiled, form,
):
    step = pl.program_id(0)
    tokens, width = att_ref.shape
    part = form[0] * WIN
    block = 4 * part
    back = after_grad_ref
    blocks = [slice(b * block, (b + 1) * block) for b in range(tokens // block)]

    @pl.when(step == 0)
    def _():
        cot[...] = into_windows(own_ref[0], other_ref[...], s_ref[SHIFT], *form).astype(BF)
        for rows in blocks:
            value = x_ref[rows, :].astype(F32) + dot(att_ref[rows, :], wo_ref[...])
            after[rows, :] = value
            unit, _ = norm_stats(value)
            normed[rows, :] = (unit * gain_ref[1:2, :]).astype(BF)

    def products(first):
        enter = lambda rows: (dot(normed[rows, :], up_ref[...]), dot(cot[rows, :], down_ref[...], 1, 1))
        ahead = enter(blocks[0])
        for b, rows in enumerate(blocks):
            pre, grads = ahead
            if b + 1 < len(blocks):
                ahead = enter(blocks[b + 1])
            value, slope = gelu_pair(pre)
            act = value.astype(BF)
            acts[rows, :] = act
            dact = (slope * grads).astype(BF)
            dacts[rows, :] = dact
            if first:
                total[rows, :] = dot(act, down_ref[...])
                back[rows, :] = dot(dact, up_ref[...], 1, 1)
            else:
                total[rows, :] += dot(act, down_ref[...])
                back[rows, :] += dot(dact, up_ref[...], 1, 1)

    @pl.when(step == 0)
    def _():
        products(True)

    @pl.when(step > 0)
    def _():
        products(False)

    put_grad(up_grad_ref, dot(normed[...], dacts[...], 0, 0).astype(BF), store_columns, 0, tiled)
    put_grad(down_grad_ref, dot(acts[...], cot[...], 0, 0).astype(BF), store_strips, 1, tiled)

    @pl.when(step == pl.num_programs(0) - 1)
    def _():
        gain_sum = jnp.zeros((1, width), F32)
        for rows in blocks:
            unit, spread = norm_stats(after[rows, :])
            grad, gain_part = norm_back(unit, spread, gain_ref[1:2, :], back[rows, :])
            gain_sum = gain_sum + gain_part
            grad = cot[rows, :].astype(F32) + grad
            after_grad_ref[rows, :] = grad
            branch = grad.astype(BF)
            normed[rows, :] = branch
            att_grad_ref[rows, :] = dot(branch, wo_ref[...], 1, 1).astype(BF)
        gain_grad_ref[...] = jnp.broadcast_to(gain_sum, gain_grad_ref.shape)
        put_grad(wo_grad_ref, dot(att_ref[...], normed[...], 0, 0).astype(BF), store_all, 0, tiled)
        halves = split_halves(after[...] + total[...], part)
        onehot = out_of_windows(s_ref[SHIFT], *form)
        out_own_ref[0] = dot(onehot, halves[0].astype(BF)).astype(BF)
        out_other_ref[...] = dot(onehot, halves[1].astype(BF)).astype(BF)


def patch_ffn(scalars, att, x, cot, cot_other, gains, wo, up, down, tiled, form, deps, chunk=768):
    tokens, width = att.shape
    half = tokens // 2
    hidden = up.shape[1]
    single = lambda a: (a, whole(a.shape, True))
    return call(
        functools.partial(patch_ffn_kernel, tiled=tiled, form=form),
        "patch_ffn",
        [
            single(att), single(x), (cot, page_block(cot.shape)), single(cot_other), single(gains), single(wo),
            (up, pl.BlockSpec((width, chunk), lambda j, *_: (0, j))),
            (down, pl.BlockSpec((chunk, width), lambda j, *_: (j, 0))),
        ],
        [
            (cot.shape, BF, page_block(cot.shape)),
            ((half, width), BF, whole((half, width))),
            ((tokens, width), F32, whole((tokens, width))),
            ((tokens, width), BF, whole((tokens, width))),
            *grad_forms(width, hidden, chunk, tiled, 0),
            ((8, width), F32, whole((8, width))),
        ],
        grid=(hidden // chunk,),
        scratch=[
            pltpu.VMEM((tokens, width), F32),
            pltpu.VMEM((tokens, width), BF),
            pltpu.VMEM((tokens, width), BF),
            pltpu.VMEM((tokens, width), F32),
            pltpu.VMEM((tokens, chunk), BF),
            pltpu.VMEM((tokens, chunk), BF),
        ],
        scalars=scalars,
        deps=deps,
        work=(12 * tokens * width * hidden, 4e7, tokens * hidden),
    )


def qkv_back_kernel(gp_ref, n_ref, w_ref, back_ref, w_grad_ref, *, tiled):
    first = dot(gp_ref[...], w_ref[...], 1, 1)

    @pl.when(pl.program_id(0) == 0)
    def _():
        back_ref[...] = first

    @pl.when(pl.program_id(0) > 0)
    def _():
        back_ref[...] += first

    put_grad(w_grad_ref, dot(n_ref[...], gp_ref[...], 0, 0).astype(BF), store_columns, 0, tiled)


def qkv_back(gp, normed, w, tiled, deps):
    tokens, width = normed.shape
    cols = w.shape[1]
    chunk = cols // 2
    natural = pl.BlockSpec((width, chunk), lambda j: (0, j))
    if tiled:
        form = (tile_shape(width, cols), BF, columns_spec(width, chunk, 1, 0, lambda j: j))
    else:
        form = (w.shape, BF, natural)
    return call(
        functools.partial(qkv_back_kernel, tiled=tiled),
        "qkv_back",
        [(gp, pl.BlockSpec((tokens, chunk), lambda j: (0, j))), (normed, whole(normed.shape, True)), (w, natural)],
        [((tokens, width), F32, whole((tokens, width))), form],
        grid=(2,),
        deps=deps,
        work=(4 * tokens * width * cols, 2e7, 0),
    )


def cross_back_kernel(
    s_ref, gk0_ref, gk1_ref, gv0_ref, gv1_ref, n_ref, x_ref, after_ref, part_ref, gain_ref, wx_ref, g2_ref, g4_ref,
    own_ref, other_ref, gain_grad_ref, *rest,
    tiled, form,
):
    step = pl.program_id(0)
    half, width = other_ref.shape
    tokens = 2 * half
    part = form[0] * WIN
    block = 4 * part
    back = rest[-1]

    def one(grad, base):
        back[...] = base[...] + dot(grad, wx_ref[...], 1, 1)
        w_grad = dot(n_ref[...], grad, 0, 0).astype(BF)
        if not tiled:
            rest[0][...] = w_grad
            return
        store_columns(rest[0], w_grad[:, : width // 2], 0)
        store_columns(rest[1], w_grad[:, width // 2 :], 1)

    @pl.when(step == 0)
    def _():
        one(jnp.concatenate([gk0_ref[...], gk1_ref[...]], axis=1), part_ref)

    @pl.when(step == 1)
    def _():
        one(jnp.concatenate([gv0_ref[...], gv1_ref[...]], axis=1), back)
        gain_sum = jnp.zeros((1, width), F32)
        for b in range(tokens // block):
            rows = slice(b * block, (b + 1) * block)
            unit, spread = norm_stats(x_ref[rows, :].astype(F32))
            grad, gain_part = norm_back(unit, spread, gain_ref[0:1, :], back[rows, :])
            gain_sum = gain_sum + gain_part
            back[rows, :] = after_ref[rows, :] + grad
        row = iota((8, width), 0)
        gain_grad_ref[...] = jnp.where(row == 0, gain_sum, jnp.where(row == 1, g2_ref[...], jnp.where(row == 3, g4_ref[...], 0.0)))
        halves = split_halves(back[...], part)
        onehot = out_of_windows(s_ref[SHIFT], *form)
        high = halves[0].astype(BF)
        low = (halves[0] - high.astype(F32)).astype(BF)
        own_ref[0] = dot(onehot, high) + dot(onehot, low)
        other_ref[...] = dot(onehot, halves[1].astype(BF)).astype(BF)


def cross_back(scalars, gks, gvs, normed, x, after, part, gains, wx, g2, g4, pages, tiled, form, deps):
    tokens, width = x.shape
    half = tokens // 2
    cols = wx.shape[1]
    if tiled:
        shape = tile_shape(width, cols // 2)
        grads = [(shape, BF, columns_spec(width, width // 2, 1, order, lambda j: j)) for order in (0, 1)]
    else:
        grads = [(wx.shape, BF, pl.BlockSpec((width, width), lambda j, *_: (0, j)))]
    single = lambda a: (a, whole(a.shape, True))
    own_shape = (pages, half, width)
    return call(
        functools.partial(cross_back_kernel, tiled=tiled, form=form),
        "cross_back",
        [single(a) for a in (*gks, *gvs, normed, x, after, part, gains)]
        + [(wx, pl.BlockSpec((width, width), lambda j, *_: (0, j))), single(g2), single(g4)],
        [
            (own_shape, F32, page_block(own_shape)),
            ((half, width), BF, whole((half, width))),
            ((8, width), F32, whole((8, width))),
            *grads,
        ],
        grid=(2,),
        scratch=[pltpu.VMEM((tokens, width), F32)],
        scalars=scalars,
        deps=deps,
        work=(4 * tokens * width * cols, 2e7, 0),
    )


def pair_rows(own, theirs, odd):
    return jnp.where(odd == 1, jnp.concatenate([theirs, own], axis=0), jnp.concatenate([own, theirs], axis=0))


def query_in_kernel(
    s_ref, seg_ref, ok_ref, own_ref, theirs_ref, gain_ref, w_ref, x_ref, n_ref, q_ref, kv_ref, same_ref, turned_ref
):
    own_slots = own_ref.shape[1]
    x = pair_rows(own_ref[0].astype(F32), theirs_ref[:own_slots, :].astype(F32), s_ref[ODD])
    slots, total = 2 * own_slots, seg_ref.shape[1]
    reach = slots + 64
    first = s_ref[UP] == 0
    segments = jnp.where(first, seg_ref[0:1, :], seg_ref[1:2, :]).astype(F32)
    amount = 32 - s_ref[BASE]
    near = pltpu.roll(jnp.broadcast_to(segments, (8, total)), jnp.where(amount < 0, amount + total, amount), 1)
    mine = jnp.where(first, ok_ref[0:1, :], ok_ref[1:2, :]).astype(F32)
    theirs = theirs_ref[own_slots : own_slots + 1, :own_slots].astype(F32)
    valid = jnp.where(s_ref[ODD] == 1, jnp.concatenate([theirs, mine], axis=1), jnp.concatenate([mine, theirs], axis=1))
    own = pltpu.roll(near, total - 32, 1)[0:1, :slots]
    own = jnp.where(valid > 0.5, own, -1.0)
    padded = -(-reach // LANES) * LANES
    column = near[:, :padded].T[:reach, 0:1]
    same = jnp.where(column == own, 1.0, 0.0)
    same_ref[...] = same.astype(BF)
    turned_ref[...] = same.T.astype(BF)
    x_ref[...] = x.astype(BF)
    unit, _ = norm_stats(x)
    normed = (unit * gain_ref[2:3, :]).astype(BF)
    n_ref[...] = normed
    width = x.shape[1]
    q_ref[...] = dot(normed, w_ref[:, :width]).astype(BF)
    kv_ref[...] = dot(normed, w_ref[:, width:]).astype(BF)


def query_in_call(scalars, segments, slots_ok, queries, theirs, gains, w, deps):
    _, own_slots, width = queries.shape
    slots = 2 * own_slots
    reach = slots + 64
    rows = lambda w: ((slots, w), BF, whole((slots, w)))
    return call(
        query_in_kernel,
        "query_in",
        [(segments, whole(segments.shape)), (slots_ok, whole(slots_ok.shape)), (queries, page_block(queries.shape))]
        + [(a, whole(a.shape)) for a in (theirs, gains, w)],
        [rows(width), rows(width), rows(width), rows(2 * width)]
        + [(shape, BF, whole(shape)) for shape in ((reach, slots), (slots, reach))],
        deps=deps,
        scalars=scalars,
        work=(2 * slots * width * w.shape[1], 5e6, 0),
    )


def forward_blocks(pieces, slots, group):
    if pieces > 1:
        blocks = [([(0, 0, slots - 32)], False), ([(0, slots - 32, 32), (1, 0, slots), (2, 0, 32)], True)]
        blocks.append(([(2, 32, slots - 32)], False))
        return blocks + [([(k, 0, slots)], False) for k in range(3, pieces)]
    blocks = [([(0, slots - 32, slots + 64)], True)]
    if slots > 32:
        blocks.append(([(0, 0, slots - 32)], False))
    at, total = 2 * slots + 32, slots * group
    while at < total:
        size = min(256, total - at)
        blocks.append(([(0, at, size)], False))
        at += size
    return blocks


def take(refs, block):
    parts = [refs[p][at : at + size, :] for p, at, size in block]
    return parts[0] if len(parts) == 1 else jnp.concatenate([p.astype(F32) for p in parts], axis=0).astype(parts[0].dtype)


def give(refs, block, value):
    done = 0
    for p, at, size in block:
        refs[p][at : at + size, :] = value[done : done + size].astype(refs[p].dtype)
        done += size


def query_forward_kernel(*refs, pieces, blocks):
    qs = refs[:pieces]
    k_ref, v_ref, sk_ref, sv_ref, kb_ref, same_ref = refs[pieces : pieces + 6]
    outs, held = refs[pieces + 6 : 2 * pieces + 6], refs[2 * pieces + 6 :]
    pair = pl.program_id(0)
    left, masks = head_masks()
    lane = iota((1, LANES), 1)

    @pl.when(pair == 0)
    def _():
        for h in held:
            h[...] = jnp.zeros_like(h)

    @pl.when(pair < HEADS // 2)
    def _():
        keys = [jnp.where(lane == 64 * (1 - side), kb_ref[...], k_ref[...]) for side in range(2)]
        marks = [jnp.where(lane == 64 * (1 - side), 1.0, 0.0).astype(BF) for side in range(2)]
        for block, near in blocks:
            q = take(qs, block) * SCALE
            size = q.shape[0]
            all_scores = [dot(q * masks[side] + marks[side], keys[side], 1, 1) for side in range(2)]
            if near:
                same = same_ref[...].astype(F32) > 0.5
                extras = [jnp.where(same, dot(q * masks[side], sk_ref[...], 1, 1), MASKED) for side in range(2)]
            mixed, columns = [], jnp.zeros((size, LANES), F32)
            for side in range(2):
                scores = all_scores[side]
                peak = jnp.max(scores, axis=-1, keepdims=True)
                if near:
                    peak = jnp.maximum(peak, jnp.max(extras[side], axis=-1, keepdims=True))
                raised = jnp.exp(scores - peak)
                total = jnp.sum(raised, axis=-1, keepdims=True)
                value = dot(raised.astype(BF), v_ref[...])
                if near:
                    raised = jnp.exp(extras[side] - peak)
                    total = total + jnp.sum(raised, axis=-1, keepdims=True)
                    value = value + dot(raised.astype(BF), sv_ref[...])
                mixed.append(value * (1.0 / total))
                columns = columns + place_lanes(peak + jnp.log(total), lane, 2 * pair + side)
            give(outs, block, jnp.where(left, mixed[0], mixed[1]))
            done = 0
            for p, at, rows in block:
                held[p][at : at + rows, :] += columns[done : done + rows]
                done += rows

    @pl.when(pair == HEADS // 2)
    def _():
        for out, h in zip(outs, held):
            out[...] = h[...].astype(BF)


def query_forward(qs, cross, slot_kv, key_bias, same, blocks, deps):
    width = qs[0].shape[1]
    patches, slots = cross.shape[0], slot_kv.shape[0]
    pairs = HEADS // 2
    total = sum(q.shape[0] for q in qs)
    col = lambda rows, first: pl.BlockSpec((rows, LANES), lambda p: (0, first + jnp.minimum(p, pairs - 1)))
    return call(
        functools.partial(query_forward_kernel, pieces=len(qs), blocks=blocks),
        "query_forward",
        [(q, col(q.shape[0], 0)) for q in qs]
        + [(cross, col(patches, 0)), (cross, col(patches, pairs)), (slot_kv, col(slots, 0)), (slot_kv, col(slots, pairs))]
        + [(a, whole(a.shape)) for a in (key_bias, same)],
        [((q.shape[0], width + LANES), BF, pl.BlockSpec((q.shape[0], LANES), lambda p: (0, p))) for q in qs],
        grid=(pairs + 1,),
        scratch=[pltpu.VMEM((q.shape[0], LANES), F32) for q in qs],
        deps=deps,
        work=(16 * total * patches * width, 1e7, total * patches * HEADS),
    )


def stat_lanes(stats, head, first, base):
    row, col = iota((LANES, LANES), 0), iota((LANES, LANES), 1)
    hit = (row == first + head + 16 * (col - base)) & (col >= base) & (col < base + 3)
    return dot(stats, jnp.where(hit, -1.0, 0.0).astype(BF)).astype(BF)


def query_back_kernel(*refs, pieces, blocks, near_block, first_pair):
    qs, gos, stats = refs[:pieces], refs[pieces : 2 * pieces], refs[2 * pieces : 3 * pieces]
    k_ref, v_ref, sk_ref, sv_ref, kb_ref, same_ref = refs[3 * pieces : 3 * pieces + 6]
    dqs = refs[3 * pieces + 6 : 4 * pieces + 6]
    dk_ref, dv_ref, dsk_ref, dsv_ref, sum_k, sum_v = refs[4 * pieces + 6 : 4 * pieces + 12]
    near_dqs = refs[4 * pieces + 12 :]
    pair = pl.program_id(0) + first_pair
    left, masks = head_masks()
    lane = iota((1, LANES), 1)
    bases = (64, 0)
    ones = [jnp.where((lane >= b) & (lane < b + 3), 1.0, 0.0).astype(BF) for b in bases]
    plain = [jnp.where(lane == b + 3, 1.0, 0.0).astype(BF) for b in bases]
    keys = [jnp.where(lane == bases[s] + 3, kb_ref[...], k_ref[...] * masks[s] + ones[s]) for s in range(2)]
    values = [v_ref[...] * masks[s] + ones[s] for s in range(2)]

    def sides(block):
        q, g, st = take(qs, block), take(gos, block), take(stats, block)
        scaled = q * SCALE
        shifted = [scaled * masks[s] + (stat_lanes(st, 2 * pair + s, 0, bases[s]) + plain[s]) for s in range(2)]
        lowered = [g * masks[s] + stat_lanes(st, 2 * pair + s, 48, bases[s]) for s in range(2)]
        return q, g, shifted, lowered

    for ref in near_dqs:
        ref[...] = jnp.zeros_like(ref)
    q, g, shifted, lowered = sides(near_block)
    same = same_ref[...].astype(F32) > 0.5
    moved, dsk, dsv = [], [], []
    for s in range(2):
        scores = dot(sk_ref[...] * masks[s] + ones[s], shifted[s], 1, 1)
        probs = jnp.exp(jnp.where(same, scores, MASKED))
        dscore = (probs * dot(sv_ref[...] * masks[s] + ones[s], lowered[s], 1, 1)).astype(BF)
        dsk.append(dot(dscore, q))
        dsv.append(dot(probs.astype(BF), g))
        moved.append(dot(dscore, sk_ref[...], 0, 0))
    give(near_dqs, near_block, jnp.where(left, moved[0], moved[1]))
    dsk_ref[...] = (jnp.where(left, dsk[0], dsk[1]) * SCALE).astype(BF)
    dsv_ref[...] = jnp.where(left, dsv[0], dsv[1]).astype(BF)

    for number, block in enumerate(blocks):
        q, g, shifted, lowered = sides(block)
        scores = [dot(keys[s], shifted[s], 1, 1) for s in range(2)]
        grads = [dot(values[s], lowered[s], 1, 1) for s in range(2)]
        dq, dk, dv = [], [], []
        for s in range(2):
            probs = jnp.exp(scores[s])
            dscore = (probs * grads[s]).astype(BF)
            dv.append(dot(probs.astype(BF), g))
            dk.append(dot(dscore, q))
            dq.append(dot(dscore, k_ref[...], 0, 0))
        near = take(near_dqs, block)
        give(dqs, block, (jnp.where(left, dq[0], dq[1]) + near) * SCALE)
        if number == 0:
            sum_k[...] = jnp.where(left, dk[0], dk[1])
            sum_v[...] = jnp.where(left, dv[0], dv[1])
        else:
            sum_k[...] += jnp.where(left, dk[0], dk[1])
            sum_v[...] += jnp.where(left, dv[0], dv[1])
    dk_ref[...] = (sum_k[...] * SCALE).astype(BF)
    dv_ref[...] = sum_v[...].astype(BF)


def query_backward(qs, gos, cross, slot_kv, key_bias, same, near_block, part, deps):
    patches, slots = cross.shape[0], slot_kv.shape[0]
    pairs = HEADS // 2
    count = pairs // 2
    width = count * LANES
    total = sum(q.shape[0] for q in qs)
    blocks = []
    for number, q in enumerate(qs):
        step = min(256, q.shape[0])
        blocks += [[(number, at, step)] for at in range(0, q.shape[0], step)]
    col = lambda rows, first: pl.BlockSpec((rows, LANES), lambda p: (0, first + part * count + p))
    out = lambda rows: ((rows, width), BF, pl.BlockSpec((rows, LANES), lambda p: (0, p)))
    found = call(
        functools.partial(
            query_back_kernel, pieces=len(qs), blocks=blocks, near_block=near_block, first_pair=part * count
        ),
        "query_backward",
        [(q, col(q.shape[0], 0)) for q in qs]
        + [(g, col(g.shape[0], 0)) for g in gos]
        + [(g, pl.BlockSpec((g.shape[0], LANES), lambda p: (0, pairs))) for g in gos]
        + [(cross, col(patches, 0)), (cross, col(patches, pairs)), (slot_kv, col(slots, 0)), (slot_kv, col(slots, pairs))]
        + [(a, whole(a.shape)) for a in (key_bias, same)],
        [out(q.shape[0]) for q in qs] + [out(patches), out(patches), out(slots), out(slots)],
        grid=(count,),
        scratch=[pltpu.VMEM((patches, LANES), F32)] * 2 + [pltpu.VMEM((q.shape[0], LANES), F32) for q in qs],
        deps=deps,
        work=(20 * total * patches * width, 1.5e7, total * patches * HEADS // 2),
    )
    return found[: len(qs)], *found[len(qs) :]


def query_ffn_kernel(s_ref, *refs, parts, tiled):
    outs = refs[:parts]
    x_ref, own_ref, theirs_ref, gain_ref, wo_ref, up_ref, down_ref = refs[parts : parts + 7]
    (
        out_own_ref, out_other_ref, grad_ref, send_ref, att_ref, normed_ref, act_ref, dact_ref, branch_ref, cot_ref,
        gain_grad_ref, mixed, after, total, back, joint,
    ) = refs[parts + 7 :]
    step = pl.program_id(0)
    width = x_ref.shape[1]

    @pl.when(step == 0)
    def _():
        each = [join_lanes(o[:, width:].astype(F32), 0) for o in outs]
        peak = functools.reduce(jnp.maximum, each)
        weights = [jnp.exp(e - peak) for e in each]
        weight_sum = functools.reduce(jnp.add, weights)
        joint[...] = peak + jnp.log(weight_sum)
        value = None
        for o, w in zip(outs, weights):
            term = o[:, :width].astype(F32) * spread_heads(w / weight_sum, width)
            value = term if value is None else value + term
        mixed[...] = value
        att_ref[...] = value.astype(BF)
        rows = x_ref[...].astype(F32) + dot(att_ref[...], wo_ref[...])
        after[...] = rows
        unit, _ = norm_stats(rows)
        normed_ref[...] = (unit * gain_ref[3:4, :]).astype(BF)
        cot_ref[...] = pair_rows(own_ref[0].astype(F32), theirs_ref[...].astype(F32), s_ref[ODD]).astype(BF)
        total[...] = jnp.zeros_like(total)
        back[...] = jnp.zeros_like(back)

    grads = dot(cot_ref[...], down_ref[...], 1, 1)
    value, slope = gelu_pair(dot(normed_ref[...], up_ref[...]))
    dact = (slope * grads).astype(BF)
    dact_ref[...] = dact
    back[...] += dot(dact, up_ref[...], 1, 1)
    act = value.astype(BF)
    act_ref[...] = act
    total[...] += dot(act, down_ref[...])

    @pl.when(step == pl.num_programs(0) - 1)
    def _():
        rows = after[...] + total[...]
        own_slots = rows.shape[0] // 2
        low, high = rows[:own_slots], rows[own_slots:]
        odd = s_ref[ODD] == 1
        out_own_ref[0] = jnp.where(odd, high, low).astype(BF)
        out_other_ref[...] = jnp.where(odd, low, high).astype(BF)
        unit, spread = norm_stats(after[...])
        grad, gain_part = norm_back(unit, spread, gain_ref[3:4, :], back[...])
        gain_grad_ref[...] = jnp.broadcast_to(gain_part, gain_grad_ref.shape)
        grad = cot_ref[...].astype(F32) + grad
        grad_ref[...] = grad
        branch = grad.astype(BF)
        branch_ref[...] = branch
        sent = dot(branch, wo_ref[...], 1, 1).astype(BF)
        send_ref[:, :width] = sent
        pick = (iota((width, LANES), 0) // (width // HEADS) == iota((width, LANES), 1)).astype(F32).astype(BF)
        high, middle, low = three_parts(sent.astype(F32) * mixed[...])
        inner = dot(high.astype(BF), pick) + dot(middle.astype(BF), pick) + dot(low.astype(BF), pick)
        lane = iota((1, LANES), 1)
        packed = jnp.zeros(inner.shape, F32)
        for source, first in ((joint[...], 0), (inner, 48)):
            kept = jnp.where(lane < HEADS, source, 0.0)
            for number, piece in enumerate(three_parts(kept)):
                amount = first + 16 * number
                packed = packed + (piece if amount == 0 else pltpu.roll(piece, amount, 1))
        send_ref[:, width:] = packed.astype(BF)


def query_ffn(scalars, outs, x, cot, cot_theirs, gains, wo, up, down, tiled, deps, chunk=768):
    slots, width = x.shape
    hidden = up.shape[1]
    rows = lambda w, kind: ((slots, w), kind, whole((slots, w)))
    chunks = ((slots, hidden), BF, pl.BlockSpec((slots, chunk), lambda j, *_: (0, j)))
    half = (slots // 2, width)
    return call(
        functools.partial(query_ffn_kernel, parts=len(outs), tiled=tiled),
        "query_ffn",
        [(a, whole(a.shape)) for a in (*outs, x)]
        + [(cot, page_block(cot.shape))]
        + [(a, whole(a.shape)) for a in (cot_theirs, gains, wo)]
        + [
            (up, pl.BlockSpec((width, chunk), lambda j, *_: (0, j))),
            (down, pl.BlockSpec((chunk, width), lambda j, *_: (j, 0))),
        ],
        [
            (cot.shape, BF, page_block(cot.shape)), (half, BF, whole(half)), rows(width, F32), rows(width + LANES, BF),
            rows(width, BF), rows(width, BF), chunks, chunks, rows(width, BF), rows(width, BF), ((8, width), F32, whole((8, width))),
        ],
        grid=(hidden // chunk,),
        scratch=[pltpu.VMEM((slots, width), F32)] * 4 + [pltpu.VMEM((slots, LANES), F32)],
        scalars=scalars,
        deps=deps,
        work=(8 * slots * width * hidden, 2e7, slots * hidden),
    )


def query_weights_kernel(normed_ref, cot_ref, att_ref, branch_ref, act_ref, dact_ref, wo_ref, up_ref, down_ref, *, tiled):
    put_grad(up_ref, dot(normed_ref[...], dact_ref[...], 0, 0).astype(BF), store_columns, 0, tiled)
    put_grad(down_ref, dot(act_ref[...], cot_ref[...], 0, 0).astype(BF), store_strips, 1, tiled)

    @pl.when(pl.program_id(0) == 0)
    def _():
        put_grad(wo_ref, dot(att_ref[...], branch_ref[...], 0, 0).astype(BF), store_all, 1, tiled)


def query_weights(normed, cot, att, branch, act, dact, tiled, deps, chunk=768):
    slots, width = normed.shape
    hidden = act.shape[1]
    return call(
        functools.partial(query_weights_kernel, tiled=tiled),
        "query_weights",
        [(a, whole((slots, width))) for a in (normed, cot, att, branch)]
        + [(a, pl.BlockSpec((slots, chunk), lambda j: (0, j))) for a in (act, dact)],
        grad_forms(width, hidden, chunk, tiled, 1),
        grid=(hidden // chunk,),
        deps=deps,
        work=(4 * slots * width * hidden, 1.6e7, 0),
    )


def query_out_kernel(s_ref, *refs, parts, tiled):
    halves = [refs[:parts], refs[parts : 2 * parts]]
    others = refs[2 * parts : 2 * parts + 4]
    n_ref, x_ref, grad_ref, gain_ref, w_ref, rows_ref = refs[2 * parts + 4 : 2 * parts + 10]
    own_ref, other_ref, w_grad_ref, gain_grad_ref = refs[2 * parts + 10 : 2 * parts + 14]
    width = x_ref.shape[1]
    sums = []
    for dqs in halves:
        value = dqs[0][...].astype(F32)
        for d in dqs[1:]:
            value = value + d[...].astype(F32)
        sums.append(value.astype(BF))
    join = lambda a, b: jnp.concatenate([a, b], axis=1)
    pieces = [join(*sums), join(others[0][...], others[1][...]), join(others[2][...], others[3][...])]
    back = None
    for number, piece in enumerate(pieces):
        cols = slice(number * width, (number + 1) * width)
        term = dot(piece, w_ref[:, cols], 1, 1)
        back = term if back is None else back + term
        (refs[-1] if tiled else w_grad_ref)[:, cols] = dot(n_ref[...], piece, 0, 0).astype(BF)
    if tiled:
        store_all(w_grad_ref, refs[-1][...], 1)
    unit, spread = norm_stats(x_ref[...].astype(F32))
    grad, gain_part = norm_back(unit, spread, gain_ref[2:3, :], back)
    rows = grad_ref[...] + grad
    own_slots = rows.shape[0] // 2
    low, high = rows[:own_slots], rows[own_slots:]
    odd = s_ref[ODD] == 1
    own_ref[0] = jnp.where(odd, high, low)
    other_ref[...] = jnp.where(odd, low, high).astype(BF)
    gain_rows = rows_ref[...] + jnp.where(iota((8, width), 0) == 2, gain_part, 0.0)
    if not tiled:
        gain_grad_ref[...] = gain_rows
        return
    turned = gain_rows.T
    size = width // 16
    lane = iota((1, LANES), 1)
    for half in range(2):
        tile = jnp.where(lane == 0, turned[:, 2 * half : 2 * half + 1], 0.0)
        tile = jnp.where(lane == 1, turned[:, 2 * half + 1 : 2 * half + 2], tile).astype(BF)
        for strip in range(8):
            for core in range(2):
                at = (2 * strip + core) * size
                gain_grad_ref[(core, *tile_index(strip, half, 0), slice(None), slice(None))] = tile[at : at + size]


def query_out(scalars, dqs, dks, dvs, normed, x, grad, gains, w, gain_rows, pages, tiled, deps):
    slots, width = x.shape
    own_shape = (pages, slots // 2, width)
    w_shape = tile_shape(width, w.shape[1]) if tiled else w.shape
    g_shape, g_kind = (tile_shape(width, 256), BF) if tiled else ((8, width), F32)
    ins = (*dqs[0], *dqs[1], *dks, *dvs, normed, x, grad, gains, w, gain_rows)
    return call(
        functools.partial(query_out_kernel, parts=len(dqs[0]), tiled=tiled),
        "query_out",
        [(a, whole(a.shape, True)) for a in ins],
        [
            (own_shape, F32, page_block(own_shape)),
            ((slots // 2, width), BF, whole((slots // 2, width))),
            (w_shape, BF, whole(w_shape)),
            (g_shape, g_kind, whole(g_shape)),
        ],
        scratch=[pltpu.VMEM(w.shape, BF)] if tiled else [],
        scalars=scalars,
        deps=deps,
        work=(4 * slots * width * w.shape[1], 1e7, 0),
    )


PAIR = pl.DeviceIdType.MESH


def coordinates():
    page, strip = lax.axis_index("page"), lax.axis_index("strip")
    core, x = lax.rem(page, 2), page // 2
    y, z_low, z_high = lax.rem(strip, 2), lax.rem(strip // 2, 2), strip // 4
    flip = lambda index, bit, weight: index + weight - 2 * weight * bit
    core_mate = (flip(page, core, 1), strip)
    mates = {
        "x": (x, (flip(page, x, 2), strip)),
        "y": (y, (page, flip(strip, y, 1))),
        "low": (z_low, (page, flip(strip, z_low, 2))),
        "high": (z_high, (page, flip(strip, z_high, 4))),
    }
    return core, core_mate, [[mates[k] for k in ("y", "x", "low", "high")], [mates[k] for k in ("x", "y", "low", "high")]]


def meet(mates):
    barrier = pltpu.get_barrier_semaphore()
    for mate in mates:
        pl.semaphore_signal(barrier, inc=1, device_id=mate, device_id_type=PAIR)
    pl.semaphore_wait(barrier, len(mates))


def send(source, target, sems, number, mate):
    copy = pltpu.make_async_remote_copy(
        src_ref=source,
        dst_ref=target,
        send_sem=sems.at[0, number],
        recv_sem=sems.at[1, number],
        device_id=mate,
        device_id_type=PAIR,
    )
    copy.start()
    return copy


def add_rows(target, first, source, start, length, at, rows):
    span = pl.ds(at, rows)

    def step(i, carry):
        total = target[first + i, span, :].astype(F32) + source[start + i, span, :].astype(F32)
        target[first + i, span, :] = total.astype(BF)
        return carry

    lax.fori_loop(0, length, step, 0)


def query_sum_kernel(*refs, rows):
    up_ref, down_ref, wo_ref, normed_ref, cot_ref, att_ref, branch_ref, act_ref, dact_ref = refs[:9]
    outs = refs[9:13]
    own_up, own_down, own_wo, held_0, held_1, remote, near = refs[13:]
    held = (held_0, held_1)
    core, core_mate, orders = coordinates()
    meet([core_mate])
    wide, small = rows
    far, mine = [], []
    for number, (grad, order, at, size) in enumerate(((up_ref, 0, 0, wide), (down_ref, 1, 0, wide), (wo_ref, 0, 2 * wide, small))):
        span, bit = pl.ds(at, size), orders[order][0][0]
        far.append(send(grad.at[1 - core], held[order].at[:, :, :, span, :], remote, number, core_mate))
        for which in range(2):
            first = bit if which else 1 - bit
            copy = pltpu.make_async_copy(
                grad.at[core, first], outs[2 * order + which].at[:, :, span, :], near.at[2 * number + which]
            )
            copy.start()
            mine.append(copy)
    width = normed_ref.shape[1]
    own_rows = ((own_up, 0, wide, wide), (own_down, 1, wide, wide), (own_wo, 1, 2 * wide, small))
    store_all(own_wo, dot(att_ref[...], branch_ref[...], 0, 0).astype(BF), 1)
    for j in range(act_ref.shape[1] // width):
        cols = slice(j * width, (j + 1) * width)
        store_columns(own_up, dot(normed_ref[...], dact_ref[:, cols], 0, 0).astype(BF), 0, j // 2, (j % 2) * (width // LANES))
        store_strips(own_down, dot(act_ref[:, cols], cot_ref[...], 0, 0).astype(BF), 1, (j % 2) * 2 + j // 2)
    later = []
    for number, (grad, order, at, size) in enumerate(own_rows):
        later.append(send(grad.at[1 - core], held[order].at[:, :, :, pl.ds(at, size), :], remote, 3 + number, core_mate))
    for copy in far + mine:
        copy.wait()

    def add(order, at, size, own):
        bit = orders[order][0][0]
        span = pl.ds(at, size)
        for which in range(2):
            out, first = outs[2 * order + which], bit if which else 1 - bit
            for i in range(2):

                def step(z, carry, out=out, first=first, i=i):
                    mine = out[i, z, span, :] if own is None else own[core, first, i, z]
                    out[i, z, span, :] = (mine.astype(F32) + held[order][first, i, z, span, :].astype(F32)).astype(BF)
                    return carry

                lax.fori_loop(0, 4, step, 0)

    for order, at, size in ((0, 0, wide), (1, 0, wide), (0, 2 * wide, small)):
        add(order, at, size, None)
    for copy, (grad, order, at, size) in zip(later, own_rows):
        copy.wait()
        add(order, at, size, grad)


def query_sum(patch_grads, normed, cot, att, branch, act, dact, collective, deps):
    width, hidden = normed.shape[1], act.shape[1]
    shapes = [tile_shape(width, hidden), tile_shape(hidden, width), tile_shape(width, width)]
    rows = (shapes[0][-2], shapes[2][-2])
    total = 2 * rows[0] + rows[1]
    vmem = pl.BlockSpec(memory_space=pltpu.VMEM)
    kernel = functools.partial(query_sum_kernel, rows=rows)
    outs = pl.pallas_call(
        lambda *refs: kernel(*refs[:9], *refs[9 + len(deps) :]),
        in_specs=[ANY] * 3 + [vmem] * 6 + [ANY] * len(deps),
        out_specs=[vmem] * 4,
        out_shape=[sds((2, 4, total, LANES), BF)] * 4,
        scratch_shapes=[
            *[pltpu.VMEM(shape, BF) for shape in shapes],
            pltpu.VMEM((2, 2, 4, total, LANES), BF),
            pltpu.VMEM((2, 2, 4, total, LANES), BF),
            pltpu.SemaphoreType.DMA((2, 6)),
            pltpu.SemaphoreType.DMA((6,)),
        ],
        compiler_params=pltpu.CompilerParams(collective_id=collective, has_side_effects=True, vmem_limit_bytes=VMEM_BYTES),
        name="query_sum",
    )(*patch_grads, normed, cot, att, branch, act, dact, *deps)
    return [out.reshape(8, total, LANES) for out in outs]


ORDERS = (("y", "x", "low", "high"), ("x", "y", "low", "high"))
PLACES = {"x": BIT_X, "y": BIT_Y, "low": BIT_LOW, "high": BIT_HIGH}


def across(array, name):
    axis, weight = {"x": ("page", 2), "y": ("strip", 1), "low": ("strip", 2), "high": ("strip", 4)}[name]
    return lax.ppermute(array, axis, [(i, i ^ weight) for i in range(lax.axis_size(axis))])


def halve_add_kernel(s_ref, *refs):
    for k in range(4):
        keep, got, out = refs[2 * k], refs[2 * k + 1], refs[8 + k]
        out[...] = (keep[...].astype(F32) + got[...].astype(F32)).astype(BF)


def halve_add(scalars, kept, got, stage, deps):
    ins, outs = [], []
    for order in range(2):
        size = kept[order].shape[0] // 2
        shape = kept[order].shape[1:]
        place = PLACES[ORDERS[order][stage]]
        for flip in (1, 0):
            spec = pl.BlockSpec(
                (1, *shape),
                lambda i, s, place=place, flip=flip, size=size: ((1 - s[place] if flip else s[place]) * size + i, 0, 0),
            )
            ins += [(kept[order], spec), (got[order], spec)]
            outs.append(((size, *shape), BF, pl.BlockSpec((1, *shape), lambda i, s: (i, 0, 0))))
    return call(
        halve_add_kernel, "halve_add", ins, outs, grid=(size,), scalars=scalars, deps=deps, work=(1e6, 6 * size * 1296 * 512, 0)
    )


def late_sum_kernel(*refs, lots, arrays, early_rows):
    grads = refs[:arrays]
    early = refs[arrays : arrays + 4]
    own, got = refs[arrays + 4 : arrays + 6], refs[arrays + 6 : arrays + 8]
    sums, first_held = refs[arrays + 8 : arrays + 10], refs[arrays + 10 : arrays + 12]
    held = [refs[arrays + 12 : arrays + 16], refs[arrays + 16 : arrays + 20]]
    done, loaded, early_held = refs[arrays + 20 : arrays + 22], refs[arrays + 22 : arrays + 26], refs[arrays + 26 : arrays + 28]
    remote, near = refs[arrays + 28 :]
    core, core_mate, orders = coordinates()
    meet([core_mate] + [mate for _, mate in orders[0]])
    numbers, local_numbers = iter(range(1000)), iter(range(1000))
    jobs = []
    for order, at, members in lots:
        copies, first = [], at
        for member, start, rows in members:
            there, span = pl.ds(start, rows), pl.ds(first, rows)
            first += rows
            copies.append(
                send(grads[member].at[1 - core, :, there, :], first_held[order].at[:, span, :], remote, next(numbers), core_mate)
            )
            copy = pltpu.make_async_copy(
                grads[member].at[core, :, there, :], sums[order].at[:, span, :], near.at[next(local_numbers)]
            )
            copy.start()
            copies.append(copy)
        jobs.append((order, at, first - at, copies))
    loads = []
    for k in range(4):
        copy = pltpu.make_async_copy(early[k], loaded[k], near.at[next(local_numbers)])
        copy.start()
        loads.append(copy)
    for copy in loads:
        copy.wait()
    early_flights = []
    for order in range(2):
        bit, mate = orders[order][3]
        kept = loaded[2 * order]
        add_rows(kept, 1 - bit, loaded[2 * order + 1], 1 - bit, 1, 0, early_rows)
        early_flights.append(send(kept.at[1 - bit], early_held[order], remote, next(numbers), mate))
        add_rows(kept, bit, loaded[2 * order + 1], bit, 1, 0, early_rows)
    bases = [0] * len(jobs)
    flights = [None] * len(jobs)
    first_exchange = []
    for stage in range(4):
        size = 8 >> stage
        for n, (order, at, rows, copies) in enumerate(jobs):
            source = first_held[order] if stage == 0 else held[order][stage - 1]
            for copy in copies if stage == 0 else [flights[n]]:
                copy.wait()
            bit, mate = orders[order][stage]
            out, keep = size * (1 - bit), size * bit
            base = bases[n]
            add_rows(sums[order], base + out, source, out, size, at, rows)
            flights[n] = send(
                sums[order].at[pl.ds(base + out, size), pl.ds(at, rows), :],
                held[order][stage].at[:, pl.ds(at, rows), :],
                remote,
                next(numbers),
                mate,
            )
            add_rows(sums[order], base + keep, source, keep, size, at, rows)
            bases[n] = base + keep
        if stage == 2:
            for order in range(2):
                early_flights[order].wait()
                total = loaded[2 * order][orders[order][3][0]].astype(F32) + early_held[order][...].astype(F32)
                own[order][:early_rows, :] = total.astype(BF)
                span = pl.ds(0, early_rows)
                first_exchange.append(send(own[order].at[span, :], done[order].at[span, :], remote, next(numbers), core_mate))
    exchange = []
    for n, (order, at, rows, _) in enumerate(jobs):
        flights[n].wait()
        value = sums[order][bases[n], pl.ds(at, rows), :].astype(F32) + held[order][3][0, pl.ds(at, rows), :].astype(F32)
        span = pl.ds(early_rows + at, rows)
        own[order][span, :] = value.astype(BF)
        exchange.append(send(own[order].at[span, :], done[order].at[span, :], remote, next(numbers), core_mate))
    for copy in first_exchange + exchange:
        copy.wait()
    for order in range(2):
        got[order][...] = done[order][...]


def late_sum(grads, lots, rows, early, collective, deps):
    grads = [g.reshape(2, 16, *g.shape[-2:]) for g in grads]
    arrays = len(grads)
    members = sum(len(lot[2]) for lot in lots)
    early_rows = early[0].shape[1]
    share = [sds((early_rows + r, LANES), BF) for r in rows]
    vmem = lambda *shape: pltpu.VMEM(shape, BF)
    kernel = functools.partial(late_sum_kernel, lots=lots, arrays=arrays, early_rows=early_rows)
    first = arrays + 4
    return pl.pallas_call(
        lambda *refs: kernel(*refs[:first], *refs[first + len(deps) :]),
        in_specs=[ANY] * (first + len(deps)),
        out_specs=[pl.BlockSpec(memory_space=pltpu.VMEM)] * 4,
        out_shape=share + share,
        scratch_shapes=[
            *[vmem(16, r, LANES) for r in rows],
            *[vmem(16, r, LANES) for r in rows],
            *[vmem(8 >> k, rows[0], LANES) for k in range(4)],
            *[vmem(8 >> k, rows[1], LANES) for k in range(4)],
            *[vmem(early_rows + r, LANES) for r in rows],
            *[vmem(2, early_rows, LANES)] * 4,
            *[vmem(early_rows, LANES)] * 2,
            pltpu.SemaphoreType.DMA((2, members + 5 * len(lots) + 4)),
            pltpu.SemaphoreType.DMA((members + 4,)),
        ],
        compiler_params=pltpu.CompilerParams(collective_id=collective, has_side_effects=True, vmem_limit_bytes=VMEM_BYTES),
        name="late_sum",
    )(*grads, *early, *deps)


def finish_kernel(core_ref, own0, own1, got0, got1, gain_ref, *outs, plan):
    first = core_ref[0] == 0
    owns, gots = (own0, own1), (got0, got1)
    lane = iota((1, LANES), 1)
    left = lane < 64

    def tile(order, at, size, part):
        mine = owns[order][at : at + size, :].astype(F32)
        theirs = gots[order][at : at + size, :].astype(F32)
        return jnp.where(first == (part == 0), mine, theirs)

    for out, (size, tiles, flipped) in zip(outs, plan):
        count = len(tiles)
        for part in range(2):
            rows = slice(part * size, (part + 1) * size)
            values = [tile(order, at, size, part) for order, at in tiles]
            if count % 2 == 0:
                for t in range(count // 2):
                    out[rows, t * LANES : (t + 1) * LANES] = jnp.where(first, values[t], values[t + count // 2])
                continue
            turned = [pltpu.roll(v, 64, 1) for v in values[count // 2 :]]
            whole_tiles = [
                jnp.where(first, values[t], jnp.where(left, turned[t], turned[t + 1])) for t in range(count // 2)
            ]
            rest = jnp.where(first, values[count // 2], turned[-1])
            if flipped:
                for t, value in enumerate(whole_tiles):
                    for at in range(0, size, 64):
                        column = part * size + at
                        out[t * LANES : (t + 1) * LANES, column : column + 64] = value[at : at + 64].T
                for at in range(0, size, 64):
                    column = part * size + at
                    out[count // 2 * LANES :, column : column + 64] = rest[at : at + 64].T[:64]
                continue
            for t, value in enumerate(whole_tiles):
                out[rows, t * LANES : (t + 1) * LANES] = value
            out[rows, count // 2 * LANES :] = rest[:, :64]
    size = gain_ref.shape[1] // 2
    at = own0.shape[0] - size
    gain = jnp.concatenate([tile(0, at, size, part) for part in range(2)], axis=0).T
    gain_ref[...] = jnp.where(first, gain[0:1], gain[1:2])


def finish(core, shares, shapes, plan, gain_rows):
    vmem = pl.BlockSpec(memory_space=pltpu.VMEM)
    outs = [shape[::-1] if flipped else shape for shape, (_, _, flipped) in zip(shapes, plan)]
    gain, *found = pl.pallas_call(
        functools.partial(finish_kernel, plan=plan),
        in_specs=[pl.BlockSpec(memory_space=pltpu.SMEM)] + [vmem] * 4,
        out_specs=[vmem] * (1 + len(outs)),
        out_shape=[sds((1, gain_rows), F32)] + [sds(shape, F32) for shape in outs],
        compiler_params=pltpu.CompilerParams(vmem_limit_bytes=VMEM_BYTES),
        name="finish",
    )(core, *shares)
    return gain.T, *[f.T if flipped else f for f, (_, _, flipped) in zip(found, plan)]


def from_ahead(array, count, distance):
    return lax.ppermute(array, "strip", [(i, (i - distance) % count) for i in range(count)])


def from_partner(array, count):
    return lax.ppermute(array, "strip", [(i, i ^ 1) for i in range(count)])


def scattered(grad):
    strips, pages = lax.axis_size("strip"), lax.axis_size("page")
    rows, cols = grad.shape
    part = lax.psum_scatter(grad, "strip", scatter_dimension=0, tiled=True)
    part = part.reshape(rows // strips, pages, cols // pages).transpose(1, 0, 2)
    return lax.psum_scatter(part, "page", scatter_dimension=0, tiled=False).astype(F32)


def local(
    visual_in, query_in, row_valid, segment_ids, slot_valid, col_shift, row_shifted, norm_gains,
    w_vqkv, w_vout, w_up, w_down, w_qqkv, w_xkv, w_qout, w_qup, w_qdown, visual_cot, query_cot,
):
    pages, strip_rows, columns, width = visual_in.shape
    own_slots, all_slots = query_in.shape[1], segment_ids.shape[1]
    count = lax.axis_size("strip")
    tiled = count == 8
    group = count // 2
    half = strip_rows * columns
    slots = 2 * own_slots
    window = WIN * WIN
    form = (strip_rows, columns)
    place, page = lax.axis_index("strip"), lax.axis_index("page")
    odd = place % 2
    up = jnp.where(odd == 1, 1 - row_shifted[0], row_shifted[0])
    down = 1 - up
    pick = lambda array, which: lax.dynamic_index_in_dim(array, which, 0, keepdims=False)
    scalars = jnp.stack([up, pick(col_shift, up), odd, page % 2, page // 2, odd, place // 2 % 2, place // 4, (place // 2) * slots]).astype(jnp.int32)

    visual, cot = visual_in.reshape(pages, half, width), visual_cot.reshape(pages, half, width)
    query_sent, patch_sent = pack(scalars, [(query_in, slot_valid), (visual, row_valid)])
    query_theirs = from_partner(query_sent, count)
    patch_sent = held_back(patch_sent, [query_theirs])
    patch_other = from_ahead(patch_sent, count, 1)
    gains = jnp.pad(norm_gains.T, ((0, 4), (0, 0)))

    order = [-1] + list(range(group - 1))
    blocks = forward_blocks(group if tiled else 1, slots, group)
    near_block = next(block for block, near in blocks if near)

    def gather(array):
        pieces = [array if k == 0 else from_ahead(array, count, 2 * k) for k in order]
        return pieces if tiled else [jnp.concatenate(pieces, axis=0)]

    def give_back(arrays):
        if not tiled:
            arrays = [arrays[0][n * slots : (n + 1) * slots] for n in range(group)]
        return [piece if k == 0 else from_ahead(piece, count, -2 * k) for piece, k in zip(arrays, order)]

    x_query, normed_three, q_own, slot_kv, same, turned = query_in_call(
        scalars, segment_ids, slot_valid, query_in, query_theirs, gains, w_qqkv, [patch_sent]
    )
    qs = gather(q_own)
    cot_sent, cot_q_sent = pack_two(scalars, cot, query_cot, [q_own])
    cot_other, cot_theirs = from_ahead(cot_sent, count, 1), from_partner(cot_q_sent, count)
    x, normed_one, qkv, cross, key_bias = patch_in(
        scalars, row_valid, visual, patch_other, gains, w_vqkv, w_xkv, form, [cot_q_sent]
    )
    att = window_forward(qkv, window, [])
    q_out = query_forward(qs, cross, slot_kv, key_bias, same, blocks, [att, cot_theirs])
    out_parts = give_back(q_out)
    (vis_own, vis_other, grad_after, grad_att, g_vout, g_up, g_down, gain_two) = patch_ffn(
        scalars, att, x, cot, cot_other, gains, w_vout, w_up, w_down, tiled, form, [q_out[0]]
    )
    vis_came = from_ahead(vis_other, count, -1)
    (q_res, q_res_other, grad_q, send_q, att_q, normed_four, act_q, dact_q, branch_q, cot_q, gain_four) = query_ffn(
        scalars, out_parts, x_query, query_cot, cot_theirs, gains, w_qout, w_qup, w_qdown, tiled, [gain_two]
    )
    gos = gather(send_q)
    res_came = from_partner(q_res_other, count)
    if tiled:
        out_0, keep_0, out_1, keep_1 = query_sum(
            [g_up, g_down, g_vout], normed_four, cot_q, att_q, branch_q, act_q, dact_q, 0, []
        )
        got = [across(out_0, "y"), across(out_1, "x")]
        last = keep_0
    else:
        g_qout, g_qup, g_qdown = query_weights(normed_four, cot_q, att_q, branch_q, act_q, dact_q, tiled, [])
        last = g_qout
    g_proj = window_backward(qkv, grad_att, window, [last, vis_came])
    last = [g_proj, res_came]
    dqs, dks, dvs, dsks, dsvs = [], [], [], [], []
    for part in range(2):
        dq, dk, dv, dsk, dsv = query_backward(qs, gos, cross, slot_kv, key_bias, turned, near_block, part, last)
        last = [dk] if part == 0 else [dk, *dqs[0]]
        dqs.append(give_back(dq))
        dks.append(dk)
        dvs.append(dv)
        dsks.append(dsk)
        dsvs.append(dsv)
        if tiled:
            out_0, keep_0, out_1, keep_1 = halve_add(scalars, [keep_0, keep_1], got, part + 1, last)
            got = [across(out_0, ORDERS[0][part + 1]), across(out_1, ORDERS[1][part + 1])]
            last = [keep_0]
    back_part, g_vqkv = qkv_back(g_proj, normed_one, w_vqkv, tiled, last)
    vin_own, vin_other, gain_rows, *g_xkv = cross_back(
        scalars, dks, dvs, normed_one, x, grad_after, back_part, gains, w_xkv, gain_two, gain_four, pages, tiled, form, []
    )
    qin_own, qin_other, g_qqkv, gain_grads = query_out(
        scalars, dqs, dsks, dsvs, normed_three, x_query, grad_q, gains, w_qqkv, gain_rows, pages, tiled, got if tiled else []
    )

    def put(array, other):
        return lax.dynamic_update_index_in_dim(array, other.astype(array.dtype), down, 0)

    shape = (pages, strip_rows, columns, width)
    visual_out = put(vis_own, vis_came).reshape(shape)
    vin_came = from_ahead(vin_other, count, -1)
    query_out_rows = put(q_res, res_came)
    qin_came = from_partner(qin_other, count)

    weights = (w_vqkv, w_vout, w_up, w_down, w_qqkv, w_xkv, w_qout, w_qup, w_qdown)
    if tiled:
        size = lambda g: g.shape[-2]
        a, b, c, d, e = g_vqkv, g_xkv[0], gain_grads, g_qqkv, g_xkv[1]
        cut = (size(a) // 2 + 15) // 16 * 16
        lots = [
            (0, 0, [(0, 0, cut)]),
            (1, 0, [(3, 0, cut)]),
            (0, cut, [(0, cut, size(a) - cut)]),
            (1, cut, [(3, cut, size(d) - cut)]),
            (0, size(a), [(1, 0, size(b)), (2, 0, size(c))]),
            (1, size(d), [(4, 0, size(e))]),
        ]
        late_rows = [size(a) + size(b) + size(c), size(d) + size(e)]
        shares = late_sum([a, b, c, d, e], lots, late_rows, [keep_0, got[0], keep_1, got[1]], 1, [])
        tall, flat = g_up.shape[-2], g_vout.shape[-2]
        end = 2 * tall + flat
        where = {2: (0, 0), 7: (0, tall), 1: (0, 2 * tall), 0: (0, end), 5: (0, end + size(a))}
        where.update({3: (1, 0), 8: (1, tall), 6: (1, 2 * tall), 4: (1, end)})
        plan, shapes = [], []
        for number, weight in enumerate(weights):
            rows, cols = weight.shape
            step, tiles = rows // 16, cols // 256
            which, at = where[number]
            spots = [(which, at + t * step) for t in range(tiles)]
            if number == 5:
                spots = spots[:3] + [(1, end + size(d) + t * step) for t in range(3)]
            flipped = rows > 2 * cols and tiles % 2 == 1
            plan.append((step, spots, flipped))
            shapes.append((rows // 8, cols // lax.axis_size("page")))
        last = shares[0]
        gain_part, *parts = finish(scalars[CORE:CORE + 1], shares, shapes, plan, width // 8)
    else:
        last = gain_rows
        parts = [scattered(g) for g in (g_vqkv, g_vout, g_up, g_down, g_qqkv, g_xkv[0], g_qout, g_qup, g_qdown)]
        gain_part = lax.psum_scatter(gain_grads[:4], "page", scatter_dimension=0, tiled=True)
        gain_part = lax.psum_scatter(gain_part, "strip", scatter_dimension=1, tiled=True).reshape(-1, 1)
    visual_in_grad, query_in_grad = put_two(scalars, vin_own, qin_own, vin_came, qin_came, [last])
    visual_in_grad = visual_in_grad.reshape(shape)
    return (visual_out, query_out_rows, visual_in_grad, query_in_grad, gain_part, *parts)


def solution(mesh):
    tokens, slots, table = P("page", "strip", None, None), P("page", "strip", None), P("page", "strip")
    tile = P("strip", "page")
    return jax.shard_map(
        local,
        mesh=mesh,
        in_specs=(tokens, slots, table, P("page", None), table, P("page"), P("page")) + (P(),) * 10 + (tokens, slots),
        out_specs=(tokens, slots, tokens, slots) + (tile,) * 10,
        check_vma=False,
    )
```

profile of v0, /device:TPU:0, one launch (start us, length us, event | category | flops | bytes accessed | tf_op | source)
XLA Modules:
  0.0 478.9 jit_solution(6198816567985368152)
XLA Ops:
  2.0 1.2 dynamic_slice.4
  3.3 1.3 stack.33.refs_0_
  4.5 3.0 pack.1
  7.5 3.0 collective-permute-start
  10.5 5.7 %collective-permute-done.refs_1_.refs_4_ = bf16[144,768]{1,0:T(8,128)(2,1)} collective-permute-done((bf16[144,768]{1,0:T(8,128)(2,1)}, bf16[144,768]{1,0:T(8,128)(2,1)}, u32[]{:S(2)}, u32[]{:S(2)}) %collective-permute-start) | collective-permute-done | bytes 221216 | tf_op jit(solution)/shard_map/ppermute | solution.py:1425
  16.2 4.8 collective-permute-start.1
  21.0 0.6 pad.4.refs_5_.refs_4_.refs_8_.refs_9_.refs_16_
  21.6 5.1 %query_in.1 = (bf16[256,768]{1,0:T(8,128)(2,1)}, bf16[256,768]{1,0:T(8,128)(2,1)}, bf16[256,768]{1,0:T(8,128)(2,1)}, bf16[256,1536]{1,0:T(8,128)(2,1)}, bf16[320...) custom-call(s32[9]{0:T(128)} %stack.33.refs_0_, s32[2,1024]{1,0:T(2,128)} %refs_1_.4, s32[2,128]{1,0:T(2,128)} %refs_2_.5, ...), custom_call_target="tpu_custom_call" | custom-call | flops 2717908992 | bytes 5000000 | tf_op jit(solution)/shard_map/query_in/pallas_call | solution.py:103
  26.7 0.8 collective-permute-start.4
  27.5 1.3 collective-permute-start.3
  28.8 2.9 pack_two.1
  31.7 0.0 collective-permute-start.6
  31.7 10.4 %collective-permute-done.1.refs_3_ = bf16[592,768]{1,0:T(8,128)(2,1)} collective-permute-done((bf16[592,768]{1,0:T(8,128)(2,1)}, bf16[592,768]{1,0:T(8,128)(2,1)}, u32[]{:S(2)}, u32[]{:S(2)}) %collective-permute-start.1) | collective-permute-done | bytes 909344 | tf_op jit(solution)/shard_map/ppermute | solution.py:1421
  42.1 5.2 %collective-permute-start.2 = (bf16[576,768]{1,0:T(8,128)(2,1)}, bf16[576,768]{1,0:T(8,128)(2,1)}, u32[]{:S(2)}, u32[]{:S(2)}) collective-permute-start(bf16[576,768]{1,0:T(8,128)(2,1)} %get-tuple-element.113), channel_id=1, source_target_pairs={{0,7},{1,0},{2,1},{3,2},{4,3},{5,4},{6,5},{7,6},{8,15},{9,8},{10,9... | collective-permute-start | bytes 2654216 | tf_op jit(solution)/shard_map/ppermute | solution.py:1421
  47.3 16.1 %patch_in.1 = (bf16[1152,768]{1,0:T(8,128)(2,1)}, bf16[1152,768]{1,0:T(8,128)(2,1)}, bf16[1152,2304]{1,0:T(8,128)(2,1)}, bf16[1152,1536]{1,0:T(8,128)(2,1)}, bf16[1152,128]{1,0:T(8,128)(2,1)}) custom-call(s32[9]{0:T(128)} %stack.33.refs_0_, s32[2,6]{1,0:T(2,128)} %refs_1_.5, bf16[2,576,768]{2,1,0:T(8,128)(2,1)} %bitcast.39, ...), custom_call_target="tpu_custom_call" | custom-call | flops 20384317440 | bytes 20000000 | tf_op jit(solution)/shard_map/patch_in/pallas_call | solution.py:103
  63.4 15.7 %window_forward.1.refs_10_.refs_1_ = bf16[1152,768]{1,0:T(8,128)(2,1)} custom-call(bf16[1152,2304]{1,0:T(8,128)(2,1)} %get-tuple-element.111.refs_0_), custom_call_target="tpu_custom_call" | custom-call | flops 6115295232 | bytes 8000000 | tf_op jit(solution)/shard_map/window_forward/pallas_call | solution.py:103
  79.2 0.0 collective-permute-done.4.refs_2_
  79.2 0.0 collective-permute-done.3.refs_0_
  79.2 28.2 %query_forward.1 = (bf16[256,896]{1,0:T(8,128)(2,1)}, bf16[256,896]{1,0:T(8,128)(2,1)}, bf16[256,896]{1,0:T(8,128)(2,1)}, bf16[256,896]{1,0:T(8,128)(2,1)}) custom-call(bf16[256,768]{1,0:T(8,128)(2,1)} %collective-permute-done.3.refs_0_, bf16[256,768]{1,0:T(8,128)(2,1)} %get-tuple-element.109.refs_3_.refs_1_, ...), custom_call_target="tpu_custom_call" | custom-call | flops 43486543872 | bytes 10000000 | tf_op jit(solution)/shard_map/query_forward/pallas_call | solution.py:103
  107.4 14.9 %collective-permute-start.9 = (bf16[256,896]{1,0:T(8,128)(2,1)}, bf16[256,896]{1,0:T(8,128)(2,1)}, u32[]{:S(2)}, u32[]{:S(2)}) collective-permute-start(bf16[256,896]{1,0:T(8,128)(2,1)} %get-tuple-element.122), channel_id=1, source_target_pairs={{0,2},{1,3},{2,4},{3,5},{4,6},{5,7},{6,0},{7,1},{8,10},{9,11},{10,... | collective-permute-start | bytes 1376264 | tf_op jit(solution)/shard_map/ppermute | solution.py:1421
  122.3 2.0 collective-permute-start.10
  124.3 2.8 collective-permute-start.8
  127.2 0.0 collective-permute-done.2.refs_4_
  127.2 70.6 %patch_ffn.1 = (bf16[2,576,768]{2,1,0:T(8,128)(2,1)}, bf16[576,768]{1,0:T(8,128)(2,1)}, f32[1152,768]{1,0:T(8,128)}, bf16[1152,768]{1,0:T(8,128)(2,1)}, bf16[2,2...) custom-call(s32[9]{0:T(128)} %stack.33.refs_0_, ...), custom_call_target="tpu_custom_call" | custom-call | flops 97844723712 | bytes 40000000 | tf_op jit(solution)/shard_map/patch_ffn/pallas_call | solution.py:103
  197.8 0.1 collective-permute-start.7
  197.9 0.0 collective-permute-done.10.refs_4_
  197.9 17.0 %query_ffn.1 = (bf16[2,128,768]{2,1,0:T(8,128)(2,1)}, bf16[128,768]{1,0:T(8,128)(2,1)}, f32[256,768]{1,0:T(8,128)}, bf16[256,896]{1,0:T(8,128)(2,1)}, bf16[256,7...) custom-call(s32[9]{0:T(128)} %stack.33.refs_0_, ...), custom_call_target="tpu_custom_call" | custom-call | flops 14495514624 | bytes 20000000 | tf_op jit(solution)/shard_map/query_ffn/pallas_call | solution.py:103
  214.9 0.7 collective-permute-start.11
  215.5 1.4 collective-permute-start.14
  216.9 3.3 collective-permute-start.13
  220.2 0.6 collective-permute-start.12
  220.8 23.1 %query_sum.1 = (bf16[2,4,1296,128]{3,2,1,0:T(8,128)(2,1)}, bf16[2,4,1296,128]{3,2,1,0:T(8,128)(2,1)}, bf16[2,4,1296,128]{3,2,1,0:T(8,128)(2,1)}, bf16[2,4,1296,128]{3,2,1,0:T(8,128)(2,1)}) custom-call(bf16[2,2,2,4,576,128]{5,4,3,2,1,0:T(8,128)(2,1)} %get-tuple-element.131.refs_0_, bf16[2,2,2,4,576,128]{5,4,3,2,1,0:T(8,128)(2,1)} %get-tuple-element.132.refs_1_, ...), custom_call_target="tpu_custom_call" | custom-call | tf_op jit(solution)/shard_map/query_sum/pallas_call | solution.py:1200
  243.8 0.0 collective-permute-done.11.refs_19_
  243.9 0.2 collective-permute-start.15
  244.0 0.0 collective-permute-done.7.refs_3_
  244.0 1.5 collective-permute-start.16
  245.5 24.5 %window_backward.1.refs_18_.refs_0_ = bf16[1152,2304]{1,0:T(8,128)(2,1)} custom-call(bf16[1152,2304]{1,0:T(8,128)(2,1)} %get-tuple-element.111.refs_0_, bf16[1152,768]{1,0:T(8,128)(2,1)} %get-tuple-element.130.refs_1_, bf16[8,1296,128]{2,1,0:T(8,128)(2,1)} %bitcast.30, bf16[576,768]{1,0:T(8,128)(2,1)} %collective-permute-done.7.refs_3_), custom_call_target="tpu_custom_call" | custom-call | flops 15288238080 | bytes 13000000 | tf_op jit(solution)/shard_map/window_backward/pallas_call | solution.py:103
  270.0 0.0 collective-permute-done.14.refs_7_.refs_11_
  270.0 0.0 collective-permute-done.13.refs_6_.refs_10_
  270.1 27.0 %query_backward.2 = (bf16[256,384]{1,0:T(8,128)(2,1)}, bf16[256,384]{1,0:T(8,128)(2,1)}, bf16[256,384]{1,0:T(8,128)(2,1)}, bf16[256,384]{1,0:T(8,128)(2,1)}, bf1...) custom-call(bf16[256,768]{1,0:T(8,128)(2,1)} %collective-permute-done.3, ...), custom_call_target="tpu_custom_call" | custom-call | flops 27179089920 | bytes 15000000 | tf_op jit(solution)/shard_map/query_backward/pallas_call | solution.py:103
  297.0 3.4 collective-permute-start.19
  300.4 0.4 collective-permute-start.20
  300.8 0.6 collective-permute-start.21
  301.5 2.4 collective-permute-done.15.refs_2_.refs_4_
  303.8 0.1 collective-permute-done.16.refs_6_.refs_8_
  303.9 7.5 %halve_add.2 = (bf16[4,1296,128]{2,1,0:T(8,128)(2,1)}, bf16[4,1296,128]{2,1,0:T(8,128)(2,1)}, bf16[4,1296,128]{2,1,0:T(8,128)(2,1)}, bf16[4,1296,128]{2,1,0:T(8,128)(2,1)}) custom-call(s32[9]{0:T(128)} %stack.33.refs_0_, bf16[8,1296,128]{2,1,0:T(8,128)(2,1)} %bitcast.31, bf16[8,1296,128]{2,1,0:T(8,128)(2,1)} %collective-permute-done.15.refs_2_.refs_4_, ...), custom_call_target="tpu_custom_call" | custom-call | flops 3000000 | bytes 15925248 | tf_op jit(solution)/shard_map/halve_add/pallas_call | solution.py:103
  311.4 1.5 collective-permute-start.17
  312.9 1.7 collective-permute-start.18
  314.6 26.9 %query_backward.3 = (bf16[256,384]{1,0:T(8,128)(2,1)}, bf16[256,384]{1,0:T(8,128)(2,1)}, bf16[256,384]{1,0:T(8,128)(2,1)}, bf16[256,384]{1,0:T(8,128)(2,1)}, bf1...) custom-call(bf16[256,768]{1,0:T(8,128)(2,1)} %collective-permute-done.3, ...), custom_call_target="tpu_custom_call" | custom-call | flops 27179089920 | bytes 15000000 | tf_op jit(solution)/shard_map/query_backward/pallas_call | solution.py:103
  341.5 3.3 collective-permute-start.22
  344.8 0.6 collective-permute-start.24
  345.5 4.5 halve_add.3
  349.9 3.8 collective-permute-start.25
  353.7 0.1 collective-permute-start.26
  353.8 17.6 %qkv_back.1 = (f32[1152,768]{1,0:T(8,128)}, bf16[2,2,2,4,432,128]{5,4,3,2,1,0:T(8,128)(2,1)}) custom-call(bf16[1152,2304]{1,0:T(8,128)(2,1)} %window_backward.1.refs_18_.refs_0_, bf16[1152,768]{1,0:T(8,128)(2,1)} %get-tuple-element.149.refs_1_.refs_5_, bf16[768,2304]{1,0:T(8,128)(2,1)} %refs_2_.7, bf16[2,1296,128]{2,1,0:T(8,128)(2,1)} %get-tuple-element.158.refs_3_.refs_5_), custom_call_target="tpu_custom_call" | custom-call | flops 24461180928 | bytes 20000000 | tf_op jit(solution)/shard_map/qkv_back/pallas_call | solution.py:103
  371.4 18.2 %cross_back.1 = (f32[2,576,768]{2,1,0:T(8,128)}, bf16[576,768]{1,0:T(8,128)(2,1)}, f32[8,768]{1,0:T(8,128)}, bf16[2,2,2,4,144,128]{5,4,3,2,1,0:T(8,128)(2,1)}, bf16[2,2,2,4,144,128]{5,4,3,2,1,0:T(8,128)(2,1)}) custom-call(s32[9]{0:T(128)} %stack.33.refs_0_, bf16[1152,384]{1,0:T(8,128)(2,1)} %get-tuple-element.141.refs_9_.refs_1_, ...), custom_call_target="tpu_custom_call" | custom-call | flops 16307453952 | bytes 20000000 | tf_op jit(solution)/shard_map/cross_back/pallas_call | solution.py:103
  389.6 0.4 collective-permute-start.27
  390.1 1.6 bitcast_dynamic-update-slice_fusion.1
  391.7 8.6 %query_out.1 = (f32[2,128,768]{2,1,0:T(8,128)}, bf16[128,768]{1,0:T(8,128)(2,1)}, bf16[2,2,2,4,432,128]{5,4,3,2,1,0:T(8,128)(2,1)}, bf16[2,2,2,4,48,128]{5,4,3,2,1,0:T(8,128)(2,1)}) custom-call(s32[9]{0:T(128)} %stack.33.refs_0_, bf16[256,384]{1,0:T(8,128)(2,1)} %collective-permute-done.19.refs_10_.refs_1_, ...), custom_call_target="tpu_custom_call" | custom-call | flops 5435817984 | bytes 10000000 | tf_op jit(solution)/shard_map/query_out/pallas_call | solution.py:103
  400.3 3.0 collective-permute-start.28
  403.3 2.1 bitcast_dynamic-update-slice_fusion
  405.4 66.3 %late_sum.1 = (bf16[1920,128]{1,0:T(8,128)(2,1)}, bf16[1872,128]{1,0:T(8,128)(2,1)}, bf16[1920,128]{1,0:T(8,128)(2,1)}, bf16[1872,128]{1,0:T(8,128)(2,1)}) custom-call(bf16[2,16,432,128]{3,2,1,0:T(8,128)(2,1)} %bitcast.35, bf16[2,16,144,128]{3,2,1,0:T(8,128)(2,1)} %bitcast.42, bf16[2,16,48,128]{3,2,1,0:T(8,128)(2,1)} %bitcast.44, ...), custom_call_target="tpu_custom_call" | custom-call | tf_op jit(solution)/shard_map/late_sum/pallas_call | solution.py:1342
  471.8 3.6 finish.1
  475.4 3.3 put_two.1
  (22 shorter events, 0.1 us)
Async XLA Ops:
  0.6 20.4 %copy-start = (f32[768,4]{0,1:T(4,128)S(1)}, f32[768,4]{0,1:T(4,128)}, u32[]{:S(2)}) copy-start(f32[768,4]{0,1:T(4,128)} %param.26) | copy-start | bytes 36868
  7.5 8.7 %collective-permute-start = (bf16[144,768]{1,0:T(8,128)(2,1)}, bf16[144,768]{1,0:T(8,128)(2,1)}, u32[]{:S(2)}, u32[]{:S(2)}) collective-permute-start(bf16[144,768]{1,0:T(8,128)(2,1)} %get-tuple-element.108), channel_id=1, source_target_pairs={{0,1},{1,0},{2,3},{3,2},{4,5},{5,4},{6,7},{7,6},{8,9},{9,8},{10,11... | collective-permute-start | bytes 663560 | tf_op jit(solution)/shard_map/ppermute | solution.py:1425
  16.2 25.9 %collective-permute-start.1 = (bf16[592,768]{1,0:T(8,128)(2,1)}, bf16[592,768]{1,0:T(8,128)(2,1)}, u32[]{:S(2)}, u32[]{:S(2)}) collective-permute-start(bf16[592,768]{1,0:T(8,128)(2,1)} %held_back.1.refs_7_), channel_id=1, source_target_pairs={{0,7},{1,0},{2,1},{3,2},{4,3},{5,4},{6,5},{7,6},{8,15},{9,8},{10,9... | collective-permute-start | bytes 2727944 | tf_op jit(solution)/shard_map/ppermute | solution.py:1421
  26.7 52.5 %collective-permute-start.5 = (bf16[256,768]{1,0:T(8,128)(2,1)}, bf16[256,768]{1,0:T(8,128)(2,1)}, u32[]{:S(2)}, u32[]{:S(2)}) collective-permute-start(bf16[256,768]{1,0:T(8,128)(2,1)} %get-tuple-element.109.refs_3_.refs_1_), channel_id=1, source_target_pairs={{0,4},{1,5},{2,6},{3,7},{4,0},{5,1},{6,2},{7,3},{8,12},{9,13},{10,... | collective-permute-start | bytes 1179656 | tf_op jit(solution)/shard_map/ppermute | solution.py:1421
  26.7 52.5 %collective-permute-start.4 = (bf16[256,768]{1,0:T(8,128)(2,1)}, bf16[256,768]{1,0:T(8,128)(2,1)}, u32[]{:S(2)}, u32[]{:S(2)}) collective-permute-start(bf16[256,768]{1,0:T(8,128)(2,1)} %get-tuple-element.109.refs_3_.refs_1_), channel_id=1, source_target_pairs={{0,6},{1,7},{2,0},{3,1},{4,2},{5,3},{6,4},{7,5},{8,14},{9,15},{10,... | collective-permute-start | bytes 1179656 | tf_op jit(solution)/shard_map/ppermute | solution.py:1421
  27.5 51.7 %collective-permute-start.3 = (bf16[256,768]{1,0:T(8,128)(2,1)}, bf16[256,768]{1,0:T(8,128)(2,1)}, u32[]{:S(2)}, u32[]{:S(2)}) collective-permute-start(bf16[256,768]{1,0:T(8,128)(2,1)} %get-tuple-element.109.refs_3_.refs_1_), channel_id=1, source_target_pairs={{0,2},{1,3},{2,4},{3,5},{4,6},{5,7},{6,0},{7,1},{8,10},{9,11},{10,... | collective-permute-start | bytes 1179656 | tf_op jit(solution)/shard_map/ppermute | solution.py:1421
  31.7 47.5 %collective-permute-start.6 = (bf16[128,768]{1,0:T(8,128)(2,1)}, bf16[128,768]{1,0:T(8,128)(2,1)}, u32[]{:S(2)}, u32[]{:S(2)}) collective-permute-start(bf16[128,768]{1,0:T(8,128)(2,1)} %get-tuple-element.110.refs_7_), channel_id=1, source_target_pairs={{0,1},{1,0},{2,3},{3,2},{4,5},{5,4},{6,7},{7,6},{8,9},{9,8},{10,11... | collective-permute-start | bytes 589832 | tf_op jit(solution)/shard_map/ppermute | solution.py:1425
  42.1 85.1 %collective-permute-start.2 = (bf16[576,768]{1,0:T(8,128)(2,1)}, bf16[576,768]{1,0:T(8,128)(2,1)}, u32[]{:S(2)}, u32[]{:S(2)}) collective-permute-start(bf16[576,768]{1,0:T(8,128)(2,1)} %get-tuple-element.113), channel_id=1, source_target_pairs={{0,7},{1,0},{2,1},{3,2},{4,3},{5,4},{6,5},{7,6},{8,15},{9,8},{10,9... | collective-permute-start | bytes 2654216 | tf_op jit(solution)/shard_map/ppermute | solution.py:1421
  107.4 90.4 %collective-permute-start.9 = (bf16[256,896]{1,0:T(8,128)(2,1)}, bf16[256,896]{1,0:T(8,128)(2,1)}, u32[]{:S(2)}, u32[]{:S(2)}) collective-permute-start(bf16[256,896]{1,0:T(8,128)(2,1)} %get-tuple-element.122), channel_id=1, source_target_pairs={{0,2},{1,3},{2,4},{3,5},{4,6},{5,7},{6,0},{7,1},{8,10},{9,11},{10,... | collective-permute-start | bytes 1376264 | tf_op jit(solution)/shard_map/ppermute | solution.py:1421
  122.3 75.5 %collective-permute-start.10 = (bf16[256,896]{1,0:T(8,128)(2,1)}, bf16[256,896]{1,0:T(8,128)(2,1)}, u32[]{:S(2)}, u32[]{:S(2)}) collective-permute-start(bf16[256,896]{1,0:T(8,128)(2,1)} %get-tuple-element.123), channel_id=1, source_target_pairs={{0,4},{1,5},{2,6},{3,7},{4,0},{5,1},{6,2},{7,3},{8,12},{9,13},{10,... | collective-permute-start | bytes 1376264 | tf_op jit(solution)/shard_map/ppermute | solution.py:1421
  124.3 73.5 %collective-permute-start.8 = (bf16[256,896]{1,0:T(8,128)(2,1)}, bf16[256,896]{1,0:T(8,128)(2,1)}, u32[]{:S(2)}, u32[]{:S(2)}) collective-permute-start(bf16[256,896]{1,0:T(8,128)(2,1)} %get-tuple-element.118.refs_9_), channel_id=1, source_target_pairs={{0,6},{1,7},{2,0},{3,1},{4,2},{5,3},{6,4},{7,5},{8,14},{9,15},{10,... | collective-permute-start | bytes 1376264 | tf_op jit(solution)/shard_map/ppermute | solution.py:1421
  197.8 46.2 %collective-permute-start.7 = (bf16[576,768]{1,0:T(8,128)(2,1)}, bf16[576,768]{1,0:T(8,128)(2,1)}, u32[]{:S(2)}, u32[]{:S(2)}) collective-permute-start(bf16[576,768]{1,0:T(8,128)(2,1)} %get-tuple-element.120), channel_id=1, source_target_pairs={{0,1},{1,2},{2,3},{3,4},{4,5},{5,6},{6,7},{7,0},{8,9},{9,10},{10,1... | collective-permute-start | bytes 2654216 | tf_op jit(solution)/shard_map/ppermute | solution.py:1421
  214.9 29.0 %collective-permute-start.11 = (bf16[128,768]{1,0:T(8,128)(2,1)}, bf16[128,768]{1,0:T(8,128)(2,1)}, u32[]{:S(2)}, u32[]{:S(2)}) collective-permute-start(bf16[128,768]{1,0:T(8,128)(2,1)} %get-tuple-element.127), channel_id=1, source_target_pairs={{0,1},{1,0},{2,3},{3,2},{4,5},{5,4},{6,7},{7,6},{8,9},{9,8},{10,11... | collective-permute-start | bytes 589832 | tf_op jit(solution)/shard_map/ppermute | solution.py:1425
  215.5 54.5 %collective-permute-start.14 = (bf16[256,896]{1,0:T(8,128)(2,1)}, bf16[256,896]{1,0:T(8,128)(2,1)}, u32[]{:S(2)}, u32[]{:S(2)}) collective-permute-start(bf16[256,896]{1,0:T(8,128)(2,1)} %get-tuple-element.128.refs_5_.refs_9_), channel_id=1, source_target_pairs={{0,4},{1,5},{2,6},{3,7},{4,0},{5,1},{6,2},{7,3},{8,12},{9,13},{10,... | collective-permute-start | bytes 1376264 | tf_op jit(solution)/shard_map/ppermute | solution.py:1421
  216.9 53.1 %collective-permute-start.13 = (bf16[256,896]{1,0:T(8,128)(2,1)}, bf16[256,896]{1,0:T(8,128)(2,1)}, u32[]{:S(2)}, u32[]{:S(2)}) collective-permute-start(bf16[256,896]{1,0:T(8,128)(2,1)} %get-tuple-element.128.refs_5_.refs_9_), channel_id=1, source_target_pairs={{0,6},{1,7},{2,0},{3,1},{4,2},{5,3},{6,4},{7,5},{8,14},{9,15},{10,... | collective-permute-start | bytes 1376264 | tf_op jit(solution)/shard_map/ppermute | solution.py:1421
  220.2 49.9 %collective-permute-start.12 = (bf16[256,896]{1,0:T(8,128)(2,1)}, bf16[256,896]{1,0:T(8,128)(2,1)}, u32[]{:S(2)}, u32[]{:S(2)}) collective-permute-start(bf16[256,896]{1,0:T(8,128)(2,1)} %get-tuple-element.128.refs_5_.refs_9_), channel_id=1, source_target_pairs={{0,2},{1,3},{2,4},{3,5},{4,6},{5,7},{6,0},{7,1},{8,10},{9,11},{10,... | collective-permute-start | bytes 1376264 | tf_op jit(solution)/shard_map/ppermute | solution.py:1421
  243.9 60.0 %collective-permute-start.15 = (bf16[8,1296,128]{2,1,0:T(8,128)(2,1)}, bf16[8,1296,128]{2,1,0:T(8,128)(2,1)}, u32[]{:S(2)}, u32[]{:S(2)}) collective-permute-start(bf16[8,1296,128]{2,1,0:T(8,128)(2,1)} %bitcast.49), channel_id=1, source_target_pairs={{0,1},{1,0},{2,3},{3,2},{4,5},{5,4},{6,7},{7,6},{8,9},{9,8},{10,11... | collective-permute-start | bytes 7962632 | tf_op jit(solution)/shard_map/ppermute | solution.py:1224
  244.0 59.9 %collective-permute-start.16 = (bf16[8,1296,128]{2,1,0:T(8,128)(2,1)}, bf16[8,1296,128]{2,1,0:T(8,128)(2,1)}, u32[]{:S(2)}, u32[]{:S(2)}) collective-permute-start(bf16[8,1296,128]{2,1,0:T(8,128)(2,1)} %bitcast.48), channel_id=1, source_target_pairs={{0,16},{8,24},{16,0},{24,8},{1,17},{9,25},{17,1},{25,9},{2,18},{10... | collective-permute-start | bytes 7962632 | tf_op jit(solution)/shard_map/ppermute | solution.py:1224
  297.0 44.4 %collective-permute-start.19 = (bf16[256,384]{1,0:T(8,128)(2,1)}, bf16[256,384]{1,0:T(8,128)(2,1)}, u32[]{:S(2)}, u32[]{:S(2)}) collective-permute-start(bf16[256,384]{1,0:T(8,128)(2,1)} %get-tuple-element.154), channel_id=1, source_target_pairs={{0,6},{1,7},{2,0},{3,1},{4,2},{5,3},{6,4},{7,5},{8,14},{9,15},{10,... | collective-permute-start | bytes 589832 | tf_op jit(solution)/shard_map/ppermute | solution.py:1421
  300.4 44.4 %collective-permute-start.20 = (bf16[256,384]{1,0:T(8,128)(2,1)}, bf16[256,384]{1,0:T(8,128)(2,1)}, u32[]{:S(2)}, u32[]{:S(2)}) collective-permute-start(bf16[256,384]{1,0:T(8,128)(2,1)} %get-tuple-element.156), channel_id=1, source_target_pairs={{0,2},{1,3},{2,4},{3,5},{4,6},{5,7},{6,0},{7,1},{8,10},{9,11},{10,... | collective-permute-start | bytes 589832 | tf_op jit(solution)/shard_map/ppermute | solution.py:1421
  300.8 44.0 %collective-permute-start.21 = (bf16[256,384]{1,0:T(8,128)(2,1)}, bf16[256,384]{1,0:T(8,128)(2,1)}, u32[]{:S(2)}, u32[]{:S(2)}) collective-permute-start(bf16[256,384]{1,0:T(8,128)(2,1)} %get-tuple-element.157), channel_id=1, source_target_pairs={{0,4},{1,5},{2,6},{3,7},{4,0},{5,1},{6,2},{7,3},{8,12},{9,13},{10,... | collective-permute-start | bytes 589832 | tf_op jit(solution)/shard_map/ppermute | solution.py:1421
  311.4 34.1 %collective-permute-start.17 = (bf16[4,1296,128]{2,1,0:T(8,128)(2,1)}, bf16[4,1296,128]{2,1,0:T(8,128)(2,1)}, u32[]{:S(2)}, u32[]{:S(2)}) collective-permute-start(bf16[4,1296,128]{2,1,0:T(8,128)(2,1)} %get-tuple-element.151), channel_id=1, source_target_pairs={{0,16},{8,24},{16,0},{24,8},{1,17},{9,25},{17,1},{25,9},{2,18},{10... | collective-permute-start | bytes 3981320 | tf_op jit(solution)/shard_map/ppermute | solution.py:1224
  312.9 32.5 %collective-permute-start.18 = (bf16[4,1296,128]{2,1,0:T(8,128)(2,1)}, bf16[4,1296,128]{2,1,0:T(8,128)(2,1)}, u32[]{:S(2)}, u32[]{:S(2)}) collective-permute-start(bf16[4,1296,128]{2,1,0:T(8,128)(2,1)} %get-tuple-element.153), channel_id=1, source_target_pairs={{0,1},{1,0},{2,3},{3,2},{4,5},{5,4},{6,7},{7,6},{8,9},{9,8},{10,11... | collective-permute-start | bytes 3981320 | tf_op jit(solution)/shard_map/ppermute | solution.py:1224
  341.5 48.1 %collective-permute-start.22 = (bf16[256,384]{1,0:T(8,128)(2,1)}, bf16[256,384]{1,0:T(8,128)(2,1)}, u32[]{:S(2)}, u32[]{:S(2)}) collective-permute-start(bf16[256,384]{1,0:T(8,128)(2,1)} %get-tuple-element.162), channel_id=1, source_target_pairs={{0,6},{1,7},{2,0},{3,1},{4,2},{5,3},{6,4},{7,5},{8,14},{9,15},{10,... | collective-permute-start | bytes 589832 | tf_op jit(solution)/shard_map/ppermute | solution.py:1421
  344.8 46.9 %collective-permute-start.23 = (bf16[256,384]{1,0:T(8,128)(2,1)}, bf16[256,384]{1,0:T(8,128)(2,1)}, u32[]{:S(2)}, u32[]{:S(2)}) collective-permute-start(bf16[256,384]{1,0:T(8,128)(2,1)} %get-tuple-element.164), channel_id=1, source_target_pairs={{0,2},{1,3},{2,4},{3,5},{4,6},{5,7},{6,0},{7,1},{8,10},{9,11},{10,... | collective-permute-start | bytes 589832 | tf_op jit(solution)/shard_map/ppermute | solution.py:1421
  344.8 46.9 %collective-permute-start.24 = (bf16[256,384]{1,0:T(8,128)(2,1)}, bf16[256,384]{1,0:T(8,128)(2,1)}, u32[]{:S(2)}, u32[]{:S(2)}) collective-permute-start(bf16[256,384]{1,0:T(8,128)(2,1)} %get-tuple-element.165), channel_id=1, source_target_pairs={{0,4},{1,5},{2,6},{3,7},{4,0},{5,1},{6,2},{7,3},{8,12},{9,13},{10,... | collective-permute-start | bytes 589832 | tf_op jit(solution)/shard_map/ppermute | solution.py:1421
  349.9 41.7 %collective-permute-start.25 = (bf16[2,1296,128]{2,1,0:T(8,128)(2,1)}, bf16[2,1296,128]{2,1,0:T(8,128)(2,1)}, u32[]{:S(2)}, u32[]{:S(2)}) collective-permute-start(bf16[2,1296,128]{2,1,0:T(8,128)(2,1)} %get-tuple-element.173), channel_id=1, source_target_pairs={{0,2},{1,3},{2,0},{3,1},{4,6},{5,7},{6,4},{7,5},{8,10},{9,11},{10,... | collective-permute-start | bytes 1990664 | tf_op jit(solution)/shard_map/ppermute | solution.py:1224
  353.7 37.9 %collective-permute-start.26 = (bf16[2,1296,128]{2,1,0:T(8,128)(2,1)}, bf16[2,1296,128]{2,1,0:T(8,128)(2,1)}, u32[]{:S(2)}, u32[]{:S(2)}) collective-permute-start(bf16[2,1296,128]{2,1,0:T(8,128)(2,1)} %get-tuple-element.174), channel_id=1, source_target_pairs={{0,2},{1,3},{2,0},{3,1},{4,6},{5,7},{6,4},{7,5},{8,10},{9,11},{10,... | collective-permute-start | bytes 1990664 | tf_op jit(solution)/shard_map/ppermute | solution.py:1224
  389.6 85.7 %collective-permute-start.27 = (bf16[576,768]{1,0:T(8,128)(2,1)}, bf16[576,768]{1,0:T(8,128)(2,1)}, u32[]{:S(2)}, u32[]{:S(2)}) collective-permute-start(bf16[576,768]{1,0:T(8,128)(2,1)} %get-tuple-element.176), channel_id=1, source_target_pairs={{0,1},{1,2},{2,3},{3,4},{4,5},{5,6},{6,7},{7,0},{8,9},{9,10},{10,1... | collective-permute-start | bytes 2654216 | tf_op jit(solution)/shard_map/ppermute | solution.py:1421
  400.3 75.1 %collective-permute-start.28 = (bf16[128,768]{1,0:T(8,128)(2,1)}, bf16[128,768]{1,0:T(8,128)(2,1)}, u32[]{:S(2)}, u32[]{:S(2)}) collective-permute-start(bf16[128,768]{1,0:T(8,128)(2,1)} %get-tuple-element.177), channel_id=1, source_target_pairs={{0,1},{1,0},{2,3},{3,2},{4,5},{5,4},{6,7},{7,6},{8,9},{9,8},{10,11... | collective-permute-start | bytes 589832 | tf_op jit(solution)/shard_map/ppermute | solution.py:1425
where the time goes:
time: 488 us; the launch traced here: 479 us
  Pallas kernels  390 us (80%)
  starting transfers between devices  61.3 us (13%)
  waiting for transfers between devices  18.7 us (4%)
  local copies, waits for them, and re-layouts  6.89 us (1%)
    pallas_call x18, Pallas kernels, call(): pl.pallas_call(body, grid_spec=pltpu.PrefetchScalarGridSpec(num_scalar_pr...  297 us
    pallas_call x1, Pallas kernels, late_sum(): pl.pallas_call(lambda *refs: kernel(*refs[:first], *refs[first + len(deps...  66.3 us
    ppermute x19, starting transfers between devices, from_ahead(): lax.ppermute(array, 'strip', [(i, (i - distance) % count) for i in range(...  45.9 us
    pallas_call x1, Pallas kernels, query_sum(): pl.pallas_call(lambda *refs: kernel(*refs[:9], *refs[9 + len(deps):]), in...  23.1 us
    ppermute x19, waiting for transfers between devices, from_ahead(): lax.ppermute(array, 'strip', [(i, (i - distance) % count) for i in range(...  10.4 us
  transfers between devices with their start and end apart: 29, of which 4 were waited for; matrix products, arithmetic and copies ran while one was open for 1% of the time, Pallas kernels for 80%

commit v1 on v0

--- a/solution.py
+++ b/solution.py
@@ -539,43 +539,9 @@
     )
 
 
-def qkv_back_kernel(gp_ref, n_ref, w_ref, back_ref, w_grad_ref, *, tiled):
-    first = dot(gp_ref[...], w_ref[...], 1, 1)
-
-    @pl.when(pl.program_id(0) == 0)
-    def _():
-        back_ref[...] = first
-
-    @pl.when(pl.program_id(0) > 0)
-    def _():
-        back_ref[...] += first
-
-    put_grad(w_grad_ref, dot(n_ref[...], gp_ref[...], 0, 0).astype(BF), store_columns, 0, tiled)
-
-
-def qkv_back(gp, normed, w, tiled, deps):
-    tokens, width = normed.shape
-    cols = w.shape[1]
-    chunk = cols // 2
-    natural = pl.BlockSpec((width, chunk), lambda j: (0, j))
-    if tiled:
-        form = (tile_shape(width, cols), BF, columns_spec(width, chunk, 1, 0, lambda j: j))
-    else:
-        form = (w.shape, BF, natural)
-    return call(
-        functools.partial(qkv_back_kernel, tiled=tiled),
-        "qkv_back",
-        [(gp, pl.BlockSpec((tokens, chunk), lambda j: (0, j))), (normed, whole(normed.shape, True)), (w, natural)],
-        [((tokens, width), F32, whole((tokens, width))), form],
-        grid=(2,),
-        deps=deps,
-        work=(4 * tokens * width * cols, 2e7, 0),
-    )
-
-
-def cross_back_kernel(
-    s_ref, gk0_ref, gk1_ref, gv0_ref, gv1_ref, n_ref, x_ref, after_ref, part_ref, gain_ref, wx_ref, g2_ref, g4_ref,
-    own_ref, other_ref, gain_grad_ref, *rest,
+def patch_back_kernel(
+    s_ref, gp_ref, wq_ref, gk0_ref, gk1_ref, gv0_ref, gv1_ref, n_ref, x_ref, after_ref, gain_ref, wx_ref, g2_ref, g4_ref,
+    own_ref, other_ref, gain_grad_ref, wq_grad_ref, *rest,
     tiled, form,
 ):
     step = pl.program_id(0)
@@ -585,8 +551,13 @@
     block = 4 * part
     back = rest[-1]
 
-    def one(grad, base):
-        back[...] = base[...] + dot(grad, wx_ref[...], 1, 1)
+    def query_part(first):
+        term = dot(gp_ref[...], wq_ref[...], 1, 1)
+        back[...] = term if first else back[...] + term
+        put_grad(wq_grad_ref, dot(n_ref[...], gp_ref[...], 0, 0).astype(BF), store_columns, 0, tiled)
+
+    def cross_part(grad):
+        back[...] += dot(grad, wx_ref[...], 1, 1)
         w_grad = dot(n_ref[...], grad, 0, 0).astype(BF)
         if not tiled:
             rest[0][...] = w_grad
@@ -596,11 +567,19 @@
 
     @pl.when(step == 0)
     def _():
-        one(jnp.concatenate([gk0_ref[...], gk1_ref[...]], axis=1), part_ref)
+        query_part(True)
 
     @pl.when(step == 1)
     def _():
-        one(jnp.concatenate([gv0_ref[...], gv1_ref[...]], axis=1), back)
+        query_part(False)
+
+    @pl.when(step == 2)
+    def _():
+        cross_part(jnp.concatenate([gk0_ref[...], gk1_ref[...]], axis=1))
+
+    @pl.when(step == 3)
+    def _():
+        cross_part(jnp.concatenate([gv0_ref[...], gv1_ref[...]], axis=1))
         gain_sum = jnp.zeros((1, width), F32)
         for b in range(tokens // block):
             rows = slice(b * block, (b + 1) * block)
@@ -618,33 +597,45 @@
         other_ref[...] = dot(onehot, halves[1].astype(BF)).astype(BF)
 
 
-def cross_back(scalars, gks, gvs, normed, x, after, part, gains, wx, g2, g4, pages, tiled, form, deps):
+def patch_back(scalars, gp, wq, gks, gvs, normed, x, after, gains, wx, g2, g4, pages, tiled, form, deps):
     tokens, width = x.shape
     half = tokens // 2
     cols = wx.shape[1]
+    chunk = wq.shape[1] // 2
+    at_q, at_x = (lambda j: jnp.minimum(j, 1)), (lambda j: jnp.maximum(j - 2, 0))
     if tiled:
         shape = tile_shape(width, cols // 2)
-        grads = [(shape, BF, columns_spec(width, width // 2, 1, order, lambda j: j)) for order in (0, 1)]
+        grads = [(tile_shape(width, wq.shape[1]), BF, columns_spec(width, chunk, 1, 0, at_q))]
+        grads += [(shape, BF, columns_spec(width, width // 2, 1, order, at_x)) for order in (0, 1)]
     else:
-        grads = [(wx.shape, BF, pl.BlockSpec((width, width), lambda j, *_: (0, j)))]
+        grads = [
+            (wq.shape, BF, pl.BlockSpec((width, chunk), lambda j, *_: (0, at_q(j)))),
+            (wx.shape, BF, pl.BlockSpec((width, width), lambda j, *_: (0, at_x(j)))),
+        ]
     single = lambda a: (a, whole(a.shape, True))
     own_shape = (pages, half, width)
     return call(
-        functools.partial(cross_back_kernel, tiled=tiled, form=form),
-        "cross_back",
-        [single(a) for a in (*gks, *gvs, normed, x, after, part, gains)]
-        + [(wx, pl.BlockSpec((width, width), lambda j, *_: (0, j))), single(g2), single(g4)],
+        functools.partial(patch_back_kernel, tiled=tiled, form=form),
+        "patch_back",
+        [
+            (gp, pl.BlockSpec((tokens, chunk), lambda j, *_: (0, at_q(j)))),
+            (wq, pl.BlockSpec((width, chunk), lambda j, *_: (0, at_q(j)))),
+            *[single(a) for a in (*gks, *gvs, normed, x, after, gains)],
+            (wx, pl.BlockSpec((width, width), lambda j, *_: (0, at_x(j)))),
+            single(g2),
+            single(g4),
+        ],
         [
             (own_shape, F32, page_block(own_shape)),
             ((half, width), BF, whole((half, width))),
             ((8, width), F32, whole((8, width))),
             *grads,
         ],
-        grid=(2,),
+        grid=(4,),
         scratch=[pltpu.VMEM((tokens, width), F32)],
         scalars=scalars,
         deps=deps,
-        work=(4 * tokens * width * cols, 2e7, 0),
+        work=(4 * tokens * width * (cols + wq.shape[1]), 4e7, 0),
     )
 
 
@@ -799,9 +790,13 @@
     )
 
 
-def stat_lanes(stats, head, first, base):
-    row, col = iota((LANES, LANES), 0), iota((LANES, LANES), 1)
-    hit = (row == first + head + 16 * (col - base)) & (col >= base) & (col < base + 3)
+def stat_lanes(stats, pair, bases):
+    shape = (LANES, 4 * LANES)
+    row, col = iota(shape, 0), iota(shape, 1)
+    group, lane = col // LANES, col % LANES
+    side = group % 2
+    place = lane - jnp.where(side == 0, bases[0], bases[1])
+    hit = (row == 48 * (group // 2) + 2 * pair + side + 16 * place) & (place >= 0) & (place < 3)
     return dot(stats, jnp.where(hit, -1.0, 0.0).astype(BF)).astype(BF)
 
 
@@ -823,8 +818,10 @@
     def sides(block):
         q, g, st = take(qs, block), take(gos, block), take(stats, block)
         scaled = q * SCALE
-        shifted = [scaled * masks[s] + (stat_lanes(st, 2 * pair + s, 0, bases[s]) + plain[s]) for s in range(2)]
-        lowered = [g * masks[s] + stat_lanes(st, 2 * pair + s, 48, bases[s]) for s in range(2)]
+        lanes = stat_lanes(st, pair, bases)
+        part = lambda k: lanes[:, k * LANES : (k + 1) * LANES]
+        shifted = [scaled * masks[s] + (part(s) + plain[s]) for s in range(2)]
+        lowered = [g * masks[s] + part(2 + s) for s in range(2)]
         return q, g, shifted, lowered
 
     for ref in near_dqs:
@@ -1477,13 +1474,13 @@
         scalars, segment_ids, slot_valid, query_in, query_theirs, gains, w_qqkv, [patch_sent]
     )
     qs = gather(q_own)
-    cot_sent, cot_q_sent = pack_two(scalars, cot, query_cot, [q_own])
+    x, normed_one, qkv, cross, key_bias = patch_in(
+        scalars, row_valid, visual, patch_other, gains, w_vqkv, w_xkv, form, [q_own]
+    )
+    att = window_forward(qkv, window, [])
+    cot_sent, cot_q_sent = pack_two(scalars, cot, query_cot, [att])
     cot_other, cot_theirs = from_ahead(cot_sent, count, 1), from_partner(cot_q_sent, count)
-    x, normed_one, qkv, cross, key_bias = patch_in(
-        scalars, row_valid, visual, patch_other, gains, w_vqkv, w_xkv, form, [cot_q_sent]
-    )
-    att = window_forward(qkv, window, [])
-    q_out = query_forward(qs, cross, slot_kv, key_bias, same, blocks, [att, cot_theirs])
+    q_out = query_forward(qs, cross, slot_kv, key_bias, same, blocks, [cot_q_sent])
     out_parts = give_back(q_out)
     (vis_own, vis_other, grad_after, grad_att, g_vout, g_up, g_down, gain_two) = patch_ffn(
         scalars, att, x, cot, cot_other, gains, w_vout, w_up, w_down, tiled, form, [q_out[0]]
@@ -1518,9 +1515,8 @@
             out_0, keep_0, out_1, keep_1 = halve_add(scalars, [keep_0, keep_1], got, part + 1, last)
             got = [across(out_0, ORDERS[0][part + 1]), across(out_1, ORDERS[1][part + 1])]
             last = [keep_0]
-    back_part, g_vqkv = qkv_back(g_proj, normed_one, w_vqkv, tiled, last)
-    vin_own, vin_other, gain_rows, *g_xkv = cross_back(
-        scalars, dks, dvs, normed_one, x, grad_after, back_part, gains, w_xkv, gain_two, gain_four, pages, tiled, form, []
+    vin_own, vin_other, gain_rows, g_vqkv, *g_xkv = patch_back(
+        scalars, g_proj, w_vqkv, dks, dvs, normed_one, x, grad_after, gains, w_xkv, gain_two, gain_four, pages, tiled, form, last
     )
     qin_own, qin_other, g_qqkv, gain_grads = query_out(
         scalars, dqs, dsks, dsvs, normed_three, x_query, grad_q, gains, w_qqkv, gain_rows, pages, tiled, got if tiled else []

time: 488 us -> 458 us (0.939)
  Pallas kernels: 390 us -> 372 us
  starting transfers between devices: 61.3 us -> 49.4 us
    pallas_call x18 -> x17, Pallas kernels: 297 us -> 277 us  [call(): pl.pallas_call(body, grid_spec=pltpu.PrefetchScalarGridSpec(num_scalar_pr...]
    ppermute x19, starting transfers between devices: 45.9 us -> 38.5 us  [from_ahead(): lax.ppermute(array, 'strip', [(i, (i - distance) % count) for i in range(...]
  transfers between devices with their start and end apart: 29 -> 29, of which waited for: 4 -> 3; matrix products, arithmetic and copies ran while one was open for 1% -> 1% of each run, Pallas kernels for 80% -> 81%
where the time goes in v1:
time: 458 us; the launch traced here: 449 us
  Pallas kernels  372 us (81%)
  starting transfers between devices  49.4 us (11%)
  waiting for transfers between devices  18.6 us (4%)
  local copies, waits for them, and re-layouts  6.85 us (1%)
    pallas_call x17, Pallas kernels, call(): pl.pallas_call(body, grid_spec=pltpu.PrefetchScalarGridSpec(num_scalar_pr...  277 us
    pallas_call x1, Pallas kernels, late_sum(): pl.pallas_call(lambda *refs: kernel(*refs[:first], *refs[first + len(deps...  67.9 us
    ppermute x19, starting transfers between devices, from_ahead(): lax.ppermute(array, 'strip', [(i, (i - distance) % count) for i in range(...  38.5 us
    pallas_call x1, Pallas kernels, query_sum(): pl.pallas_call(lambda *refs: kernel(*refs[:9], *refs[9 + len(deps):]), in...  23.1 us
    ppermute x19, waiting for transfers between devices, from_ahead(): lax.ppermute(array, 'strip', [(i, (i - distance) % count) for i in range(...  11.5 us
  transfers between devices with their start and end apart: 29, of which 3 were waited for; matrix products, arithmetic and copies ran while one was open for 1% of the time, Pallas kernels for 81%

profile of v1, /device:TPU:0, one launch (start us, length us, event | category | flops | bytes accessed | tf_op | source)
XLA Modules:
  0.0 448.8 jit_solution(7061924946008676309)
XLA Ops:
  2.0 1.2 dynamic_slice.4
  3.3 1.2 stack.33.refs_0_
  4.5 3.0 pack.1
  7.5 3.0 collective-permute-start
  10.5 5.7 %collective-permute-done.refs_1_.refs_4_ = bf16[144,768]{1,0:T(8,128)(2,1)} collective-permute-done((bf16[144,768]{1,0:T(8,128)(2,1)}, bf16[144,768]{1,0:T(8,128)(2,1)}, u32[]{:S(2)}, u32[]{:S(2)}) %collective-permute-start) | collective-permute-done | bytes 221216 | tf_op jit(solution)/shard_map/ppermute | solution.py:1422
  16.2 4.8 %collective-permute-start.1 = (bf16[592,768]{1,0:T(8,128)(2,1)}, bf16[592,768]{1,0:T(8,128)(2,1)}, u32[]{:S(2)}, u32[]{:S(2)}) collective-permute-start(bf16[592,768]{1,0:T(8,128)(2,1)} %held_back.1.refs_7_), channel_id=1, source_target_pairs={{0,7},{1,0},{2,1},{3,2},{4,3},{5,4},{6,5},{7,6},{8,15},{9,8},{10,9... | collective-permute-start | bytes 2727944 | tf_op jit(solution)/shard_map/ppermute | solution.py:1418
  21.0 0.6 pad.4.refs_5_.refs_4_.refs_8_.refs_10_.refs_16_
  21.6 5.1 %query_in.1 = (bf16[256,768]{1,0:T(8,128)(2,1)}, bf16[256,768]{1,0:T(8,128)(2,1)}, bf16[256,768]{1,0:T(8,128)(2,1)}, bf16[256,1536]{1,0:T(8,128)(2,1)}, bf16[320...) custom-call(s32[9]{0:T(128)} %stack.33.refs_0_, s32[2,1024]{1,0:T(2,128)} %refs_1_.4, s32[2,128]{1,0:T(2,128)} %refs_2_.5, ...), custom_call_target="tpu_custom_call" | custom-call | flops 2717908992 | bytes 5000000 | tf_op jit(solution)/shard_map/query_in/pallas_call | solution.py:103
  26.7 0.0 collective-permute-start.3
  26.7 3.8 collective-permute-start.4
  30.5 0.0 collective-permute-start.5
  30.5 11.4 %collective-permute-done.1.refs_3_ = bf16[592,768]{1,0:T(8,128)(2,1)} collective-permute-done((bf16[592,768]{1,0:T(8,128)(2,1)}, bf16[592,768]{1,0:T(8,128)(2,1)}, u32[]{:S(2)}, u32[]{:S(2)}) %collective-permute-start.1) | collective-permute-done | bytes 909344 | tf_op jit(solution)/shard_map/ppermute | solution.py:1418
  42.0 16.1 %patch_in.1 = (bf16[1152,768]{1,0:T(8,128)(2,1)}, bf16[1152,768]{1,0:T(8,128)(2,1)}, bf16[1152,2304]{1,0:T(8,128)(2,1)}, bf16[1152,1536]{1,0:T(8,128)(2,1)}, bf16[1152,128]{1,0:T(8,128)(2,1)}) custom-call(s32[9]{0:T(128)} %stack.33.refs_0_, s32[2,6]{1,0:T(2,128)} %refs_1_.5, bf16[2,576,768]{2,1,0:T(8,128)(2,1)} %bitcast.39, ...), custom_call_target="tpu_custom_call" | custom-call | flops 20384317440 | bytes 20000000 | tf_op jit(solution)/shard_map/patch_in/pallas_call | solution.py:103
  58.1 15.7 %window_forward.1.refs_3_.refs_1_ = bf16[1152,768]{1,0:T(8,128)(2,1)} custom-call(bf16[1152,2304]{1,0:T(8,128)(2,1)} %get-tuple-element.109.refs_0_), custom_call_target="tpu_custom_call" | custom-call | flops 6115295232 | bytes 8000000 | tf_op jit(solution)/shard_map/window_forward/pallas_call | solution.py:103
  73.8 2.9 pack_two.1
  76.7 5.2 %collective-permute-start.2 = (bf16[576,768]{1,0:T(8,128)(2,1)}, bf16[576,768]{1,0:T(8,128)(2,1)}, u32[]{:S(2)}, u32[]{:S(2)}) collective-permute-start(bf16[576,768]{1,0:T(8,128)(2,1)} %get-tuple-element.111), channel_id=1, source_target_pairs={{0,7},{1,0},{2,1},{3,2},{4,3},{5,4},{6,5},{7,6},{8,15},{9,8},{10,9... | collective-permute-start | bytes 2654216 | tf_op jit(solution)/shard_map/ppermute | solution.py:1418
  81.9 0.0 collective-permute-start.10
  81.9 0.0 collective-permute-done.5.refs_3_
  81.9 28.2 %query_forward.1 = (bf16[256,896]{1,0:T(8,128)(2,1)}, bf16[256,896]{1,0:T(8,128)(2,1)}, bf16[256,896]{1,0:T(8,128)(2,1)}, bf16[256,896]{1,0:T(8,128)(2,1)}) custom-call(bf16[256,768]{1,0:T(8,128)(2,1)} %collective-permute-done.3.refs_0_, bf16[256,768]{1,0:T(8,128)(2,1)} %get-tuple-element.108.refs_7_.refs_1_, ...), custom_call_target="tpu_custom_call" | custom-call | flops 43486543872 | bytes 10000000 | tf_op jit(solution)/shard_map/query_forward/pallas_call | solution.py:103
  110.1 0.6 collective-permute-start.7
  110.7 3.6 collective-permute-start.8
  114.3 2.9 collective-permute-start.9
  117.2 56.0 %patch_ffn.1 = (bf16[2,576,768]{2,1,0:T(8,128)(2,1)}, bf16[576,768]{1,0:T(8,128)(2,1)}, f32[1152,768]{1,0:T(8,128)}, bf16[1152,768]{1,0:T(8,128)(2,1)}, bf16[2,2...) custom-call(s32[9]{0:T(128)} %stack.33.refs_0_, ...), custom_call_target="tpu_custom_call" | custom-call | flops 97844723712 | bytes 40000000 | tf_op jit(solution)/shard_map/patch_ffn/pallas_call | solution.py:103
  173.1 2.1 collective-permute-start.6
  175.2 0.0 collective-permute-done.10.refs_7_
  175.2 0.0 collective-permute-done.7.refs_1_
  175.2 0.0 collective-permute-done.9.refs_4_
  175.2 17.0 %query_ffn.1 = (bf16[2,128,768]{2,1,0:T(8,128)(2,1)}, bf16[128,768]{1,0:T(8,128)(2,1)}, f32[256,768]{1,0:T(8,128)}, bf16[256,896]{1,0:T(8,128)(2,1)}, bf16[256,7...) custom-call(s32[9]{0:T(128)} %stack.33.refs_0_, ...), custom_call_target="tpu_custom_call" | custom-call | flops 14495514624 | bytes 20000000 | tf_op jit(solution)/shard_map/query_ffn/pallas_call | solution.py:103
  192.2 0.1 collective-permute-start.11
  192.3 0.0 collective-permute-start.12
  192.4 3.8 collective-permute-start.13
  196.2 23.1 %query_sum.1 = (bf16[2,4,1296,128]{3,2,1,0:T(8,128)(2,1)}, bf16[2,4,1296,128]{3,2,1,0:T(8,128)(2,1)}, bf16[2,4,1296,128]{3,2,1,0:T(8,128)(2,1)}, bf16[2,4,1296,128]{3,2,1,0:T(8,128)(2,1)}) custom-call(bf16[2,2,2,4,576,128]{5,4,3,2,1,0:T(8,128)(2,1)} %get-tuple-element.128.refs_0_, bf16[2,2,2,4,576,128]{5,4,3,2,1,0:T(8,128)(2,1)} %get-tuple-element.129.refs_1_, ...), custom_call_target="tpu_custom_call" | custom-call | tf_op jit(solution)/shard_map/query_sum/pallas_call | solution.py:1197
  219.3 0.0 collective-permute-done.11.refs_19_
  219.3 2.0 collective-permute-start.15
  221.3 1.5 collective-permute-start.16
  222.8 24.5 %window_backward.1.refs_18_.refs_1_ = bf16[1152,2304]{1,0:T(8,128)(2,1)} custom-call(bf16[1152,2304]{1,0:T(8,128)(2,1)} %get-tuple-element.109.refs_0_, bf16[1152,768]{1,0:T(8,128)(2,1)} %get-tuple-element.127.refs_1_, bf16[8,1296,128]{2,1,0:T(8,128)(2,1)} %bitcast.30, bf16[576,768]{1,0:T(8,128)(2,1)} %collective-permute-done.6.refs_3_), custom_call_target="tpu_custom_call" | custom-call | flops 15288238080 | bytes 13000000 | tf_op jit(solution)/shard_map/window_backward/pallas_call | solution.py:103
  247.3 0.0 collective-permute-done.12.refs_4_.refs_8_
  247.3 0.0 collective-permute-done.13.refs_6_.refs_10_
  247.3 27.2 %query_backward.2 = (bf16[256,384]{1,0:T(8,128)(2,1)}, bf16[256,384]{1,0:T(8,128)(2,1)}, bf16[256,384]{1,0:T(8,128)(2,1)}, bf16[256,384]{1,0:T(8,128)(2,1)}, bf1...) custom-call(bf16[256,768]{1,0:T(8,128)(2,1)} %collective-permute-done.3, ...), custom_call_target="tpu_custom_call" | custom-call | flops 27179089920 | bytes 15000000 | tf_op jit(solution)/shard_map/query_backward/pallas_call | solution.py:103
  274.6 0.6 collective-permute-start.19
  275.2 1.5 collective-permute-start.20
  276.7 2.9 collective-permute-start.21
  279.6 0.0 collective-permute-done.15.refs_2_.refs_4_
  279.6 1.4 collective-permute-done.16.refs_6_.refs_8_
  280.9 7.8 %halve_add.2 = (bf16[4,1296,128]{2,1,0:T(8,128)(2,1)}, bf16[4,1296,128]{2,1,0:T(8,128)(2,1)}, bf16[4,1296,128]{2,1,0:T(8,128)(2,1)}, bf16[4,1296,128]{2,1,0:T(8,128)(2,1)}) custom-call(s32[9]{0:T(128)} %stack.33.refs_0_, bf16[8,1296,128]{2,1,0:T(8,128)(2,1)} %bitcast.31, bf16[8,1296,128]{2,1,0:T(8,128)(2,1)} %collective-permute-done.15.refs_2_.refs_4_, ...), custom_call_target="tpu_custom_call" | custom-call | flops 3000000 | bytes 15925248 | tf_op jit(solution)/shard_map/halve_add/pallas_call | solution.py:103
  288.8 1.5 collective-permute-start.17
  290.3 0.4 collective-permute-start.18
  290.7 27.1 %query_backward.3 = (bf16[256,384]{1,0:T(8,128)(2,1)}, bf16[256,384]{1,0:T(8,128)(2,1)}, bf16[256,384]{1,0:T(8,128)(2,1)}, bf16[256,384]{1,0:T(8,128)(2,1)}, bf1...) custom-call(bf16[256,768]{1,0:T(8,128)(2,1)} %collective-permute-done.3, ...), custom_call_target="tpu_custom_call" | custom-call | flops 27179089920 | bytes 15000000 | tf_op jit(solution)/shard_map/query_backward/pallas_call | solution.py:103
  317.8 0.0 collective-permute-done.19.refs_10_.refs_1_
  317.8 1.2 collective-permute-start.22
  319.0 0.9 collective-permute-start.23
  319.9 2.9 collective-permute-start.24
  322.8 4.5 halve_add.3
  327.3 0.6 collective-permute-start.25
  327.9 1.5 collective-permute-start.26
  329.4 29.9 %patch_back.1 = (f32[2,576,768]{2,1,0:T(8,128)}, bf16[576,768]{1,0:T(8,128)(2,1)}, f32[8,768]{1,0:T(8,128)}, bf16[2,2,2,4,432,128]{5,4,3,2,1,0:T(8,128)(2,1)}, b...) custom-call(s32[9]{0:T(128)} %stack.33.refs_0_, ...), custom_call_target="tpu_custom_call" | custom-call | flops 40768634880 | bytes 40000000 | tf_op jit(solution)/shard_map/patch_back/pallas_call | solution.py:103
  359.3 1.7 collective-permute-start.27
  361.0 1.6 bitcast_dynamic-update-slice_fusion.1
  362.7 8.6 %query_out.1 = (f32[2,128,768]{2,1,0:T(8,128)}, bf16[128,768]{1,0:T(8,128)(2,1)}, bf16[2,2,2,4,432,128]{5,4,3,2,1,0:T(8,128)(2,1)}, bf16[2,2,2,4,48,128]{5,4,3,2,1,0:T(8,128)(2,1)}) custom-call(s32[9]{0:T(128)} %stack.33.refs_0_, bf16[256,384]{1,0:T(8,128)(2,1)} %collective-permute-done.19.refs_10_.refs_1_, ...), custom_call_target="tpu_custom_call" | custom-call | flops 5435817984 | bytes 10000000 | tf_op jit(solution)/shard_map/query_out/pallas_call | solution.py:103
  371.2 0.4 collective-permute-start.28
  371.6 2.1 bitcast_dynamic-update-slice_fusion
  373.7 67.9 %late_sum.1 = (bf16[1920,128]{1,0:T(8,128)(2,1)}, bf16[1872,128]{1,0:T(8,128)(2,1)}, bf16[1920,128]{1,0:T(8,128)(2,1)}, bf16[1872,128]{1,0:T(8,128)(2,1)}) custom-call(bf16[2,16,432,128]{3,2,1,0:T(8,128)(2,1)} %bitcast.35, bf16[2,16,144,128]{3,2,1,0:T(8,128)(2,1)} %bitcast.42, bf16[2,16,48,128]{3,2,1,0:T(8,128)(2,1)} %bitcast.44, ...), custom_call_target="tpu_custom_call" | custom-call | tf_op jit(solution)/shard_map/late_sum/pallas_call | solution.py:1339
  441.7 3.6 finish.1
  445.3 3.3 put_two.1
  (21 shorter events, 0.1 us)
Async XLA Ops:
  0.6 20.3 %copy-start = (f32[768,4]{0,1:T(4,128)S(1)}, f32[768,4]{0,1:T(4,128)}, u32[]{:S(2)}) copy-start(f32[768,4]{0,1:T(4,128)} %param.26) | copy-start | bytes 36868
  7.5 8.7 %collective-permute-start = (bf16[144,768]{1,0:T(8,128)(2,1)}, bf16[144,768]{1,0:T(8,128)(2,1)}, u32[]{:S(2)}, u32[]{:S(2)}) collective-permute-start(bf16[144,768]{1,0:T(8,128)(2,1)} %get-tuple-element.107), channel_id=1, source_target_pairs={{0,1},{1,0},{2,3},{3,2},{4,5},{5,4},{6,7},{7,6},{8,9},{9,8},{10,11... | collective-permute-start | bytes 663560 | tf_op jit(solution)/shard_map/ppermute | solution.py:1422
  16.2 25.8 %collective-permute-start.1 = (bf16[592,768]{1,0:T(8,128)(2,1)}, bf16[592,768]{1,0:T(8,128)(2,1)}, u32[]{:S(2)}, u32[]{:S(2)}) collective-permute-start(bf16[592,768]{1,0:T(8,128)(2,1)} %held_back.1.refs_7_), channel_id=1, source_target_pairs={{0,7},{1,0},{2,1},{3,2},{4,3},{5,4},{6,5},{7,6},{8,15},{9,8},{10,9... | collective-permute-start | bytes 2727944 | tf_op jit(solution)/shard_map/ppermute | solution.py:1418
  26.7 55.2 %collective-permute-start.3 = (bf16[256,768]{1,0:T(8,128)(2,1)}, bf16[256,768]{1,0:T(8,128)(2,1)}, u32[]{:S(2)}, u32[]{:S(2)}) collective-permute-start(bf16[256,768]{1,0:T(8,128)(2,1)} %get-tuple-element.108.refs_7_.refs_1_), channel_id=1, source_target_pairs={{0,2},{1,3},{2,4},{3,5},{4,6},{5,7},{6,0},{7,1},{8,10},{9,11},{10,... | collective-permute-start | bytes 1179656 | tf_op jit(solution)/shard_map/ppermute | solution.py:1418
  26.7 55.2 %collective-permute-start.4 = (bf16[256,768]{1,0:T(8,128)(2,1)}, bf16[256,768]{1,0:T(8,128)(2,1)}, u32[]{:S(2)}, u32[]{:S(2)}) collective-permute-start(bf16[256,768]{1,0:T(8,128)(2,1)} %get-tuple-element.108.refs_7_.refs_1_), channel_id=1, source_target_pairs={{0,6},{1,7},{2,0},{3,1},{4,2},{5,3},{6,4},{7,5},{8,14},{9,15},{10,... | collective-permute-start | bytes 1179656 | tf_op jit(solution)/shard_map/ppermute | solution.py:1418
  30.5 51.4 %collective-permute-start.5 = (bf16[256,768]{1,0:T(8,128)(2,1)}, bf16[256,768]{1,0:T(8,128)(2,1)}, u32[]{:S(2)}, u32[]{:S(2)}) collective-permute-start(bf16[256,768]{1,0:T(8,128)(2,1)} %get-tuple-element.108.refs_7_.refs_1_), channel_id=1, source_target_pairs={{0,4},{1,5},{2,6},{3,7},{4,0},{5,1},{6,2},{7,3},{8,12},{9,13},{10,... | collective-permute-start | bytes 1179656 | tf_op jit(solution)/shard_map/ppermute | solution.py:1418
  76.7 40.4 %collective-permute-start.2 = (bf16[576,768]{1,0:T(8,128)(2,1)}, bf16[576,768]{1,0:T(8,128)(2,1)}, u32[]{:S(2)}, u32[]{:S(2)}) collective-permute-start(bf16[576,768]{1,0:T(8,128)(2,1)} %get-tuple-element.111), channel_id=1, source_target_pairs={{0,7},{1,0},{2,1},{3,2},{4,3},{5,4},{6,5},{7,6},{8,15},{9,8},{10,9... | collective-permute-start | bytes 2654216 | tf_op jit(solution)/shard_map/ppermute | solution.py:1418
  81.9 93.3 %collective-permute-start.10 = (bf16[128,768]{1,0:T(8,128)(2,1)}, bf16[128,768]{1,0:T(8,128)(2,1)}, u32[]{:S(2)}, u32[]{:S(2)}) collective-permute-start(bf16[128,768]{1,0:T(8,128)(2,1)} %get-tuple-element.116.refs_10_), channel_id=1, source_target_pairs={{0,1},{1,0},{2,3},{3,2},{4,5},{5,4},{6,7},{7,6},{8,9},{9,8},{10,11... | collective-permute-start | bytes 589832 | tf_op jit(solution)/shard_map/ppermute | solution.py:1422
  110.1 65.1 %collective-permute-start.7 = (bf16[256,896]{1,0:T(8,128)(2,1)}, bf16[256,896]{1,0:T(8,128)(2,1)}, u32[]{:S(2)}, u32[]{:S(2)}) collective-permute-start(bf16[256,896]{1,0:T(8,128)(2,1)} %get-tuple-element.117.refs_9_), channel_id=1, source_target_pairs={{0,6},{1,7},{2,0},{3,1},{4,2},{5,3},{6,4},{7,5},{8,14},{9,15},{10,... | collective-permute-start | bytes 1376264 | tf_op jit(solution)/shard_map/ppermute | solution.py:1418
  110.7 64.5 %collective-permute-start.8 = (bf16[256,896]{1,0:T(8,128)(2,1)}, bf16[256,896]{1,0:T(8,128)(2,1)}, u32[]{:S(2)}, u32[]{:S(2)}) collective-permute-start(bf16[256,896]{1,0:T(8,128)(2,1)} %get-tuple-element.121), channel_id=1, source_target_pairs={{0,2},{1,3},{2,4},{3,5},{4,6},{5,7},{6,0},{7,1},{8,10},{9,11},{10,... | collective-permute-start | bytes 1376264 | tf_op jit(solution)/shard_map/ppermute | solution.py:1418
  114.3 60.9 %collective-permute-start.9 = (bf16[256,896]{1,0:T(8,128)(2,1)}, bf16[256,896]{1,0:T(8,128)(2,1)}, u32[]{:S(2)}, u32[]{:S(2)}) collective-permute-start(bf16[256,896]{1,0:T(8,128)(2,1)} %get-tuple-element.122), channel_id=1, source_target_pairs={{0,4},{1,5},{2,6},{3,7},{4,0},{5,1},{6,2},{7,3},{8,12},{9,13},{10,... | collective-permute-start | bytes 1376264 | tf_op jit(solution)/shard_map/ppermute | solution.py:1418
  173.1 48.2 %collective-permute-start.6 = (bf16[576,768]{1,0:T(8,128)(2,1)}, bf16[576,768]{1,0:T(8,128)(2,1)}, u32[]{:S(2)}, u32[]{:S(2)}) collective-permute-start(bf16[576,768]{1,0:T(8,128)(2,1)} %get-tuple-element.119), channel_id=1, source_target_pairs={{0,1},{1,2},{2,3},{3,4},{4,5},{5,6},{6,7},{7,0},{8,9},{9,10},{10,1... | collective-permute-start | bytes 2654216 | tf_op jit(solution)/shard_map/ppermute | solution.py:1418
  192.2 27.1 %collective-permute-start.11 = (bf16[128,768]{1,0:T(8,128)(2,1)}, bf16[128,768]{1,0:T(8,128)(2,1)}, u32[]{:S(2)}, u32[]{:S(2)}) collective-permute-start(bf16[128,768]{1,0:T(8,128)(2,1)} %get-tuple-element.126), channel_id=1, source_target_pairs={{0,1},{1,0},{2,3},{3,2},{4,5},{5,4},{6,7},{7,6},{8,9},{9,8},{10,11... | collective-permute-start | bytes 589832 | tf_op jit(solution)/shard_map/ppermute | solution.py:1422
  192.3 55.0 %collective-permute-start.12 = (bf16[256,896]{1,0:T(8,128)(2,1)}, bf16[256,896]{1,0:T(8,128)(2,1)}, u32[]{:S(2)}, u32[]{:S(2)}) collective-permute-start(bf16[256,896]{1,0:T(8,128)(2,1)} %get-tuple-element.138.refs_5_.refs_9_), channel_id=1, source_target_pairs={{0,2},{1,3},{2,4},{3,5},{4,6},{5,7},{6,0},{7,1},{8,10},{9,11},{10,... | collective-permute-start | bytes 1376264 | tf_op jit(solution)/shard_map/ppermute | solution.py:1418
  192.4 55.0 %collective-permute-start.13 = (bf16[256,896]{1,0:T(8,128)(2,1)}, bf16[256,896]{1,0:T(8,128)(2,1)}, u32[]{:S(2)}, u32[]{:S(2)}) collective-permute-start(bf16[256,896]{1,0:T(8,128)(2,1)} %get-tuple-element.138.refs_5_.refs_9_), channel_id=1, source_target_pairs={{0,6},{1,7},{2,0},{3,1},{4,2},{5,3},{6,4},{7,5},{8,14},{9,15},{10,... | collective-permute-start | bytes 1376264 | tf_op jit(solution)/shard_map/ppermute | solution.py:1418
  196.2 51.2 %collective-permute-start.14 = (bf16[256,896]{1,0:T(8,128)(2,1)}, bf16[256,896]{1,0:T(8,128)(2,1)}, u32[]{:S(2)}, u32[]{:S(2)}) collective-permute-start(bf16[256,896]{1,0:T(8,128)(2,1)} %get-tuple-element.138.refs_5_.refs_9_), channel_id=1, source_target_pairs={{0,4},{1,5},{2,6},{3,7},{4,0},{5,1},{6,2},{7,3},{8,12},{9,13},{10,... | collective-permute-start | bytes 1376264 | tf_op jit(solution)/shard_map/ppermute | solution.py:1418
  219.3 60.3 %collective-permute-start.15 = (bf16[8,1296,128]{2,1,0:T(8,128)(2,1)}, bf16[8,1296,128]{2,1,0:T(8,128)(2,1)}, u32[]{:S(2)}, u32[]{:S(2)}) collective-permute-start(bf16[8,1296,128]{2,1,0:T(8,128)(2,1)} %bitcast.49), channel_id=1, source_target_pairs={{0,1},{1,0},{2,3},{3,2},{4,5},{5,4},{6,7},{7,6},{8,9},{9,8},{10,11... | collective-permute-start | bytes 7962632 | tf_op jit(solution)/shard_map/ppermute | solution.py:1221
  221.3 59.6 %collective-permute-start.16 = (bf16[8,1296,128]{2,1,0:T(8,128)(2,1)}, bf16[8,1296,128]{2,1,0:T(8,128)(2,1)}, u32[]{:S(2)}, u32[]{:S(2)}) collective-permute-start(bf16[8,1296,128]{2,1,0:T(8,128)(2,1)} %bitcast.48), channel_id=1, source_target_pairs={{0,16},{8,24},{16,0},{24,8},{1,17},{9,25},{17,1},{25,9},{2,18},{10... | collective-permute-start | bytes 7962632 | tf_op jit(solution)/shard_map/ppermute | solution.py:1221
  274.6 43.2 %collective-permute-start.19 = (bf16[256,384]{1,0:T(8,128)(2,1)}, bf16[256,384]{1,0:T(8,128)(2,1)}, u32[]{:S(2)}, u32[]{:S(2)}) collective-permute-start(bf16[256,384]{1,0:T(8,128)(2,1)} %get-tuple-element.154), channel_id=1, source_target_pairs={{0,6},{1,7},{2,0},{3,1},{4,2},{5,3},{6,4},{7,5},{8,14},{9,15},{10,... | collective-permute-start | bytes 589832 | tf_op jit(solution)/shard_map/ppermute | solution.py:1418
  275.2 43.8 %collective-permute-start.20 = (bf16[256,384]{1,0:T(8,128)(2,1)}, bf16[256,384]{1,0:T(8,128)(2,1)}, u32[]{:S(2)}, u32[]{:S(2)}) collective-permute-start(bf16[256,384]{1,0:T(8,128)(2,1)} %get-tuple-element.156), channel_id=1, source_target_pairs={{0,2},{1,3},{2,4},{3,5},{4,6},{5,7},{6,0},{7,1},{8,10},{9,11},{10,... | collective-permute-start | bytes 589832 | tf_op jit(solution)/shard_map/ppermute | solution.py:1418
  276.7 43.2 %collective-permute-start.21 = (bf16[256,384]{1,0:T(8,128)(2,1)}, bf16[256,384]{1,0:T(8,128)(2,1)}, u32[]{:S(2)}, u32[]{:S(2)}) collective-permute-start(bf16[256,384]{1,0:T(8,128)(2,1)} %get-tuple-element.157), channel_id=1, source_target_pairs={{0,4},{1,5},{2,6},{3,7},{4,0},{5,1},{6,2},{7,3},{8,12},{9,13},{10,... | collective-permute-start | bytes 589832 | tf_op jit(solution)/shard_map/ppermute | solution.py:1418
  288.8 34.0 %collective-permute-start.17 = (bf16[4,1296,128]{2,1,0:T(8,128)(2,1)}, bf16[4,1296,128]{2,1,0:T(8,128)(2,1)}, u32[]{:S(2)}, u32[]{:S(2)}) collective-permute-start(bf16[4,1296,128]{2,1,0:T(8,128)(2,1)} %get-tuple-element.151), channel_id=1, source_target_pairs={{0,16},{8,24},{16,0},{24,8},{1,17},{9,25},{17,1},{25,9},{2,18},{10... | collective-permute-start | bytes 3981320 | tf_op jit(solution)/shard_map/ppermute | solution.py:1221
  290.3 32.5 %collective-permute-start.18 = (bf16[4,1296,128]{2,1,0:T(8,128)(2,1)}, bf16[4,1296,128]{2,1,0:T(8,128)(2,1)}, u32[]{:S(2)}, u32[]{:S(2)}) collective-permute-start(bf16[4,1296,128]{2,1,0:T(8,128)(2,1)} %get-tuple-element.153), channel_id=1, source_target_pairs={{0,1},{1,0},{2,3},{3,2},{4,5},{5,4},{6,7},{7,6},{8,9},{9,8},{10,11... | collective-permute-start | bytes 3981320 | tf_op jit(solution)/shard_map/ppermute | solution.py:1221
  317.8 41.5 %collective-permute-start.22 = (bf16[256,384]{1,0:T(8,128)(2,1)}, bf16[256,384]{1,0:T(8,128)(2,1)}, u32[]{:S(2)}, u32[]{:S(2)}) collective-permute-start(bf16[256,384]{1,0:T(8,128)(2,1)} %get-tuple-element.160), channel_id=1, source_target_pairs={{0,6},{1,7},{2,0},{3,1},{4,2},{5,3},{6,4},{7,5},{8,14},{9,15},{10,... | collective-permute-start | bytes 589832 | tf_op jit(solution)/shard_map/ppermute | solution.py:1418
  319.0 43.7 %collective-permute-start.23 = (bf16[256,384]{1,0:T(8,128)(2,1)}, bf16[256,384]{1,0:T(8,128)(2,1)}, u32[]{:S(2)}, u32[]{:S(2)}) collective-permute-start(bf16[256,384]{1,0:T(8,128)(2,1)} %get-tuple-element.162), channel_id=1, source_target_pairs={{0,2},{1,3},{2,4},{3,5},{4,6},{5,7},{6,0},{7,1},{8,10},{9,11},{10,... | collective-permute-start | bytes 589832 | tf_op jit(solution)/shard_map/ppermute | solution.py:1418
  319.9 42.8 %collective-permute-start.24 = (bf16[256,384]{1,0:T(8,128)(2,1)}, bf16[256,384]{1,0:T(8,128)(2,1)}, u32[]{:S(2)}, u32[]{:S(2)}) collective-permute-start(bf16[256,384]{1,0:T(8,128)(2,1)} %get-tuple-element.163), channel_id=1, source_target_pairs={{0,4},{1,5},{2,6},{3,7},{4,0},{5,1},{6,2},{7,3},{8,12},{9,13},{10,... | collective-permute-start | bytes 589832 | tf_op jit(solution)/shard_map/ppermute | solution.py:1418
  327.3 35.4 %collective-permute-start.25 = (bf16[2,1296,128]{2,1,0:T(8,128)(2,1)}, bf16[2,1296,128]{2,1,0:T(8,128)(2,1)}, u32[]{:S(2)}, u32[]{:S(2)}) collective-permute-start(bf16[2,1296,128]{2,1,0:T(8,128)(2,1)} %get-tuple-element.171), channel_id=1, source_target_pairs={{0,2},{1,3},{2,0},{3,1},{4,6},{5,7},{6,4},{7,5},{8,10},{9,11},{10,... | collective-permute-start | bytes 1990664 | tf_op jit(solution)/shard_map/ppermute | solution.py:1221
  327.9 34.8 %collective-permute-start.26 = (bf16[2,1296,128]{2,1,0:T(8,128)(2,1)}, bf16[2,1296,128]{2,1,0:T(8,128)(2,1)}, u32[]{:S(2)}, u32[]{:S(2)}) collective-permute-start(bf16[2,1296,128]{2,1,0:T(8,128)(2,1)} %get-tuple-element.172), channel_id=1, source_target_pairs={{0,2},{1,3},{2,0},{3,1},{4,6},{5,7},{6,4},{7,5},{8,10},{9,11},{10,... | collective-permute-start | bytes 1990664 | tf_op jit(solution)/shard_map/ppermute | solution.py:1221
  359.3 85.9 %collective-permute-start.27 = (bf16[576,768]{1,0:T(8,128)(2,1)}, bf16[576,768]{1,0:T(8,128)(2,1)}, u32[]{:S(2)}, u32[]{:S(2)}) collective-permute-start(bf16[576,768]{1,0:T(8,128)(2,1)} %get-tuple-element.174), channel_id=1, source_target_pairs={{0,1},{1,2},{2,3},{3,4},{4,5},{5,6},{6,7},{7,0},{8,9},{9,10},{10,1... | collective-permute-start | bytes 2654216 | tf_op jit(solution)/shard_map/ppermute | solution.py:1418
  371.2 74.0 %collective-permute-start.28 = (bf16[128,768]{1,0:T(8,128)(2,1)}, bf16[128,768]{1,0:T(8,128)(2,1)}, u32[]{:S(2)}, u32[]{:S(2)}) collective-permute-start(bf16[128,768]{1,0:T(8,128)(2,1)} %get-tuple-element.175), channel_id=1, source_target_pairs={{0,1},{1,0},{2,3},{3,2},{4,5},{5,4},{6,7},{7,6},{8,9},{9,8},{10,11... | collective-permute-start | bytes 589832 | tf_op jit(solution)/shard_map/ppermute | solution.py:1422

commit v2 on v1

--- a/solution.py
+++ b/solution.py
@@ -326,20 +326,21 @@
     )
 
 
-def put_two_kernel(s_ref, a_ref, b_ref, a_came, b_came, a_out, b_out):
-    a_out[0] = a_came[...].astype(a_out.dtype)
-    b_out[0] = b_came[...].astype(b_out.dtype)
-
-
-def put_two(scalars, a, b, a_came, b_came, deps):
+def put_kernel(s_ref, *refs):
+    count = len(refs) // 3
+    for came, out in zip(refs[count : 2 * count], refs[2 * count :]):
+        out[0] = came[...].astype(out.dtype)
+
+
+def put(scalars, arrays, came, deps):
     return call(
-        put_two_kernel,
-        "put_two",
-        [(a, ANY), (b, ANY)] + [(x, whole(x.shape)) for x in (a_came, b_came)],
-        [(x.shape, x.dtype, other_page(x.shape)) for x in (a, b)],
+        put_kernel,
+        "put",
+        [(a, ANY) for a in arrays] + [(c, whole(c.shape)) for c in came],
+        [(a.shape, a.dtype, other_page(a.shape)) for a in arrays],
         scalars=scalars,
         deps=deps,
-        aliases={1: 0, 2: 1},
+        aliases={k + 1: k for k in range(len(arrays))},
     )
 
 
@@ -347,6 +348,10 @@
     lane = iota((1, LANES), 1)
     left = lane < 64
     return left, [left.astype(F32).astype(BF), (~left).astype(F32).astype(BF)]
+
+
+def stack(parts, axis=0):
+    return jnp.concatenate(parts, axis=axis)
 
 
 def window_kernel(qkv_ref, out_ref):
@@ -357,13 +362,11 @@
         q = qkv_ref[:, at : at + LANES] * SCALE
         k = qkv_ref[:, width + at : width + at + LANES]
         v = qkv_ref[:, 2 * width + at : 2 * width + at + LANES]
-        all_scores = [dot(q * masks[side], k, 1, 1) for side in range(2)]
-        mixed = []
-        for scores in all_scores:
-            raised = jnp.exp(scores - jnp.max(scores, axis=-1, keepdims=True))
-            total = jnp.sum(raised, axis=-1, keepdims=True)
-            mixed.append(dot(raised.astype(BF), v) * (1.0 / total))
-        out_ref[:, at : at + LANES] = jnp.where(left, mixed[0], mixed[1]).astype(BF)
+        scores = dot(stack([q * masks[0], q * masks[1]]), k, 1, 1)
+        raised = jnp.exp(scores - jnp.max(scores, axis=-1, keepdims=True))
+        total = jnp.sum(raised, axis=-1, keepdims=True)
+        mixed = dot(raised.astype(BF), v) * (1.0 / total)
+        out_ref[:, at : at + LANES] = jnp.where(left, mixed[:tokens], mixed[tokens:]).astype(BF)
 
 
 def window_forward(qkv, tokens, deps):
@@ -790,13 +793,12 @@
     )
 
 
-def stat_lanes(stats, pair, bases):
-    shape = (LANES, 4 * LANES)
+def stat_lanes(stats, pair):
+    shape = (LANES, 2 * LANES)
     row, col = iota(shape, 0), iota(shape, 1)
     group, lane = col // LANES, col % LANES
-    side = group % 2
-    place = lane - jnp.where(side == 0, bases[0], bases[1])
-    hit = (row == 48 * (group // 2) + 2 * pair + side + 16 * place) & (place >= 0) & (place < 3)
+    side, place = lane // 4, lane % 4
+    hit = (row == 48 * group + 2 * pair + side + 16 * place) & (side < 2) & (place < 3)
     return dot(stats, jnp.where(hit, -1.0, 0.0).astype(BF)).astype(BF)
 
 
@@ -809,56 +811,52 @@
     pair = pl.program_id(0) + first_pair
     left, masks = head_masks()
     lane = iota((1, LANES), 1)
-    bases = (64, 0)
-    ones = [jnp.where((lane >= b) & (lane < b + 3), 1.0, 0.0).astype(BF) for b in bases]
-    plain = [jnp.where(lane == b + 3, 1.0, 0.0).astype(BF) for b in bases]
-    keys = [jnp.where(lane == bases[s] + 3, kb_ref[...], k_ref[...] * masks[s] + ones[s]) for s in range(2)]
-    values = [v_ref[...] * masks[s] + ones[s] for s in range(2)]
+    patches, slots = k_ref.shape[0], sk_ref.shape[0]
+    ones = [jnp.where((lane >= 4 * k) & (lane < 4 * k + 3), 1.0, 0.0).astype(BF) for k in range(2)]
+    plain = jnp.where(lane == 8, 1.0, 0.0).astype(BF)
+
+    def both_heads(rows, bias=None):
+        extra = [jnp.broadcast_to(ones[k], rows.shape) for k in range(2)]
+        if bias is not None:
+            extra = [jnp.where(lane == 8, bias, e) for e in extra]
+        return stack([stack([rows * masks[k], extra[k]], 1) for k in range(2)])
+
+    keys, values = both_heads(k_ref[...], kb_ref[...]), both_heads(v_ref[...])
 
     def sides(block):
         q, g, st = take(qs, block), take(gos, block), take(stats, block)
-        scaled = q * SCALE
-        lanes = stat_lanes(st, pair, bases)
-        part = lambda k: lanes[:, k * LANES : (k + 1) * LANES]
-        shifted = [scaled * masks[s] + (part(s) + plain[s]) for s in range(2)]
-        lowered = [g * masks[s] + part(2 + s) for s in range(2)]
-        return q, g, shifted, lowered
+        lanes = stat_lanes(st, pair)
+        return q, g, stack([q * SCALE, lanes[:, :LANES] + plain], 1), stack([g, lanes[:, LANES:]], 1)
 
     for ref in near_dqs:
         ref[...] = jnp.zeros_like(ref)
     q, g, shifted, lowered = sides(near_block)
-    same = same_ref[...].astype(F32) > 0.5
-    moved, dsk, dsv = [], [], []
-    for s in range(2):
-        scores = dot(sk_ref[...] * masks[s] + ones[s], shifted[s], 1, 1)
-        probs = jnp.exp(jnp.where(same, scores, MASKED))
-        dscore = (probs * dot(sv_ref[...] * masks[s] + ones[s], lowered[s], 1, 1)).astype(BF)
-        dsk.append(dot(dscore, q))
-        dsv.append(dot(probs.astype(BF), g))
-        moved.append(dot(dscore, sk_ref[...], 0, 0))
+    same = same_ref[...].astype(F32)
+    scores = dot(both_heads(sk_ref[...]), shifted, 1, 1)
+    probs = jnp.exp(jnp.where(stack([same, same]) > 0.5, scores, MASKED))
+    dscore = (probs * dot(both_heads(sv_ref[...]), lowered, 1, 1)).astype(BF)
+    dsk, dsv = dot(dscore, q), dot(probs.astype(BF), g)
+    moved = [dot(dscore[k * slots : (k + 1) * slots], sk_ref[...], 0, 0) for k in range(2)]
     give(near_dqs, near_block, jnp.where(left, moved[0], moved[1]))
-    dsk_ref[...] = (jnp.where(left, dsk[0], dsk[1]) * SCALE).astype(BF)
-    dsv_ref[...] = jnp.where(left, dsv[0], dsv[1]).astype(BF)
+    dsk_ref[...] = (jnp.where(left, dsk[:slots], dsk[slots:]) * SCALE).astype(BF)
+    dsv_ref[...] = jnp.where(left, dsv[:slots], dsv[slots:]).astype(BF)
 
     for number, block in enumerate(blocks):
         q, g, shifted, lowered = sides(block)
-        scores = [dot(keys[s], shifted[s], 1, 1) for s in range(2)]
-        grads = [dot(values[s], lowered[s], 1, 1) for s in range(2)]
-        dq, dk, dv = [], [], []
-        for s in range(2):
-            probs = jnp.exp(scores[s])
-            dscore = (probs * grads[s]).astype(BF)
-            dv.append(dot(probs.astype(BF), g))
-            dk.append(dot(dscore, q))
-            dq.append(dot(dscore, k_ref[...], 0, 0))
+        size = q.shape[0]
+        probs = jnp.exp(dot(keys, shifted, 1, 1))
+        dscore = (probs * dot(values, lowered, 1, 1)).astype(BF)
+        dv = dot(probs.astype(BF), g)
+        dk = dot(dscore, q)
+        dq = dot(stack([dscore[:patches], dscore[patches:]], 1), k_ref[...], 0, 0)
         near = take(near_dqs, block)
-        give(dqs, block, (jnp.where(left, dq[0], dq[1]) + near) * SCALE)
+        give(dqs, block, (jnp.where(left, dq[:size], dq[size:]) + near) * SCALE)
         if number == 0:
-            sum_k[...] = jnp.where(left, dk[0], dk[1])
-            sum_v[...] = jnp.where(left, dv[0], dv[1])
+            sum_k[...] = jnp.where(left, dk[:patches], dk[patches:])
+            sum_v[...] = jnp.where(left, dv[:patches], dv[patches:])
         else:
-            sum_k[...] += jnp.where(left, dk[0], dk[1])
-            sum_v[...] += jnp.where(left, dv[0], dv[1])
+            sum_k[...] += jnp.where(left, dk[:patches], dk[patches:])
+            sum_v[...] += jnp.where(left, dv[:patches], dv[patches:])
     dk_ref[...] = (sum_k[...] * SCALE).astype(BF)
     dv_ref[...] = sum_v[...].astype(BF)
 
@@ -1478,7 +1476,7 @@
         scalars, row_valid, visual, patch_other, gains, w_vqkv, w_xkv, form, [q_own]
     )
     att = window_forward(qkv, window, [])
-    cot_sent, cot_q_sent = pack_two(scalars, cot, query_cot, [att])
+    cot_sent, cot_q_sent = pack_two(scalars, cot, query_cot, [att, *qs])
     cot_other, cot_theirs = from_ahead(cot_sent, count, 1), from_partner(cot_q_sent, count)
     q_out = query_forward(qs, cross, slot_kv, key_bias, same, blocks, [cot_q_sent])
     out_parts = give_back(q_out)
@@ -1522,13 +1520,7 @@
         scalars, dqs, dsks, dsvs, normed_three, x_query, grad_q, gains, w_qqkv, gain_rows, pages, tiled, got if tiled else []
     )
 
-    def put(array, other):
-        return lax.dynamic_update_index_in_dim(array, other.astype(array.dtype), down, 0)
-
-    shape = (pages, strip_rows, columns, width)
-    visual_out = put(vis_own, vis_came).reshape(shape)
     vin_came = from_ahead(vin_other, count, -1)
-    query_out_rows = put(q_res, res_came)
     qin_came = from_partner(qin_other, count)
 
     weights = (w_vqkv, w_vout, w_up, w_down, w_qqkv, w_xkv, w_qout, w_qup, w_qdown)
@@ -1568,8 +1560,11 @@
         parts = [scattered(g) for g in (g_vqkv, g_vout, g_up, g_down, g_qqkv, g_xkv[0], g_qout, g_qup, g_qdown)]
         gain_part = lax.psum_scatter(gain_grads[:4], "page", scatter_dimension=0, tiled=True)
         gain_part = lax.psum_scatter(gain_part, "strip", scatter_dimension=1, tiled=True).reshape(-1, 1)
-    visual_in_grad, query_in_grad = put_two(scalars, vin_own, qin_own, vin_came, qin_came, [last])
-    visual_in_grad = visual_in_grad.reshape(shape)
+    visual_out, query_out_rows, visual_in_grad, query_in_grad = put(
+        scalars, [vis_own, q_res, vin_own, qin_own], [vis_came, res_came, vin_came, qin_came], [last]
+    )
+    shape = (pages, strip_rows, columns, width)
+    visual_out, visual_in_grad = visual_out.reshape(shape), visual_in_grad.reshape(shape)
     return (visual_out, query_out_rows, visual_in_grad, query_in_grad, gain_part, *parts)
 
 

time: 458 us -> 453 us (0.989)
  Pallas kernels: 372 us -> 366 us
  waiting for transfers between devices: 18.6 us -> 24.4 us
    pallas_call x17, Pallas kernels: 277 us -> 269 us  [call(): pl.pallas_call(body, grid_spec=pltpu.PrefetchScalarGridSpec(num_scalar_pr...]
    ppermute x19, starting transfers between devices: 38.5 us -> 31 us  [from_ahead(): lax.ppermute(array, 'strip', [(i, (i - distance) % count) for i in range(...]
    ppermute x4, starting transfers between devices: 3.43 us -> 8.19 us  [from_partner(): return lax.ppermute(array, 'strip', [(i, i ^ 1) for i in range(count)])]
  transfers between devices with their start and end apart: 29 -> 29, of which waited for: 3 -> 5; matrix products, arithmetic and copies ran while one was open for 1% -> 0% of each run, Pallas kernels for 81% -> 80%
where the time goes in v2:
time: 453 us; the launch traced here: 444 us
  Pallas kernels  366 us (81%)
  starting transfers between devices  48 us (11%)
  waiting for transfers between devices  24.4 us (5%)
    pallas_call x17, Pallas kernels, call(): pl.pallas_call(body, grid_spec=pltpu.PrefetchScalarGridSpec(num_scalar_pr...  269 us
    pallas_call x1, Pallas kernels, late_sum(): pl.pallas_call(lambda *refs: kernel(*refs[:first], *refs[first + len(deps...  70.1 us
    ppermute x19, starting transfers between devices, from_ahead(): lax.ppermute(array, 'strip', [(i, (i - distance) % count) for i in range(...  31 us
    pallas_call x1, Pallas kernels, query_sum(): pl.pallas_call(lambda *refs: kernel(*refs[:9], *refs[9 + len(deps):]), in...  23.1 us
    ppermute x19, waiting for transfers between devices, from_ahead(): lax.ppermute(array, 'strip', [(i, (i - distance) % count) for i in range(...  13.3 us
  transfers between devices with their start and end apart: 29, of which 5 were waited for; matrix products, arithmetic and copies ran while one was open for 0% of the time, Pallas kernels for 80%

profile of v2, /device:TPU:0, one launch (start us, length us, event | category | flops | bytes accessed | tf_op | source)
XLA Modules:
  0.0 443.8 jit_solution(15084599293601745868)
XLA Ops:
  2.0 1.2 dynamic_slice.4
  3.3 1.2 stack.33.refs_0_
  4.5 3.0 pack.1
  7.5 3.0 collective-permute-start
  10.5 5.7 %collective-permute-done.refs_1_.refs_4_ = bf16[144,768]{1,0:T(8,128)(2,1)} collective-permute-done((bf16[144,768]{1,0:T(8,128)(2,1)}, bf16[144,768]{1,0:T(8,128)(2,1)}, u32[]{:S(2)}, u32[]{:S(2)}) %collective-permute-start) | collective-permute-done | bytes 221216 | tf_op jit(solution)/shard_map/ppermute | solution.py:1420
  16.2 4.8 %collective-permute-start.1 = (bf16[592,768]{1,0:T(8,128)(2,1)}, bf16[592,768]{1,0:T(8,128)(2,1)}, u32[]{:S(2)}, u32[]{:S(2)}) collective-permute-start(bf16[592,768]{1,0:T(8,128)(2,1)} %held_back.1.refs_7_), channel_id=1, source_target_pairs={{0,7},{1,0},{2,1},{3,2},{4,3},{5,4},{6,5},{7,6},{8,15},{9,8},{10,9... | collective-permute-start | bytes 2727944 | tf_op jit(solution)/shard_map/ppermute | solution.py:1416
  21.0 0.6 pad.4.refs_5_.refs_4_.refs_8_.refs_10_.refs_16_
  21.6 5.1 %query_in.1 = (bf16[256,768]{1,0:T(8,128)(2,1)}, bf16[256,768]{1,0:T(8,128)(2,1)}, bf16[256,768]{1,0:T(8,128)(2,1)}, bf16[256,1536]{1,0:T(8,128)(2,1)}, bf16[320...) custom-call(s32[9]{0:T(128)} %stack.33.refs_0_, s32[2,1024]{1,0:T(2,128)} %refs_1_.4, s32[2,128]{1,0:T(2,128)} %refs_2_.5, ...), custom_call_target="tpu_custom_call" | custom-call | flops 2717908992 | bytes 5000000 | tf_op jit(solution)/shard_map/query_in/pallas_call | solution.py:103
  26.7 0.0 collective-permute-start.4
  26.7 0.8 collective-permute-start.3
  27.5 1.3 collective-permute-start.2
  28.8 13.2 %collective-permute-done.1.refs_3_ = bf16[592,768]{1,0:T(8,128)(2,1)} collective-permute-done((bf16[592,768]{1,0:T(8,128)(2,1)}, bf16[592,768]{1,0:T(8,128)(2,1)}, u32[]{:S(2)}, u32[]{:S(2)}) %collective-permute-start.1) | collective-permute-done | bytes 909344 | tf_op jit(solution)/shard_map/ppermute | solution.py:1416
  42.0 16.1 %patch_in.1 = (bf16[1152,768]{1,0:T(8,128)(2,1)}, bf16[1152,768]{1,0:T(8,128)(2,1)}, bf16[1152,2304]{1,0:T(8,128)(2,1)}, bf16[1152,1536]{1,0:T(8,128)(2,1)}, bf16[1152,128]{1,0:T(8,128)(2,1)}) custom-call(s32[9]{0:T(128)} %stack.33.refs_0_, s32[2,6]{1,0:T(2,128)} %refs_1_.5, bf16[2,576,768]{2,1,0:T(8,128)(2,1)} %bitcast.38, ...), custom_call_target="tpu_custom_call" | custom-call | flops 20384317440 | bytes 20000000 | tf_op jit(solution)/shard_map/patch_in/pallas_call | solution.py:103
  58.1 10.6 %window_forward.1.refs_3_.refs_1_ = bf16[1152,768]{1,0:T(8,128)(2,1)} custom-call(bf16[1152,2304]{1,0:T(8,128)(2,1)} %get-tuple-element.111.refs_0_), custom_call_target="tpu_custom_call" | custom-call | flops 6115295232 | bytes 8000000 | tf_op jit(solution)/shard_map/window_forward/pallas_call | solution.py:103
  68.7 0.0 collective-permute-done.4.refs_7_.refs_3_
  68.8 2.9 pack_two.1
  71.6 1.6 collective-permute-start.9
  73.3 3.6 collective-permute-start.5
  76.9 28.2 %query_forward.1 = (bf16[256,896]{1,0:T(8,128)(2,1)}, bf16[256,896]{1,0:T(8,128)(2,1)}, bf16[256,896]{1,0:T(8,128)(2,1)}, bf16[256,896]{1,0:T(8,128)(2,1)}) custom-call(bf16[256,768]{1,0:T(8,128)(2,1)} %collective-permute-done.2.refs_4_.refs_0_, bf16[256,768]{1,0:T(8,128)(2,1)} %get-tuple-element.110.refs_7_.refs_5_.refs_1_, ...), custom_call_target="tpu_custom_call" | custom-call | flops 43486543872 | bytes 10000000 | tf_op jit(solution)/shard_map/query_forward/pallas_call | solution.py:103
  105.1 4.0 collective-permute-start.7
  109.1 2.5 collective-permute-start.8
  111.6 1.3 collective-permute-start.6
  112.9 0.0 collective-permute-done.5.refs_4_
  112.9 56.0 %patch_ffn.1 = (bf16[2,576,768]{2,1,0:T(8,128)(2,1)}, bf16[576,768]{1,0:T(8,128)(2,1)}, f32[1152,768]{1,0:T(8,128)}, bf16[1152,768]{1,0:T(8,128)(2,1)}, bf16[2,2...) custom-call(s32[9]{0:T(128)} %stack.33.refs_0_, ...), custom_call_target="tpu_custom_call" | custom-call | flops 97844723712 | bytes 40000000 | tf_op jit(solution)/shard_map/patch_ffn/pallas_call | solution.py:103
  168.9 0.7 collective-permute-start.10
  169.6 0.0 collective-permute-done.9.refs_7_
  169.6 0.0 collective-permute-done.7.refs_3_
  169.6 0.0 collective-permute-done.8.refs_4_
  169.6 0.0 collective-permute-done.6.refs_1_
  169.6 17.0 %query_ffn.1 = (bf16[2,128,768]{2,1,0:T(8,128)(2,1)}, bf16[128,768]{1,0:T(8,128)(2,1)}, f32[256,768]{1,0:T(8,128)}, bf16[256,896]{1,0:T(8,128)(2,1)}, bf16[256,7...) custom-call(s32[9]{0:T(128)} %stack.33.refs_0_, ...), custom_call_target="tpu_custom_call" | custom-call | flops 14495514624 | bytes 20000000 | tf_op jit(solution)/shard_map/query_ffn/pallas_call | solution.py:103
  186.6 1.6 collective-permute-start.14
  188.2 0.4 collective-permute-start.13
  188.6 2.7 collective-permute-start.12
  191.3 0.6 collective-permute-start.11
  191.8 23.1 %query_sum.1 = (bf16[2,4,1296,128]{3,2,1,0:T(8,128)(2,1)}, bf16[2,4,1296,128]{3,2,1,0:T(8,128)(2,1)}, bf16[2,4,1296,128]{3,2,1,0:T(8,128)(2,1)}, bf16[2,4,1296,128]{3,2,1,0:T(8,128)(2,1)}) custom-call(bf16[2,2,2,4,576,128]{5,4,3,2,1,0:T(8,128)(2,1)} %get-tuple-element.128.refs_0_, bf16[2,2,2,4,576,128]{5,4,3,2,1,0:T(8,128)(2,1)} %get-tuple-element.129.refs_1_, ...), custom_call_target="tpu_custom_call" | custom-call | tf_op jit(solution)/shard_map/query_sum/pallas_call | solution.py:1195
  214.9 0.0 collective-permute-done.14.refs_19_.refs_6_
  215.0 0.1 collective-permute-start.15
  215.1 0.0 collective-permute-done.10.refs_3_.refs_5_
  215.1 1.5 collective-permute-start.16
  216.6 24.5 %window_backward.1.refs_18_.refs_1_ = bf16[1152,2304]{1,0:T(8,128)(2,1)} custom-call(bf16[1152,2304]{1,0:T(8,128)(2,1)} %get-tuple-element.111.refs_0_, bf16[1152,768]{1,0:T(8,128)(2,1)} %get-tuple-element.127.refs_1_, bf16[8,1296,128]{2,1,0:T(8,128)(2,1)} %bitcast.26, bf16[576,768]{1,0:T(8,128)(2,1)} %collective-permute-done.10.refs_3_.refs_5_), custom_call_target="tpu_custom_call" | custom-call | flops 15288238080 | bytes 13000000 | tf_op jit(solution)/shard_map/window_backward/pallas_call | solution.py:103
  241.1 0.0 collective-permute-done.11.refs_4_.refs_8_
  241.2 25.6 %query_backward.2 = (bf16[256,384]{1,0:T(8,128)(2,1)}, bf16[256,384]{1,0:T(8,128)(2,1)}, bf16[256,384]{1,0:T(8,128)(2,1)}, bf16[256,384]{1,0:T(8,128)(2,1)}, bf1...) custom-call(bf16[256,768]{1,0:T(8,128)(2,1)} %collective-permute-done.2, ...), custom_call_target="tpu_custom_call" | custom-call | flops 27179089920 | bytes 15000000 | tf_op jit(solution)/shard_map/query_backward/pallas_call | solution.py:103
  266.8 3.4 collective-permute-start.19
  270.2 0.6 collective-permute-start.21
  270.8 4.2 collective-permute-done.15.refs_2_.refs_4_
  274.9 0.1 collective-permute-done.16.refs_6_.refs_8_
  275.0 7.8 %halve_add.2 = (bf16[4,1296,128]{2,1,0:T(8,128)(2,1)}, bf16[4,1296,128]{2,1,0:T(8,128)(2,1)}, bf16[4,1296,128]{2,1,0:T(8,128)(2,1)}, bf16[4,1296,128]{2,1,0:T(8,128)(2,1)}) custom-call(s32[9]{0:T(128)} %stack.33.refs_0_, bf16[8,1296,128]{2,1,0:T(8,128)(2,1)} %bitcast.27, bf16[8,1296,128]{2,1,0:T(8,128)(2,1)} %collective-permute-done.15.refs_2_.refs_4_, ...), custom_call_target="tpu_custom_call" | custom-call | flops 3000000 | bytes 15925248 | tf_op jit(solution)/shard_map/halve_add/pallas_call | solution.py:103
  282.9 1.5 collective-permute-start.17
  284.4 1.7 collective-permute-start.18
  286.1 25.5 %query_backward.3 = (bf16[256,384]{1,0:T(8,128)(2,1)}, bf16[256,384]{1,0:T(8,128)(2,1)}, bf16[256,384]{1,0:T(8,128)(2,1)}, bf16[256,384]{1,0:T(8,128)(2,1)}, bf1...) custom-call(bf16[256,768]{1,0:T(8,128)(2,1)} %collective-permute-done.2, ...), custom_call_target="tpu_custom_call" | custom-call | flops 27179089920 | bytes 15000000 | tf_op jit(solution)/shard_map/query_backward/pallas_call | solution.py:103
  311.6 3.3 collective-permute-start.22
  314.9 0.0 collective-permute-start.23
  314.9 0.6 collective-permute-start.24
  315.5 4.5 %halve_add.3 = (bf16[2,1296,128]{2,1,0:T(8,128)(2,1)}, bf16[2,1296,128]{2,1,0:T(8,128)(2,1)}, bf16[2,1296,128]{2,1,0:T(8,128)(2,1)}, bf16[2,1296,128]{2,1,0:T(8,128)(2,1)}) custom-call(s32[9]{0:T(128)} %stack.33.refs_0_, bf16[4,1296,128]{2,1,0:T(8,128)(2,1)} %get-tuple-element.146.refs_18_.refs_1_.refs_3_, ...), custom_call_target="tpu_custom_call" | custom-call | flops 3000000 | bytes 7962624 | tf_op jit(solution)/shard_map/halve_add/pallas_call | solution.py:103
  320.0 3.8 collective-permute-start.25
  323.8 0.1 collective-permute-start.26
  323.9 29.9 %patch_back.1 = (f32[2,576,768]{2,1,0:T(8,128)}, bf16[576,768]{1,0:T(8,128)(2,1)}, f32[8,768]{1,0:T(8,128)}, bf16[2,2,2,4,432,128]{5,4,3,2,1,0:T(8,128)(2,1)}, b...) custom-call(s32[9]{0:T(128)} %stack.33.refs_0_, ...), custom_call_target="tpu_custom_call" | custom-call | flops 40768634880 | bytes 40000000 | tf_op jit(solution)/shard_map/patch_back/pallas_call | solution.py:103
  353.8 0.4 collective-permute-start.27
  354.3 1.1 collective-permute-done.26.refs_20_.refs_8_
  355.4 8.6 %query_out.1 = (f32[2,128,768]{2,1,0:T(8,128)}, bf16[128,768]{1,0:T(8,128)(2,1)}, bf16[2,2,2,4,432,128]{5,4,3,2,1,0:T(8,128)(2,1)}, bf16[2,2,2,4,48,128]{5,4,3,2,1,0:T(8,128)(2,1)}) custom-call(s32[9]{0:T(128)} %stack.33.refs_0_, bf16[256,384]{1,0:T(8,128)(2,1)} %collective-permute-done.19.refs_10_.refs_1_, ...), custom_call_target="tpu_custom_call" | custom-call | flops 5435817984 | bytes 10000000 | tf_op jit(solution)/shard_map/query_out/pallas_call | solution.py:103
  364.0 2.0 collective-permute-start.28
  365.9 70.1 %late_sum.1 = (bf16[1920,128]{1,0:T(8,128)(2,1)}, bf16[1872,128]{1,0:T(8,128)(2,1)}, bf16[1920,128]{1,0:T(8,128)(2,1)}, bf16[1872,128]{1,0:T(8,128)(2,1)}) custom-call(bf16[2,16,432,128]{3,2,1,0:T(8,128)(2,1)} %bitcast.32, bf16[2,16,144,128]{3,2,1,0:T(8,128)(2,1)} %bitcast.39, bf16[2,16,48,128]{3,2,1,0:T(8,128)(2,1)} %bitcast.41, ...), custom_call_target="tpu_custom_call" | custom-call | tf_op jit(solution)/shard_map/late_sum/pallas_call | solution.py:1337
  436.0 3.6 finish.1
  439.6 3.9 put.1
  (19 shorter events, 0.0 us)
Async XLA Ops:
  0.6 20.3 %copy-start = (f32[768,4]{0,1:T(4,128)S(1)}, f32[768,4]{0,1:T(4,128)}, u32[]{:S(2)}) copy-start(f32[768,4]{0,1:T(4,128)} %param.26) | copy-start | bytes 36868
  7.5 8.7 %collective-permute-start = (bf16[144,768]{1,0:T(8,128)(2,1)}, bf16[144,768]{1,0:T(8,128)(2,1)}, u32[]{:S(2)}, u32[]{:S(2)}) collective-permute-start(bf16[144,768]{1,0:T(8,128)(2,1)} %get-tuple-element.109), channel_id=1, source_target_pairs={{0,1},{1,0},{2,3},{3,2},{4,5},{5,4},{6,7},{7,6},{8,9},{9,8},{10,11... | collective-permute-start | bytes 663560 | tf_op jit(solution)/shard_map/ppermute | solution.py:1420
  16.2 25.8 %collective-permute-start.1 = (bf16[592,768]{1,0:T(8,128)(2,1)}, bf16[592,768]{1,0:T(8,128)(2,1)}, u32[]{:S(2)}, u32[]{:S(2)}) collective-permute-start(bf16[592,768]{1,0:T(8,128)(2,1)} %held_back.1.refs_7_), channel_id=1, source_target_pairs={{0,7},{1,0},{2,1},{3,2},{4,3},{5,4},{6,5},{7,6},{8,15},{9,8},{10,9... | collective-permute-start | bytes 2727944 | tf_op jit(solution)/shard_map/ppermute | solution.py:1416
  26.7 42.1 %collective-permute-start.4 = (bf16[256,768]{1,0:T(8,128)(2,1)}, bf16[256,768]{1,0:T(8,128)(2,1)}, u32[]{:S(2)}, u32[]{:S(2)}) collective-permute-start(bf16[256,768]{1,0:T(8,128)(2,1)} %get-tuple-element.110.refs_7_.refs_5_.refs_1_), channel_id=1, source_target_pairs={{0,4},{1,5},{2,6},{3,7},{4,0},{5,1},{6,2},{7,3},{8,12},{9,13},{10,... | collective-permute-start | bytes 1179656 | tf_op jit(solution)/shard_map/ppermute | solution.py:1416
  26.7 42.1 %collective-permute-start.3 = (bf16[256,768]{1,0:T(8,128)(2,1)}, bf16[256,768]{1,0:T(8,128)(2,1)}, u32[]{:S(2)}, u32[]{:S(2)}) collective-permute-start(bf16[256,768]{1,0:T(8,128)(2,1)} %get-tuple-element.110.refs_7_.refs_5_.refs_1_), channel_id=1, source_target_pairs={{0,6},{1,7},{2,0},{3,1},{4,2},{5,3},{6,4},{7,5},{8,14},{9,15},{10,... | collective-permute-start | bytes 1179656 | tf_op jit(solution)/shard_map/ppermute | solution.py:1416
  27.5 41.3 %collective-permute-start.2 = (bf16[256,768]{1,0:T(8,128)(2,1)}, bf16[256,768]{1,0:T(8,128)(2,1)}, u32[]{:S(2)}, u32[]{:S(2)}) collective-permute-start(bf16[256,768]{1,0:T(8,128)(2,1)} %get-tuple-element.110.refs_7_.refs_5_.refs_1_), channel_id=1, source_target_pairs={{0,2},{1,3},{2,4},{3,5},{4,6},{5,7},{6,0},{7,1},{8,10},{9,11},{10,... | collective-permute-start | bytes 1179656 | tf_op jit(solution)/shard_map/ppermute | solution.py:1416
  71.6 97.9 %collective-permute-start.9 = (bf16[128,768]{1,0:T(8,128)(2,1)}, bf16[128,768]{1,0:T(8,128)(2,1)}, u32[]{:S(2)}, u32[]{:S(2)}) collective-permute-start(bf16[128,768]{1,0:T(8,128)(2,1)} %get-tuple-element.118.refs_10_), channel_id=1, source_target_pairs={{0,1},{1,0},{2,3},{3,2},{4,5},{5,4},{6,7},{7,6},{8,9},{9,8},{10,11... | collective-permute-start | bytes 589832 | tf_op jit(solution)/shard_map/ppermute | solution.py:1420
  73.3 39.6 %collective-permute-start.5 = (bf16[576,768]{1,0:T(8,128)(2,1)}, bf16[576,768]{1,0:T(8,128)(2,1)}, u32[]{:S(2)}, u32[]{:S(2)}) collective-permute-start(bf16[576,768]{1,0:T(8,128)(2,1)} %get-tuple-element.113), channel_id=1, source_target_pairs={{0,7},{1,0},{2,1},{3,2},{4,3},{5,4},{6,5},{7,6},{8,15},{9,8},{10,9... | collective-permute-start | bytes 2654216 | tf_op jit(solution)/shard_map/ppermute | solution.py:1416
  105.1 64.5 %collective-permute-start.7 = (bf16[256,896]{1,0:T(8,128)(2,1)}, bf16[256,896]{1,0:T(8,128)(2,1)}, u32[]{:S(2)}, u32[]{:S(2)}) collective-permute-start(bf16[256,896]{1,0:T(8,128)(2,1)} %get-tuple-element.122), channel_id=1, source_target_pairs={{0,2},{1,3},{2,4},{3,5},{4,6},{5,7},{6,0},{7,1},{8,10},{9,11},{10,... | collective-permute-start | bytes 1376264 | tf_op jit(solution)/shard_map/ppermute | solution.py:1416
  109.1 60.5 %collective-permute-start.8 = (bf16[256,896]{1,0:T(8,128)(2,1)}, bf16[256,896]{1,0:T(8,128)(2,1)}, u32[]{:S(2)}, u32[]{:S(2)}) collective-permute-start(bf16[256,896]{1,0:T(8,128)(2,1)} %get-tuple-element.123), channel_id=1, source_target_pairs={{0,4},{1,5},{2,6},{3,7},{4,0},{5,1},{6,2},{7,3},{8,12},{9,13},{10,... | collective-permute-start | bytes 1376264 | tf_op jit(solution)/shard_map/ppermute | solution.py:1416
  111.6 58.0 %collective-permute-start.6 = (bf16[256,896]{1,0:T(8,128)(2,1)}, bf16[256,896]{1,0:T(8,128)(2,1)}, u32[]{:S(2)}, u32[]{:S(2)}) collective-permute-start(bf16[256,896]{1,0:T(8,128)(2,1)} %get-tuple-element.119.refs_9_), channel_id=1, source_target_pairs={{0,6},{1,7},{2,0},{3,1},{4,2},{5,3},{6,4},{7,5},{8,14},{9,15},{10,... | collective-permute-start | bytes 1376264 | tf_op jit(solution)/shard_map/ppermute | solution.py:1416
  168.9 46.2 %collective-permute-start.10 = (bf16[576,768]{1,0:T(8,128)(2,1)}, bf16[576,768]{1,0:T(8,128)(2,1)}, u32[]{:S(2)}, u32[]{:S(2)}) collective-permute-start(bf16[576,768]{1,0:T(8,128)(2,1)} %get-tuple-element.138), channel_id=1, source_target_pairs={{0,1},{1,2},{2,3},{3,4},{4,5},{5,6},{6,7},{7,0},{8,9},{9,10},{10,1... | collective-permute-start | bytes 2654216 | tf_op jit(solution)/shard_map/ppermute | solution.py:1416
  186.6 28.4 %collective-permute-start.14 = (bf16[128,768]{1,0:T(8,128)(2,1)}, bf16[128,768]{1,0:T(8,128)(2,1)}, u32[]{:S(2)}, u32[]{:S(2)}) collective-permute-start(bf16[128,768]{1,0:T(8,128)(2,1)} %get-tuple-element.141), channel_id=1, source_target_pairs={{0,1},{1,0},{2,3},{3,2},{4,5},{5,4},{6,7},{7,6},{8,9},{9,8},{10,11... | collective-permute-start | bytes 589832 | tf_op jit(solution)/shard_map/ppermute | solution.py:1420
  188.2 53.0 %collective-permute-start.13 = (bf16[256,896]{1,0:T(8,128)(2,1)}, bf16[256,896]{1,0:T(8,128)(2,1)}, u32[]{:S(2)}, u32[]{:S(2)}) collective-permute-start(bf16[256,896]{1,0:T(8,128)(2,1)} %get-tuple-element.139.refs_5_.refs_9_), channel_id=1, source_target_pairs={{0,4},{1,5},{2,6},{3,7},{4,0},{5,1},{6,2},{7,3},{8,12},{9,13},{10,... | collective-permute-start | bytes 1376264 | tf_op jit(solution)/shard_map/ppermute | solution.py:1416
  188.6 52.6 %collective-permute-start.12 = (bf16[256,896]{1,0:T(8,128)(2,1)}, bf16[256,896]{1,0:T(8,128)(2,1)}, u32[]{:S(2)}, u32[]{:S(2)}) collective-permute-start(bf16[256,896]{1,0:T(8,128)(2,1)} %get-tuple-element.139.refs_5_.refs_9_), channel_id=1, source_target_pairs={{0,6},{1,7},{2,0},{3,1},{4,2},{5,3},{6,4},{7,5},{8,14},{9,15},{10,... | collective-permute-start | bytes 1376264 | tf_op jit(solution)/shard_map/ppermute | solution.py:1416
  191.3 49.9 %collective-permute-start.11 = (bf16[256,896]{1,0:T(8,128)(2,1)}, bf16[256,896]{1,0:T(8,128)(2,1)}, u32[]{:S(2)}, u32[]{:S(2)}) collective-permute-start(bf16[256,896]{1,0:T(8,128)(2,1)} %get-tuple-element.139.refs_5_.refs_9_), channel_id=1, source_target_pairs={{0,2},{1,3},{2,4},{3,5},{4,6},{5,7},{6,0},{7,1},{8,10},{9,11},{10,... | collective-permute-start | bytes 1376264 | tf_op jit(solution)/shard_map/ppermute | solution.py:1416
  215.0 60.0 %collective-permute-start.15 = (bf16[8,1296,128]{2,1,0:T(8,128)(2,1)}, bf16[8,1296,128]{2,1,0:T(8,128)(2,1)}, u32[]{:S(2)}, u32[]{:S(2)}) collective-permute-start(bf16[8,1296,128]{2,1,0:T(8,128)(2,1)} %bitcast.46), channel_id=1, source_target_pairs={{0,1},{1,0},{2,3},{3,2},{4,5},{5,4},{6,7},{7,6},{8,9},{9,8},{10,11... | collective-permute-start | bytes 7962632 | tf_op jit(solution)/shard_map/ppermute | solution.py:1219
  215.1 59.9 %collective-permute-start.16 = (bf16[8,1296,128]{2,1,0:T(8,128)(2,1)}, bf16[8,1296,128]{2,1,0:T(8,128)(2,1)}, u32[]{:S(2)}, u32[]{:S(2)}) collective-permute-start(bf16[8,1296,128]{2,1,0:T(8,128)(2,1)} %bitcast.45), channel_id=1, source_target_pairs={{0,16},{8,24},{16,0},{24,8},{1,17},{9,25},{17,1},{25,9},{2,18},{10... | collective-permute-start | bytes 7962632 | tf_op jit(solution)/shard_map/ppermute | solution.py:1219
  266.8 44.8 %collective-permute-start.19 = (bf16[256,384]{1,0:T(8,128)(2,1)}, bf16[256,384]{1,0:T(8,128)(2,1)}, u32[]{:S(2)}, u32[]{:S(2)}) collective-permute-start(bf16[256,384]{1,0:T(8,128)(2,1)} %get-tuple-element.156), channel_id=1, source_target_pairs={{0,6},{1,7},{2,0},{3,1},{4,2},{5,3},{6,4},{7,5},{8,14},{9,15},{10,... | collective-permute-start | bytes 589832 | tf_op jit(solution)/shard_map/ppermute | solution.py:1416
  270.2 44.7 %collective-permute-start.20 = (bf16[256,384]{1,0:T(8,128)(2,1)}, bf16[256,384]{1,0:T(8,128)(2,1)}, u32[]{:S(2)}, u32[]{:S(2)}) collective-permute-start(bf16[256,384]{1,0:T(8,128)(2,1)} %get-tuple-element.158), channel_id=1, source_target_pairs={{0,2},{1,3},{2,4},{3,5},{4,6},{5,7},{6,0},{7,1},{8,10},{9,11},{10,... | collective-permute-start | bytes 589832 | tf_op jit(solution)/shard_map/ppermute | solution.py:1416
  270.2 44.7 %collective-permute-start.21 = (bf16[256,384]{1,0:T(8,128)(2,1)}, bf16[256,384]{1,0:T(8,128)(2,1)}, u32[]{:S(2)}, u32[]{:S(2)}) collective-permute-start(bf16[256,384]{1,0:T(8,128)(2,1)} %get-tuple-element.159), channel_id=1, source_target_pairs={{0,4},{1,5},{2,6},{3,7},{4,0},{5,1},{6,2},{7,3},{8,12},{9,13},{10,... | collective-permute-start | bytes 589832 | tf_op jit(solution)/shard_map/ppermute | solution.py:1416
  282.9 32.6 %collective-permute-start.17 = (bf16[4,1296,128]{2,1,0:T(8,128)(2,1)}, bf16[4,1296,128]{2,1,0:T(8,128)(2,1)}, u32[]{:S(2)}, u32[]{:S(2)}) collective-permute-start(bf16[4,1296,128]{2,1,0:T(8,128)(2,1)} %get-tuple-element.153), channel_id=1, source_target_pairs={{0,16},{8,24},{16,0},{24,8},{1,17},{9,25},{17,1},{25,9},{2,18},{10... | collective-permute-start | bytes 3981320 | tf_op jit(solution)/shard_map/ppermute | solution.py:1219
  284.4 31.1 %collective-permute-start.18 = (bf16[4,1296,128]{2,1,0:T(8,128)(2,1)}, bf16[4,1296,128]{2,1,0:T(8,128)(2,1)}, u32[]{:S(2)}, u32[]{:S(2)}) collective-permute-start(bf16[4,1296,128]{2,1,0:T(8,128)(2,1)} %get-tuple-element.155), channel_id=1, source_target_pairs={{0,1},{1,0},{2,3},{3,2},{4,5},{5,4},{6,7},{7,6},{8,9},{9,8},{10,11... | collective-permute-start | bytes 3981320 | tf_op jit(solution)/shard_map/ppermute | solution.py:1219
  311.6 42.3 %collective-permute-start.22 = (bf16[256,384]{1,0:T(8,128)(2,1)}, bf16[256,384]{1,0:T(8,128)(2,1)}, u32[]{:S(2)}, u32[]{:S(2)}) collective-permute-start(bf16[256,384]{1,0:T(8,128)(2,1)} %get-tuple-element.162), channel_id=1, source_target_pairs={{0,6},{1,7},{2,0},{3,1},{4,2},{5,3},{6,4},{7,5},{8,14},{9,15},{10,... | collective-permute-start | bytes 589832 | tf_op jit(solution)/shard_map/ppermute | solution.py:1416
  314.9 39.4 %collective-permute-start.23 = (bf16[256,384]{1,0:T(8,128)(2,1)}, bf16[256,384]{1,0:T(8,128)(2,1)}, u32[]{:S(2)}, u32[]{:S(2)}) collective-permute-start(bf16[256,384]{1,0:T(8,128)(2,1)} %get-tuple-element.164), channel_id=1, source_target_pairs={{0,2},{1,3},{2,4},{3,5},{4,6},{5,7},{6,0},{7,1},{8,10},{9,11},{10,... | collective-permute-start | bytes 589832 | tf_op jit(solution)/shard_map/ppermute | solution.py:1416
  314.9 39.4 %collective-permute-start.24 = (bf16[256,384]{1,0:T(8,128)(2,1)}, bf16[256,384]{1,0:T(8,128)(2,1)}, u32[]{:S(2)}, u32[]{:S(2)}) collective-permute-start(bf16[256,384]{1,0:T(8,128)(2,1)} %get-tuple-element.165), channel_id=1, source_target_pairs={{0,4},{1,5},{2,6},{3,7},{4,0},{5,1},{6,2},{7,3},{8,12},{9,13},{10,... | collective-permute-start | bytes 589832 | tf_op jit(solution)/shard_map/ppermute | solution.py:1416
  320.0 34.3 %collective-permute-start.25 = (bf16[2,1296,128]{2,1,0:T(8,128)(2,1)}, bf16[2,1296,128]{2,1,0:T(8,128)(2,1)}, u32[]{:S(2)}, u32[]{:S(2)}) collective-permute-start(bf16[2,1296,128]{2,1,0:T(8,128)(2,1)} %get-tuple-element.173), channel_id=1, source_target_pairs={{0,2},{1,3},{2,0},{3,1},{4,6},{5,7},{6,4},{7,5},{8,10},{9,11},{10,... | collective-permute-start | bytes 1990664 | tf_op jit(solution)/shard_map/ppermute | solution.py:1219
  323.8 31.6 %collective-permute-start.26 = (bf16[2,1296,128]{2,1,0:T(8,128)(2,1)}, bf16[2,1296,128]{2,1,0:T(8,128)(2,1)}, u32[]{:S(2)}, u32[]{:S(2)}) collective-permute-start(bf16[2,1296,128]{2,1,0:T(8,128)(2,1)} %get-tuple-element.174), channel_id=1, source_target_pairs={{0,2},{1,3},{2,0},{3,1},{4,6},{5,7},{6,4},{7,5},{8,10},{9,11},{10,... | collective-permute-start | bytes 1990664 | tf_op jit(solution)/shard_map/ppermute | solution.py:1219
  353.8 85.8 %collective-permute-start.27 = (bf16[576,768]{1,0:T(8,128)(2,1)}, bf16[576,768]{1,0:T(8,128)(2,1)}, u32[]{:S(2)}, u32[]{:S(2)}) collective-permute-start(bf16[576,768]{1,0:T(8,128)(2,1)} %get-tuple-element.176), channel_id=1, source_target_pairs={{0,1},{1,2},{2,3},{3,4},{4,5},{5,6},{6,7},{7,0},{8,9},{9,10},{10,1... | collective-permute-start | bytes 2654216 | tf_op jit(solution)/shard_map/ppermute | solution.py:1416
  364.0 75.7 %collective-permute-start.28 = (bf16[128,768]{1,0:T(8,128)(2,1)}, bf16[128,768]{1,0:T(8,128)(2,1)}, u32[]{:S(2)}, u32[]{:S(2)}) collective-permute-start(bf16[128,768]{1,0:T(8,128)(2,1)} %get-tuple-element.177), channel_id=1, source_target_pairs={{0,1},{1,0},{2,3},{3,2},{4,5},{5,4},{6,7},{7,6},{8,9},{9,8},{10,11... | collective-permute-start | bytes 589832 | tf_op jit(solution)/shard_map/ppermute | solution.py:1420

commit v3 on v2

--- a/solution.py
+++ b/solution.py
@@ -1274,15 +1274,7 @@
         copy = pltpu.make_async_copy(early[k], loaded[k], near.at[next(local_numbers)])
         copy.start()
         loads.append(copy)
-    for copy in loads:
-        copy.wait()
     early_flights = []
-    for order in range(2):
-        bit, mate = orders[order][3]
-        kept = loaded[2 * order]
-        add_rows(kept, 1 - bit, loaded[2 * order + 1], 1 - bit, 1, 0, early_rows)
-        early_flights.append(send(kept.at[1 - bit], early_held[order], remote, next(numbers), mate))
-        add_rows(kept, bit, loaded[2 * order + 1], bit, 1, 0, early_rows)
     bases = [0] * len(jobs)
     flights = [None] * len(jobs)
     first_exchange = []
@@ -1305,6 +1297,15 @@
             )
             add_rows(sums[order], base + keep, source, keep, size, at, rows)
             bases[n] = base + keep
+        if stage == 0:
+            for copy in loads:
+                copy.wait()
+            for order in range(2):
+                bit, mate = orders[order][3]
+                kept = loaded[2 * order]
+                add_rows(kept, 1 - bit, loaded[2 * order + 1], 1 - bit, 1, 0, early_rows)
+                early_flights.append(send(kept.at[1 - bit], early_held[order], remote, next(numbers), mate))
+                add_rows(kept, bit, loaded[2 * order + 1], bit, 1, 0, early_rows)
         if stage == 2:
             for order in range(2):
                 early_flights[order].wait()
@@ -1355,8 +1356,12 @@
     )(*grads, *early, *deps)
 
 
-def finish_kernel(core_ref, own0, own1, got0, got1, gain_ref, *outs, plan):
-    first = core_ref[0] == 0
+def finish_kernel(s_ref, own0, own1, got0, got1, *refs, plan, puts):
+    came, gain_ref = refs[puts : 2 * puts], refs[2 * puts]
+    outs, put_outs = refs[2 * puts + 1 : 2 * puts + 1 + len(plan)], refs[2 * puts + 1 + len(plan) :]
+    for c, out in zip(came, put_outs):
+        out[0] = c[...].astype(out.dtype)
+    first = s_ref[CORE] == 0
     owns, gots = (own0, own1), (got0, got1)
     lane = iota((1, LANES), 1)
     left = lane < 64
@@ -1398,18 +1403,20 @@
     gain_ref[...] = jnp.where(first, gain[0:1], gain[1:2])
 
 
-def finish(core, shares, shapes, plan, gain_rows):
-    vmem = pl.BlockSpec(memory_space=pltpu.VMEM)
+def finish(scalars, shares, shapes, plan, gain_rows, arrays, came):
     outs = [shape[::-1] if flipped else shape for shape, (_, _, flipped) in zip(shapes, plan)]
-    gain, *found = pl.pallas_call(
-        functools.partial(finish_kernel, plan=plan),
-        in_specs=[pl.BlockSpec(memory_space=pltpu.SMEM)] + [vmem] * 4,
-        out_specs=[vmem] * (1 + len(outs)),
-        out_shape=[sds((1, gain_rows), F32)] + [sds(shape, F32) for shape in outs],
-        compiler_params=pltpu.CompilerParams(vmem_limit_bytes=VMEM_BYTES),
-        name="finish",
-    )(core, *shares)
-    return gain.T, *[f.T if flipped else f for f, (_, _, flipped) in zip(found, plan)]
+    gain, *found = call(
+        functools.partial(finish_kernel, plan=plan, puts=len(arrays)),
+        "finish",
+        [(a, whole(a.shape)) for a in shares] + [(a, ANY) for a in arrays] + [(c, whole(c.shape)) for c in came],
+        [((1, gain_rows), F32, whole((1, gain_rows)))]
+        + [(shape, F32, whole(shape)) for shape in outs]
+        + [(a.shape, a.dtype, other_page(a.shape)) for a in arrays],
+        scalars=scalars,
+        aliases={1 + len(shares) + k: 1 + len(outs) + k for k in range(len(arrays))},
+    )
+    weights = [f.T if flipped else f for f, (_, _, flipped) in zip(found, plan)]
+    return gain.T, weights, found[len(outs) :]
 
 
 def from_ahead(array, count, distance):
@@ -1446,7 +1453,8 @@
     up = jnp.where(odd == 1, 1 - row_shifted[0], row_shifted[0])
     down = 1 - up
     pick = lambda array, which: lax.dynamic_index_in_dim(array, which, 0, keepdims=False)
-    scalars = jnp.stack([up, pick(col_shift, up), odd, page % 2, page // 2, odd, place // 2 % 2, place // 4, (place // 2) * slots]).astype(jnp.int32)
+    shift = jnp.where(up == 0, col_shift[0], col_shift[1])
+    scalars = jnp.stack([up, shift, odd, page % 2, page // 2, odd, place // 2 % 2, place // 4, (place // 2) * slots]).astype(jnp.int32)
 
     visual, cot = visual_in.reshape(pages, half, width), visual_cot.reshape(pages, half, width)
     query_sent, patch_sent = pack(scalars, [(query_in, slot_valid), (visual, row_valid)])
@@ -1522,6 +1530,7 @@
 
     vin_came = from_ahead(vin_other, count, -1)
     qin_came = from_partner(qin_other, count)
+    arrays, came = [vis_own, q_res, vin_own, qin_own], [vis_came, res_came, vin_came, qin_came]
 
     weights = (w_vqkv, w_vout, w_up, w_down, w_qqkv, w_xkv, w_qout, w_qup, w_qdown)
     if tiled:
@@ -1553,16 +1562,13 @@
             flipped = rows > 2 * cols and tiles % 2 == 1
             plan.append((step, spots, flipped))
             shapes.append((rows // 8, cols // lax.axis_size("page")))
-        last = shares[0]
-        gain_part, *parts = finish(scalars[CORE:CORE + 1], shares, shapes, plan, width // 8)
+        gain_part, parts, placed = finish(scalars, shares, shapes, plan, width // 8, arrays, came)
     else:
-        last = gain_rows
+        placed = put(scalars, arrays, came, [gain_rows])
         parts = [scattered(g) for g in (g_vqkv, g_vout, g_up, g_down, g_qqkv, g_xkv[0], g_qout, g_qup, g_qdown)]
         gain_part = lax.psum_scatter(gain_grads[:4], "page", scatter_dimension=0, tiled=True)
         gain_part = lax.psum_scatter(gain_part, "strip", scatter_dimension=1, tiled=True).reshape(-1, 1)
-    visual_out, query_out_rows, visual_in_grad, query_in_grad = put(
-        scalars, [vis_own, q_res, vin_own, qin_own], [vis_came, res_came, vin_came, qin_came], [last]
-    )
+    visual_out, query_out_rows, visual_in_grad, query_in_grad = placed
     shape = (pages, strip_rows, columns, width)
     visual_out, visual_in_grad = visual_out.reshape(shape), visual_in_grad.reshape(shape)
     return (visual_out, query_out_rows, visual_in_grad, query_in_grad, gain_part, *parts)

time: 453 us -> 452 us (level)
  no operation moved by 1% of the time
where the time goes in v3:
time: 452 us; the launch traced here: 443 us
  Pallas kernels  365 us (81%)
  starting transfers between devices  48 us (11%)
  waiting for transfers between devices  24.4 us (5%)
    pallas_call x17, Pallas kernels, call(): pl.pallas_call(body, grid_spec=pltpu.PrefetchScalarGridSpec(num_scalar_pr...  271 us
    pallas_call x1, Pallas kernels, late_sum(): pl.pallas_call(lambda *refs: kernel(*refs[:first], *refs[first + len(deps...  70.1 us
    ppermute x19, starting transfers between devices, from_ahead(): lax.ppermute(array, 'strip', [(i, (i - distance) % count) for i in range(...  31 us
    pallas_call x1, Pallas kernels, query_sum(): pl.pallas_call(lambda *refs: kernel(*refs[:9], *refs[9 + len(deps):]), in...  23.1 us
    ppermute x19, waiting for transfers between devices, from_ahead(): lax.ppermute(array, 'strip', [(i, (i - distance) % count) for i in range(...  13.3 us
  transfers between devices with their start and end apart: 29, of which 5 were waited for; matrix products, arithmetic and copies ran while one was open for 0% of the time, Pallas kernels for 80%

profile of v3, /device:TPU:0, one launch (start us, length us, event | category | flops | bytes accessed | tf_op | source)
XLA Modules:
  0.0 443.2 jit_solution(11139750157050703458)
XLA Ops:
  2.0 1.3 fusion
  4.6 0.6 stack.36.refs_0_
  5.2 3.0 pack.1
  8.2 3.0 collective-permute-start
  11.2 5.7 %collective-permute-done.refs_1_.refs_4_ = bf16[144,768]{1,0:T(8,128)(2,1)} collective-permute-done((bf16[144,768]{1,0:T(8,128)(2,1)}, bf16[144,768]{1,0:T(8,128)(2,1)}, u32[]{:S(2)}, u32[]{:S(2)}) %collective-permute-start) | collective-permute-done | bytes 221216 | tf_op jit(solution)/shard_map/ppermute | solution.py:1427
  16.9 4.8 %collective-permute-start.1 = (bf16[592,768]{1,0:T(8,128)(2,1)}, bf16[592,768]{1,0:T(8,128)(2,1)}, u32[]{:S(2)}, u32[]{:S(2)}) collective-permute-start(bf16[592,768]{1,0:T(8,128)(2,1)} %held_back.1.refs_7_), channel_id=1, source_target_pairs={{0,7},{1,0},{2,1},{3,2},{4,3},{5,4},{6,5},{7,6},{8,15},{9,8},{10,9... | collective-permute-start | bytes 2727944 | tf_op jit(solution)/shard_map/ppermute | solution.py:1423
  21.7 0.6 pad.4.refs_5_.refs_4_.refs_8_.refs_10_.refs_16_
  22.3 5.1 %query_in.1 = (bf16[256,768]{1,0:T(8,128)(2,1)}, bf16[256,768]{1,0:T(8,128)(2,1)}, bf16[256,768]{1,0:T(8,128)(2,1)}, bf16[256,1536]{1,0:T(8,128)(2,1)}, bf16[320...) custom-call(s32[9]{0:T(128)} %stack.36.refs_0_, s32[2,1024]{1,0:T(2,128)} %refs_1_.4, s32[2,128]{1,0:T(2,128)} %refs_2_.5, ...), custom_call_target="tpu_custom_call" | custom-call | flops 2717908992 | bytes 5000000 | tf_op jit(solution)/shard_map/query_in/pallas_call | solution.py:103
  27.4 0.0 collective-permute-start.4
  27.4 0.8 collective-permute-start.3
  28.2 1.3 collective-permute-start.2
  29.5 13.2 %collective-permute-done.1.refs_3_ = bf16[592,768]{1,0:T(8,128)(2,1)} collective-permute-done((bf16[592,768]{1,0:T(8,128)(2,1)}, bf16[592,768]{1,0:T(8,128)(2,1)}, u32[]{:S(2)}, u32[]{:S(2)}) %collective-permute-start.1) | collective-permute-done | bytes 909344 | tf_op jit(solution)/shard_map/ppermute | solution.py:1423
  42.7 16.1 %patch_in.1 = (bf16[1152,768]{1,0:T(8,128)(2,1)}, bf16[1152,768]{1,0:T(8,128)(2,1)}, bf16[1152,2304]{1,0:T(8,128)(2,1)}, bf16[1152,1536]{1,0:T(8,128)(2,1)}, bf16[1152,128]{1,0:T(8,128)(2,1)}) custom-call(s32[9]{0:T(128)} %stack.36.refs_0_, s32[2,6]{1,0:T(2,128)} %refs_1_.5, bf16[2,576,768]{2,1,0:T(8,128)(2,1)} %bitcast.41, ...), custom_call_target="tpu_custom_call" | custom-call | flops 20384317440 | bytes 20000000 | tf_op jit(solution)/shard_map/patch_in/pallas_call | solution.py:103
  58.9 10.6 %window_forward.1.refs_3_.refs_1_ = bf16[1152,768]{1,0:T(8,128)(2,1)} custom-call(bf16[1152,2304]{1,0:T(8,128)(2,1)} %get-tuple-element.111.refs_0_), custom_call_target="tpu_custom_call" | custom-call | flops 6115295232 | bytes 8000000 | tf_op jit(solution)/shard_map/window_forward/pallas_call | solution.py:103
  69.5 2.9 pack_two.1
  72.4 1.6 collective-permute-start.9
  74.0 3.6 collective-permute-start.5
  77.6 28.2 %query_forward.1 = (bf16[256,896]{1,0:T(8,128)(2,1)}, bf16[256,896]{1,0:T(8,128)(2,1)}, bf16[256,896]{1,0:T(8,128)(2,1)}, bf16[256,896]{1,0:T(8,128)(2,1)}) custom-call(bf16[256,768]{1,0:T(8,128)(2,1)} %collective-permute-done.2.refs_4_.refs_0_, bf16[256,768]{1,0:T(8,128)(2,1)} %get-tuple-element.110.refs_7_.refs_5_.refs_1_, ...), custom_call_target="tpu_custom_call" | custom-call | flops 43486543872 | bytes 10000000 | tf_op jit(solution)/shard_map/query_forward/pallas_call | solution.py:103
  105.8 4.0 collective-permute-start.7
  109.8 2.5 collective-permute-start.8
  112.3 1.3 collective-permute-start.6
  113.6 0.0 collective-permute-done.5.refs_4_
  113.6 56.0 %patch_ffn.1 = (bf16[2,576,768]{2,1,0:T(8,128)(2,1)}, bf16[576,768]{1,0:T(8,128)(2,1)}, f32[1152,768]{1,0:T(8,128)}, bf16[1152,768]{1,0:T(8,128)(2,1)}, bf16[2,2...) custom-call(s32[9]{0:T(128)} %stack.36.refs_0_, ...), custom_call_target="tpu_custom_call" | custom-call | flops 97844723712 | bytes 40000000 | tf_op jit(solution)/shard_map/patch_ffn/pallas_call | solution.py:103
  169.6 0.7 collective-permute-start.10
  170.3 0.0 collective-permute-done.9.refs_7_
  170.3 0.0 collective-permute-done.6.refs_1_
  170.3 17.0 %query_ffn.1 = (bf16[2,128,768]{2,1,0:T(8,128)(2,1)}, bf16[128,768]{1,0:T(8,128)(2,1)}, f32[256,768]{1,0:T(8,128)}, bf16[256,896]{1,0:T(8,128)(2,1)}, bf16[256,7...) custom-call(s32[9]{0:T(128)} %stack.36.refs_0_, ...), custom_call_target="tpu_custom_call" | custom-call | flops 14495514624 | bytes 20000000 | tf_op jit(solution)/shard_map/query_ffn/pallas_call | solution.py:103
  187.3 1.6 collective-permute-start.14
  188.9 0.4 collective-permute-start.13
  189.3 2.7 collective-permute-start.12
  192.0 0.6 collective-permute-start.11
  192.6 23.1 %query_sum.1 = (bf16[2,4,1296,128]{3,2,1,0:T(8,128)(2,1)}, bf16[2,4,1296,128]{3,2,1,0:T(8,128)(2,1)}, bf16[2,4,1296,128]{3,2,1,0:T(8,128)(2,1)}, bf16[2,4,1296,128]{3,2,1,0:T(8,128)(2,1)}) custom-call(bf16[2,2,2,4,576,128]{5,4,3,2,1,0:T(8,128)(2,1)} %get-tuple-element.121.refs_0_, bf16[2,2,2,4,576,128]{5,4,3,2,1,0:T(8,128)(2,1)} %get-tuple-element.122.refs_1_, ...), custom_call_target="tpu_custom_call" | custom-call | tf_op jit(solution)/shard_map/query_sum/pallas_call | solution.py:1195
  215.7 0.0 collective-permute-done.14.refs_19_.refs_10_
  215.7 0.1 collective-permute-start.15
  215.8 1.5 collective-permute-start.16
  217.3 24.5 %window_backward.1.refs_18_.refs_1_ = bf16[1152,2304]{1,0:T(8,128)(2,1)} custom-call(bf16[1152,2304]{1,0:T(8,128)(2,1)} %get-tuple-element.111.refs_0_, bf16[1152,768]{1,0:T(8,128)(2,1)} %get-tuple-element.120.refs_1_, bf16[8,1296,128]{2,1,0:T(8,128)(2,1)} %bitcast.29, bf16[576,768]{1,0:T(8,128)(2,1)} %collective-permute-done.10.refs_3_.refs_9_), custom_call_target="tpu_custom_call" | custom-call | flops 15288238080 | bytes 13000000 | tf_op jit(solution)/shard_map/window_backward/pallas_call | solution.py:103
  241.9 0.0 collective-permute-done.11.refs_4_.refs_8_
  241.9 25.6 %query_backward.2 = (bf16[256,384]{1,0:T(8,128)(2,1)}, bf16[256,384]{1,0:T(8,128)(2,1)}, bf16[256,384]{1,0:T(8,128)(2,1)}, bf16[256,384]{1,0:T(8,128)(2,1)}, bf1...) custom-call(bf16[256,768]{1,0:T(8,128)(2,1)} %collective-permute-done.2, ...), custom_call_target="tpu_custom_call" | custom-call | flops 27179089920 | bytes 15000000 | tf_op jit(solution)/shard_map/query_backward/pallas_call | solution.py:103
  267.5 3.4 collective-permute-start.19
  270.9 0.6 collective-permute-start.21
  271.5 4.2 collective-permute-done.15.refs_2_.refs_4_
  275.7 0.1 collective-permute-done.16.refs_6_.refs_8_
  275.8 7.8 %halve_add.2 = (bf16[4,1296,128]{2,1,0:T(8,128)(2,1)}, bf16[4,1296,128]{2,1,0:T(8,128)(2,1)}, bf16[4,1296,128]{2,1,0:T(8,128)(2,1)}, bf16[4,1296,128]{2,1,0:T(8,128)(2,1)}) custom-call(s32[9]{0:T(128)} %stack.36.refs_0_, bf16[8,1296,128]{2,1,0:T(8,128)(2,1)} %bitcast.30, bf16[8,1296,128]{2,1,0:T(8,128)(2,1)} %collective-permute-done.15.refs_2_.refs_4_, ...), custom_call_target="tpu_custom_call" | custom-call | flops 3000000 | bytes 15925248 | tf_op jit(solution)/shard_map/halve_add/pallas_call | solution.py:103
  283.6 1.6 collective-permute-start.17
  285.2 1.7 collective-permute-start.18
  286.8 25.5 %query_backward.3 = (bf16[256,384]{1,0:T(8,128)(2,1)}, bf16[256,384]{1,0:T(8,128)(2,1)}, bf16[256,384]{1,0:T(8,128)(2,1)}, bf16[256,384]{1,0:T(8,128)(2,1)}, bf1...) custom-call(bf16[256,768]{1,0:T(8,128)(2,1)} %collective-permute-done.2, ...), custom_call_target="tpu_custom_call" | custom-call | flops 27179089920 | bytes 15000000 | tf_op jit(solution)/shard_map/query_backward/pallas_call | solution.py:103
  312.3 3.3 collective-permute-start.22
  315.6 0.0 collective-permute-done.20.refs_12_.refs_3_
  315.6 0.0 collective-permute-start.23
  315.6 0.0 collective-permute-done.21.refs_13_.refs_4_
  315.6 0.6 collective-permute-start.24
  316.3 4.5 %halve_add.3 = (bf16[2,1296,128]{2,1,0:T(8,128)(2,1)}, bf16[2,1296,128]{2,1,0:T(8,128)(2,1)}, bf16[2,1296,128]{2,1,0:T(8,128)(2,1)}, bf16[2,1296,128]{2,1,0:T(8,128)(2,1)}) custom-call(s32[9]{0:T(128)} %stack.36.refs_0_, bf16[4,1296,128]{2,1,0:T(8,128)(2,1)} %get-tuple-element.144.refs_18_.refs_1_.refs_3_, ...), custom_call_target="tpu_custom_call" | custom-call | flops 3000000 | bytes 7962624 | tf_op jit(solution)/shard_map/halve_add/pallas_call | solution.py:103
  320.7 3.8 collective-permute-start.25
  324.6 0.1 collective-permute-start.26
  324.6 29.9 %patch_back.1 = (f32[2,576,768]{2,1,0:T(8,128)}, bf16[576,768]{1,0:T(8,128)(2,1)}, f32[8,768]{1,0:T(8,128)}, bf16[2,2,2,4,432,128]{5,4,3,2,1,0:T(8,128)(2,1)}, b...) custom-call(s32[9]{0:T(128)} %stack.36.refs_0_, ...), custom_call_target="tpu_custom_call" | custom-call | flops 40768634880 | bytes 40000000 | tf_op jit(solution)/shard_map/patch_back/pallas_call | solution.py:103
  354.6 0.4 collective-permute-start.27
  355.0 0.0 collective-permute-done.25.refs_19_.refs_6_
  355.0 1.1 collective-permute-done.26.refs_20_.refs_8_
  356.1 8.6 %query_out.1 = (f32[2,128,768]{2,1,0:T(8,128)}, bf16[128,768]{1,0:T(8,128)(2,1)}, bf16[2,2,2,4,432,128]{5,4,3,2,1,0:T(8,128)(2,1)}, bf16[2,2,2,4,48,128]{5,4,3,2,1,0:T(8,128)(2,1)}) custom-call(s32[9]{0:T(128)} %stack.36.refs_0_, bf16[256,384]{1,0:T(8,128)(2,1)} %collective-permute-done.19.refs_10_.refs_1_, ...), custom_call_target="tpu_custom_call" | custom-call | flops 5435817984 | bytes 10000000 | tf_op jit(solution)/shard_map/query_out/pallas_call | solution.py:103
  364.7 2.0 collective-permute-start.28
  366.7 70.1 %late_sum.1 = (bf16[1920,128]{1,0:T(8,128)(2,1)}, bf16[1872,128]{1,0:T(8,128)(2,1)}, bf16[1920,128]{1,0:T(8,128)(2,1)}, bf16[1872,128]{1,0:T(8,128)(2,1)}) custom-call(bf16[2,16,432,128]{3,2,1,0:T(8,128)(2,1)} %bitcast.35, bf16[2,16,144,128]{3,2,1,0:T(8,128)(2,1)} %bitcast.42, bf16[2,16,48,128]{3,2,1,0:T(8,128)(2,1)} %bitcast.44, ...), custom_call_target="tpu_custom_call" | custom-call | tf_op jit(solution)/shard_map/late_sum/pallas_call | solution.py:1338
  436.8 0.0 collective-permute-done.28.refs_12_
  436.8 0.0 collective-permute-done.27.refs_11_
  436.8 6.2 %finish.1 = (f32[1,96]{1,0:T(1,128)}, f32[96,576]{1,0:T(8,128)}, f32[96,192]{1,0:T(8,128)}, f32[96,768]{1,0:T(8,128)}, f32[192,384]{1,0:T(8,128)}, /*index=5*/f3...) custom-call(s32[9]{0:T(128)} %stack.36.refs_0_, ...), custom_call_target="tpu_custom_call", output_to_operand_aliasing={{10}: (5, {}), {11}: (6, {}), {12}: (7, {}), {13}: (8, {})} | custom-call | tf_op jit(solution)/shard_map/finish/pallas_call | solution.py:103
  (18 shorter events, 0.0 us)
Async XLA Ops:
  0.6 21.1 %copy-start = (f32[768,4]{0,1:T(4,128)S(1)}, f32[768,4]{0,1:T(4,128)}, u32[]{:S(2)}) copy-start(f32[768,4]{0,1:T(4,128)} %param.26) | copy-start | bytes 36868
  8.2 8.7 %collective-permute-start = (bf16[144,768]{1,0:T(8,128)(2,1)}, bf16[144,768]{1,0:T(8,128)(2,1)}, u32[]{:S(2)}, u32[]{:S(2)}) collective-permute-start(bf16[144,768]{1,0:T(8,128)(2,1)} %get-tuple-element.109), channel_id=1, source_target_pairs={{0,1},{1,0},{2,3},{3,2},{4,5},{5,4},{6,7},{7,6},{8,9},{9,8},{10,11... | collective-permute-start | bytes 663560 | tf_op jit(solution)/shard_map/ppermute | solution.py:1427
  16.9 25.8 %collective-permute-start.1 = (bf16[592,768]{1,0:T(8,128)(2,1)}, bf16[592,768]{1,0:T(8,128)(2,1)}, u32[]{:S(2)}, u32[]{:S(2)}) collective-permute-start(bf16[592,768]{1,0:T(8,128)(2,1)} %held_back.1.refs_7_), channel_id=1, source_target_pairs={{0,7},{1,0},{2,1},{3,2},{4,3},{5,4},{6,5},{7,6},{8,15},{9,8},{10,9... | collective-permute-start | bytes 2727944 | tf_op jit(solution)/shard_map/ppermute | solution.py:1423
  27.4 42.0 %collective-permute-start.4 = (bf16[256,768]{1,0:T(8,128)(2,1)}, bf16[256,768]{1,0:T(8,128)(2,1)}, u32[]{:S(2)}, u32[]{:S(2)}) collective-permute-start(bf16[256,768]{1,0:T(8,128)(2,1)} %get-tuple-element.110.refs_7_.refs_5_.refs_1_), channel_id=1, source_target_pairs={{0,4},{1,5},{2,6},{3,7},{4,0},{5,1},{6,2},{7,3},{8,12},{9,13},{10,... | collective-permute-start | bytes 1179656 | tf_op jit(solution)/shard_map/ppermute | solution.py:1423
  27.4 42.0 %collective-permute-start.3 = (bf16[256,768]{1,0:T(8,128)(2,1)}, bf16[256,768]{1,0:T(8,128)(2,1)}, u32[]{:S(2)}, u32[]{:S(2)}) collective-permute-start(bf16[256,768]{1,0:T(8,128)(2,1)} %get-tuple-element.110.refs_7_.refs_5_.refs_1_), channel_id=1, source_target_pairs={{0,6},{1,7},{2,0},{3,1},{4,2},{5,3},{6,4},{7,5},{8,14},{9,15},{10,... | collective-permute-start | bytes 1179656 | tf_op jit(solution)/shard_map/ppermute | solution.py:1423
  28.2 41.3 %collective-permute-start.2 = (bf16[256,768]{1,0:T(8,128)(2,1)}, bf16[256,768]{1,0:T(8,128)(2,1)}, u32[]{:S(2)}, u32[]{:S(2)}) collective-permute-start(bf16[256,768]{1,0:T(8,128)(2,1)} %get-tuple-element.110.refs_7_.refs_5_.refs_1_), channel_id=1, source_target_pairs={{0,2},{1,3},{2,4},{3,5},{4,6},{5,7},{6,0},{7,1},{8,10},{9,11},{10,... | collective-permute-start | bytes 1179656 | tf_op jit(solution)/shard_map/ppermute | solution.py:1423
  72.4 97.9 %collective-permute-start.9 = (bf16[128,768]{1,0:T(8,128)(2,1)}, bf16[128,768]{1,0:T(8,128)(2,1)}, u32[]{:S(2)}, u32[]{:S(2)}) collective-permute-start(bf16[128,768]{1,0:T(8,128)(2,1)} %get-tuple-element.118.refs_10_), channel_id=1, source_target_pairs={{0,1},{1,0},{2,3},{3,2},{4,5},{5,4},{6,7},{7,6},{8,9},{9,8},{10,11... | collective-permute-start | bytes 589832 | tf_op jit(solution)/shard_map/ppermute | solution.py:1427
  74.0 39.6 %collective-permute-start.5 = (bf16[576,768]{1,0:T(8,128)(2,1)}, bf16[576,768]{1,0:T(8,128)(2,1)}, u32[]{:S(2)}, u32[]{:S(2)}) collective-permute-start(bf16[576,768]{1,0:T(8,128)(2,1)} %get-tuple-element.113), channel_id=1, source_target_pairs={{0,7},{1,0},{2,1},{3,2},{4,3},{5,4},{6,5},{7,6},{8,15},{9,8},{10,9... | collective-permute-start | bytes 2654216 | tf_op jit(solution)/shard_map/ppermute | solution.py:1423
  105.8 64.5 %collective-permute-start.7 = (bf16[256,896]{1,0:T(8,128)(2,1)}, bf16[256,896]{1,0:T(8,128)(2,1)}, u32[]{:S(2)}, u32[]{:S(2)}) collective-permute-start(bf16[256,896]{1,0:T(8,128)(2,1)} %get-tuple-element.125), channel_id=1, source_target_pairs={{0,2},{1,3},{2,4},{3,5},{4,6},{5,7},{6,0},{7,1},{8,10},{9,11},{10,... | collective-permute-start | bytes 1376264 | tf_op jit(solution)/shard_map/ppermute | solution.py:1423
  109.8 60.5 %collective-permute-start.8 = (bf16[256,896]{1,0:T(8,128)(2,1)}, bf16[256,896]{1,0:T(8,128)(2,1)}, u32[]{:S(2)}, u32[]{:S(2)}) collective-permute-start(bf16[256,896]{1,0:T(8,128)(2,1)} %get-tuple-element.126), channel_id=1, source_target_pairs={{0,4},{1,5},{2,6},{3,7},{4,0},{5,1},{6,2},{7,3},{8,12},{9,13},{10,... | collective-permute-start | bytes 1376264 | tf_op jit(solution)/shard_map/ppermute | solution.py:1423
  112.3 58.0 %collective-permute-start.6 = (bf16[256,896]{1,0:T(8,128)(2,1)}, bf16[256,896]{1,0:T(8,128)(2,1)}, u32[]{:S(2)}, u32[]{:S(2)}) collective-permute-start(bf16[256,896]{1,0:T(8,128)(2,1)} %get-tuple-element.119.refs_9_), channel_id=1, source_target_pairs={{0,6},{1,7},{2,0},{3,1},{4,2},{5,3},{6,4},{7,5},{8,14},{9,15},{10,... | collective-permute-start | bytes 1376264 | tf_op jit(solution)/shard_map/ppermute | solution.py:1423
  169.6 46.2 %collective-permute-start.10 = (bf16[576,768]{1,0:T(8,128)(2,1)}, bf16[576,768]{1,0:T(8,128)(2,1)}, u32[]{:S(2)}, u32[]{:S(2)}) collective-permute-start(bf16[576,768]{1,0:T(8,128)(2,1)} %get-tuple-element.136), channel_id=1, source_target_pairs={{0,1},{1,2},{2,3},{3,4},{4,5},{5,6},{6,7},{7,0},{8,9},{9,10},{10,1... | collective-permute-start | bytes 2654216 | tf_op jit(solution)/shard_map/ppermute | solution.py:1423
  187.3 28.4 %collective-permute-start.14 = (bf16[128,768]{1,0:T(8,128)(2,1)}, bf16[128,768]{1,0:T(8,128)(2,1)}, u32[]{:S(2)}, u32[]{:S(2)}) collective-permute-start(bf16[128,768]{1,0:T(8,128)(2,1)} %get-tuple-element.139), channel_id=1, source_target_pairs={{0,1},{1,0},{2,3},{3,2},{4,5},{5,4},{6,7},{7,6},{8,9},{9,8},{10,11... | collective-permute-start | bytes 589832 | tf_op jit(solution)/shard_map/ppermute | solution.py:1427
  188.9 53.0 %collective-permute-start.13 = (bf16[256,896]{1,0:T(8,128)(2,1)}, bf16[256,896]{1,0:T(8,128)(2,1)}, u32[]{:S(2)}, u32[]{:S(2)}) collective-permute-start(bf16[256,896]{1,0:T(8,128)(2,1)} %get-tuple-element.137.refs_5_.refs_9_), channel_id=1, source_target_pairs={{0,4},{1,5},{2,6},{3,7},{4,0},{5,1},{6,2},{7,3},{8,12},{9,13},{10,... | collective-permute-start | bytes 1376264 | tf_op jit(solution)/shard_map/ppermute | solution.py:1423
  189.3 52.6 %collective-permute-start.12 = (bf16[256,896]{1,0:T(8,128)(2,1)}, bf16[256,896]{1,0:T(8,128)(2,1)}, u32[]{:S(2)}, u32[]{:S(2)}) collective-permute-start(bf16[256,896]{1,0:T(8,128)(2,1)} %get-tuple-element.137.refs_5_.refs_9_), channel_id=1, source_target_pairs={{0,6},{1,7},{2,0},{3,1},{4,2},{5,3},{6,4},{7,5},{8,14},{9,15},{10,... | collective-permute-start | bytes 1376264 | tf_op jit(solution)/shard_map/ppermute | solution.py:1423
  192.0 49.9 %collective-permute-start.11 = (bf16[256,896]{1,0:T(8,128)(2,1)}, bf16[256,896]{1,0:T(8,128)(2,1)}, u32[]{:S(2)}, u32[]{:S(2)}) collective-permute-start(bf16[256,896]{1,0:T(8,128)(2,1)} %get-tuple-element.137.refs_5_.refs_9_), channel_id=1, source_target_pairs={{0,2},{1,3},{2,4},{3,5},{4,6},{5,7},{6,0},{7,1},{8,10},{9,11},{10,... | collective-permute-start | bytes 1376264 | tf_op jit(solution)/shard_map/ppermute | solution.py:1423
  215.7 60.0 %collective-permute-start.15 = (bf16[8,1296,128]{2,1,0:T(8,128)(2,1)}, bf16[8,1296,128]{2,1,0:T(8,128)(2,1)}, u32[]{:S(2)}, u32[]{:S(2)}) collective-permute-start(bf16[8,1296,128]{2,1,0:T(8,128)(2,1)} %bitcast.49), channel_id=1, source_target_pairs={{0,1},{1,0},{2,3},{3,2},{4,5},{5,4},{6,7},{7,6},{8,9},{9,8},{10,11... | collective-permute-start | bytes 7962632 | tf_op jit(solution)/shard_map/ppermute | solution.py:1219
  215.8 59.9 %collective-permute-start.16 = (bf16[8,1296,128]{2,1,0:T(8,128)(2,1)}, bf16[8,1296,128]{2,1,0:T(8,128)(2,1)}, u32[]{:S(2)}, u32[]{:S(2)}) collective-permute-start(bf16[8,1296,128]{2,1,0:T(8,128)(2,1)} %bitcast.48), channel_id=1, source_target_pairs={{0,16},{8,24},{16,0},{24,8},{1,17},{9,25},{17,1},{25,9},{2,18},{10... | collective-permute-start | bytes 7962632 | tf_op jit(solution)/shard_map/ppermute | solution.py:1219
  267.5 44.8 %collective-permute-start.19 = (bf16[256,384]{1,0:T(8,128)(2,1)}, bf16[256,384]{1,0:T(8,128)(2,1)}, u32[]{:S(2)}, u32[]{:S(2)}) collective-permute-start(bf16[256,384]{1,0:T(8,128)(2,1)} %get-tuple-element.154), channel_id=1, source_target_pairs={{0,6},{1,7},{2,0},{3,1},{4,2},{5,3},{6,4},{7,5},{8,14},{9,15},{10,... | collective-permute-start | bytes 589832 | tf_op jit(solution)/shard_map/ppermute | solution.py:1423
  270.9 44.7 %collective-permute-start.20 = (bf16[256,384]{1,0:T(8,128)(2,1)}, bf16[256,384]{1,0:T(8,128)(2,1)}, u32[]{:S(2)}, u32[]{:S(2)}) collective-permute-start(bf16[256,384]{1,0:T(8,128)(2,1)} %get-tuple-element.156), channel_id=1, source_target_pairs={{0,2},{1,3},{2,4},{3,5},{4,6},{5,7},{6,0},{7,1},{8,10},{9,11},{10,... | collective-permute-start | bytes 589832 | tf_op jit(solution)/shard_map/ppermute | solution.py:1423
  270.9 44.7 %collective-permute-start.21 = (bf16[256,384]{1,0:T(8,128)(2,1)}, bf16[256,384]{1,0:T(8,128)(2,1)}, u32[]{:S(2)}, u32[]{:S(2)}) collective-permute-start(bf16[256,384]{1,0:T(8,128)(2,1)} %get-tuple-element.157), channel_id=1, source_target_pairs={{0,4},{1,5},{2,6},{3,7},{4,0},{5,1},{6,2},{7,3},{8,12},{9,13},{10,... | collective-permute-start | bytes 589832 | tf_op jit(solution)/shard_map/ppermute | solution.py:1423
  283.6 32.7 %collective-permute-start.17 = (bf16[4,1296,128]{2,1,0:T(8,128)(2,1)}, bf16[4,1296,128]{2,1,0:T(8,128)(2,1)}, u32[]{:S(2)}, u32[]{:S(2)}) collective-permute-start(bf16[4,1296,128]{2,1,0:T(8,128)(2,1)} %get-tuple-element.151), channel_id=1, source_target_pairs={{0,16},{8,24},{16,0},{24,8},{1,17},{9,25},{17,1},{25,9},{2,18},{10... | collective-permute-start | bytes 3981320 | tf_op jit(solution)/shard_map/ppermute | solution.py:1219
  285.2 31.1 %collective-permute-start.18 = (bf16[4,1296,128]{2,1,0:T(8,128)(2,1)}, bf16[4,1296,128]{2,1,0:T(8,128)(2,1)}, u32[]{:S(2)}, u32[]{:S(2)}) collective-permute-start(bf16[4,1296,128]{2,1,0:T(8,128)(2,1)} %get-tuple-element.153), channel_id=1, source_target_pairs={{0,1},{1,0},{2,3},{3,2},{4,5},{5,4},{6,7},{7,6},{8,9},{9,8},{10,11... | collective-permute-start | bytes 3981320 | tf_op jit(solution)/shard_map/ppermute | solution.py:1219
  312.3 42.3 %collective-permute-start.22 = (bf16[256,384]{1,0:T(8,128)(2,1)}, bf16[256,384]{1,0:T(8,128)(2,1)}, u32[]{:S(2)}, u32[]{:S(2)}) collective-permute-start(bf16[256,384]{1,0:T(8,128)(2,1)} %get-tuple-element.161), channel_id=1, source_target_pairs={{0,6},{1,7},{2,0},{3,1},{4,2},{5,3},{6,4},{7,5},{8,14},{9,15},{10,... | collective-permute-start | bytes 589832 | tf_op jit(solution)/shard_map/ppermute | solution.py:1423
  315.6 39.4 %collective-permute-start.23 = (bf16[256,384]{1,0:T(8,128)(2,1)}, bf16[256,384]{1,0:T(8,128)(2,1)}, u32[]{:S(2)}, u32[]{:S(2)}) collective-permute-start(bf16[256,384]{1,0:T(8,128)(2,1)} %get-tuple-element.163), channel_id=1, source_target_pairs={{0,2},{1,3},{2,4},{3,5},{4,6},{5,7},{6,0},{7,1},{8,10},{9,11},{10,... | collective-permute-start | bytes 589832 | tf_op jit(solution)/shard_map/ppermute | solution.py:1423
  315.6 39.4 %collective-permute-start.24 = (bf16[256,384]{1,0:T(8,128)(2,1)}, bf16[256,384]{1,0:T(8,128)(2,1)}, u32[]{:S(2)}, u32[]{:S(2)}) collective-permute-start(bf16[256,384]{1,0:T(8,128)(2,1)} %get-tuple-element.164), channel_id=1, source_target_pairs={{0,4},{1,5},{2,6},{3,7},{4,0},{5,1},{6,2},{7,3},{8,12},{9,13},{10,... | collective-permute-start | bytes 589832 | tf_op jit(solution)/shard_map/ppermute | solution.py:1423
  320.7 34.3 %collective-permute-start.25 = (bf16[2,1296,128]{2,1,0:T(8,128)(2,1)}, bf16[2,1296,128]{2,1,0:T(8,128)(2,1)}, u32[]{:S(2)}, u32[]{:S(2)}) collective-permute-start(bf16[2,1296,128]{2,1,0:T(8,128)(2,1)} %get-tuple-element.172), channel_id=1, source_target_pairs={{0,2},{1,3},{2,0},{3,1},{4,6},{5,7},{6,4},{7,5},{8,10},{9,11},{10,... | collective-permute-start | bytes 1990664 | tf_op jit(solution)/shard_map/ppermute | solution.py:1219
  324.6 31.6 %collective-permute-start.26 = (bf16[2,1296,128]{2,1,0:T(8,128)(2,1)}, bf16[2,1296,128]{2,1,0:T(8,128)(2,1)}, u32[]{:S(2)}, u32[]{:S(2)}) collective-permute-start(bf16[2,1296,128]{2,1,0:T(8,128)(2,1)} %get-tuple-element.173), channel_id=1, source_target_pairs={{0,2},{1,3},{2,0},{3,1},{4,6},{5,7},{6,4},{7,5},{8,10},{9,11},{10,... | collective-permute-start | bytes 1990664 | tf_op jit(solution)/shard_map/ppermute | solution.py:1219
  354.6 82.2 %collective-permute-start.27 = (bf16[576,768]{1,0:T(8,128)(2,1)}, bf16[576,768]{1,0:T(8,128)(2,1)}, u32[]{:S(2)}, u32[]{:S(2)}) collective-permute-start(bf16[576,768]{1,0:T(8,128)(2,1)} %get-tuple-element.186), channel_id=1, source_target_pairs={{0,1},{1,2},{2,3},{3,4},{4,5},{5,6},{6,7},{7,0},{8,9},{9,10},{10,1... | collective-permute-start | bytes 2654216 | tf_op jit(solution)/shard_map/ppermute | solution.py:1423
  364.7 72.1 %collective-permute-start.28 = (bf16[128,768]{1,0:T(8,128)(2,1)}, bf16[128,768]{1,0:T(8,128)(2,1)}, u32[]{:S(2)}, u32[]{:S(2)}) collective-permute-start(bf16[128,768]{1,0:T(8,128)(2,1)} %get-tuple-element.187), channel_id=1, source_target_pairs={{0,1},{1,0},{2,3},{3,2},{4,5},{5,4},{6,7},{7,6},{8,9},{9,8},{10,11... | collective-permute-start | bytes 589832 | tf_op jit(solution)/shard_map/ppermute | solution.py:1427
